TPU v7x, 32 devices: a whole 2x2x4 slice. The times are simulated.
32 devices in a mesh: tm: 2 (over x), chan: 16 (over z, y, core).
Axes of the slice: x: 2, y: 2, z: 4, core: 2. Of those that a mesh axis runs over, the one named last changes fastest.
Arguments:
- voltage_frequency_samples: bfloat16 [2, 64, 30, 2, 8192], P(None, ('tm', 'chan')), may hold values from -6 to 6
- lag_lookup_entry: int32 [2, 2, 30], P('tm'), may hold values from 0 to 63
- lag_lookup_turning: float32 [64, 8192], P(None, 'chan'), may hold values from -3.140625 to 3.140625
- antenna_pair_members: int32 [435, 2], replicated, may hold values from 0 to 29, as said below
- frequency_bin_target: int32 [8192], P('chan'), may hold values from 0 to 63, as said below
Outputs:
- centre_vis: float32 [128, 2, 4, 435], P(('tm', 'chan'))
Inputs may be any that keep to these rules, and one draw needn't show every extreme that they name: `antenna_pair_members`: every unordered pair of two different stations of the 30 appears in exactly one row, in either order. `frequency_bin_target`: each of the 64 output channels receives exactly 128 fine channels.
All inputs are finite; a program needn't handle non-finite values.
Results may differ from a plain program's by a relative error of at most 0.0029.
Values may be sent and summed in bfloat16 or wider, within the bound.
No kernel may reach another device: no remote copies, remote signals or barrier semaphores. Data moves between devices by JAX's collectives and lax.ppermute only.
A program may use at most 128 MiB of HBM per device.

v0:
```python
import jax
import jax.numpy as jnp
from jax import lax
from jax.sharding import PartitionSpec as P

F = 8192
Q = 64
G_DEV = 1


def correlate(left_part, right_part):
    return jnp.einsum("gtaf,gtbf->gabf", left_part, right_part, preferred_element_type=jnp.float32)


def on_device(
    voltage_frequency_samples,
    lag_lookup_entry,
    lag_lookup_turning,
    antenna_pair_members,
    frequency_bin_target,
):
    regrouped = lax.all_to_all(
        voltage_frequency_samples, "chan", split_axis=4, concat_axis=1, tiled=True
    )
    fine_local = regrouped.shape[4]
    selector = (frequency_bin_target[:, None] == jnp.arange(Q, dtype=jnp.int32)[None, :]).astype(
        jnp.bfloat16
    )
    spectra_count = regrouped.shape[1]
    stations = regrouped.shape[2]
    polars = regrouped.shape[3]
    antenna_pair_total = antenna_pair_members.shape[0]
    shaped = regrouped.reshape(2, G_DEV, spectra_count // G_DEV, stations * polars, fine_local)
    real_part = shaped[0]
    imag_part = shaped[1]
    vis_real = correlate(real_part, real_part) + correlate(imag_part, imag_part)
    vis_imag = correlate(imag_part, real_part) - correlate(real_part, imag_part)
    left_antenna_number = antenna_pair_members[:, 0]
    right_antenna_number = antenna_pair_members[:, 1]
    full_shape = (G_DEV, stations, polars, stations, polars, fine_local)
    picked_real = vis_real.reshape(full_shape)[:, left_antenna_number, :, right_antenna_number]
    picked_imag = vis_imag.reshape(full_shape)[:, left_antenna_number, :, right_antenna_number]
    base_real = jnp.transpose(picked_real, (1, 2, 3, 0, 4)).reshape(
        G_DEV, polars * polars, antenna_pair_total, fine_local
    )
    base_imag = jnp.transpose(picked_imag, (1, 2, 3, 0, 4)).reshape(
        G_DEV, polars * polars, antenna_pair_total, fine_local
    )
    station_phase = jnp.take(lag_lookup_turning, lag_lookup_entry, axis=0)
    phase_diff = (
        station_phase[:, :, left_antenna_number] - station_phase[:, :, right_antenna_number]
    )
    cosine = jnp.cos(phase_diff)
    sine = jnp.sin(phase_diff)
    centres = lag_lookup_entry.shape[1]
    partial_list = []
    for centre in range(centres):
        cos_now = cosine[:, centre][:, None]
        sin_now = sine[:, centre][:, None]
        rot_real = (base_real * cos_now + base_imag * sin_now).astype(jnp.bfloat16)
        rot_imag = (base_imag * cos_now - base_real * sin_now).astype(jnp.bfloat16)
        rotated = jnp.stack([rot_real, rot_imag])
        partial_list.append(
            jnp.einsum("rgpbf,fq->qrpb", rotated, selector, preferred_element_type=jnp.float32)
        )
    partial_value = jnp.stack(partial_list)
    columns = selector.shape[1]
    tail = (2, polars * polars, antenna_pair_total)
    flat = partial_value.reshape((centres * columns,) + tail)
    channel_summed_products = lax.psum_scatter(
        flat, ("tm", "chan"), scatter_dimension=0, tiled=True
    )
    return channel_summed_products * (Q / F)


def solution(mesh):
    return jax.shard_map(
        on_device,
        mesh=mesh,
        in_specs=(
            P(None, ("tm", "chan"), None, None, None),
            P("tm", None, None),
            P(None, "chan"),
            P(),
            P("chan"),
        ),
        out_specs=P(("tm", "chan"), None, None, None),
        check_vma=False,
    )
```

profile of v0, /device:TPU:0, one launch (start us, length us, event | category | flops | bytes accessed | tf_op | source)
XLA Modules:
  0.0 579.3 jit_solution(6218963569826198733)
XLA Ops:
  6.5 38.2 %copy.44 = bf16[2,2,30,2,8192]{2,3,1,0,4:T(2,128)(2,1)} copy(bf16[2,2,30,2,8192]{4,3,2,1,0:T(2,128)(2,1)} %param.5) | data formatting | bytes 7864320 | tf_op args[0]
  44.7 32.7 %reshape.293 = bf16[16,2,61440]{2,1,0:T(2,128)(2,1)} reshape(bf16[8192,2,2,2,30]{4,3,2,1,0:T(2,128)(2,1)} %bitcast.115) | data formatting | bytes 7864320
  77.4 7.6 %all-to-all-start = ((bf16[16,2,61440]{2,1,0:T(2,128)(2,1)}), bf16[16,2,61440]{2,1,0:T(2,128)(2,1)}, u32[]{:S(2)}, u32[]{:S(2)}) async-start(bf16[16,2,61440]{2,1,0:T(2,128)(2,1)} %reshape.293), calls=%async_computation | async-start | bytes 7864320 | tf_op jit(solution)/shard_map/all_to_all | solution.py:22
  94.2 26.2 %cosine_bitcast_fusion = (f32[1,2,435,512]{3,1,2,0:T(2,128)S(1)}, f32[1,2,435,512]{3,1,2,0:T(2,128)S(1)}) fusion(f32[435,2,512]{2,1,0:T(2,128)S(1)} %gather_fusion.2, f32[435,2,512]{2,1,0:T(2,128)} %gather_fusion.3), kind=kLoop, calls=%fused_computation.33 | loop fusion | flops 445440 | bytes 7127040 | tf_op jit(solution)/shard_map/cos | solution.py:53
  126.3 31.7 %all-to-all-done = bf16[16,2,61440]{2,1,0:T(2,128)(2,1)} async-done(((bf16[16,2,61440]{2,1,0:T(2,128)(2,1)}), bf16[16,2,61440]{2,1,0:T(2,128)(2,1)}, u32[]{:S(2)}, u32[]{:S(2)}) %all-to-all-start) | async-done | bytes 3932192 | tf_op jit(solution)/shard_map/all_to_all | solution.py:22
  158.0 46.6 %reshape.294 = bf16[8192,2,2,2,30]{4,3,2,1,0:T(2,128)(2,1)} reshape(bf16[16,2,61440]{2,1,0:T(2,128)(2,1)} %all-to-all-done) | data formatting | bytes 7864320
  204.6 40.6 %copy.45 = bf16[2,2,30,2,16,512]{5,1,4,3,2,0:T(2,128)(2,1)} copy(bf16[2,2,30,2,16,512]{2,3,1,0,5,4:T(2,128)(2,1)} %bitcast.114) | data formatting | bytes 7864320 | tf_op jit(solution)/shard_map/all_to_all | solution.py:22
  245.2 7.3 %fusion.24 = (bf16[1,16,2,30,2,512]{5,2,1,4,3,0:T(2,128)(2,1)}, bf16[1,16,2,30,2,512]{5,2,1,4,3,0:T(2,128)(2,1)}) fusion(bf16[2,16,2,30,2,512]{5,2,1,4,3,0:T(2,128)(2,1)} %bitcast.116), kind=kLoop, calls=%fused_computation.57 | loop fusion | bytes 7864320 | tf_op jit(solution)/shard_map/slice | solution.py:35
  252.5 4.3 reshape.231
  256.8 7.9 %copy.46 = bf16[32,60,512]{1,0,2:T(8,128)(2,1)} copy(bf16[32,60,512]{2,0,1:T(8,128)(2,1)S(1)} %reshape.231) | data formatting | bytes 3932160 | tf_op jit(solution)/shard_map/reshape.5
  264.7 4.5 reshape.232
  269.2 7.8 %copy.48 = bf16[32,60,512]{1,0,2:T(8,128)(2,1)} copy(bf16[32,60,512]{2,0,1:T(8,128)(2,1)S(1)} %reshape.232) | data formatting | bytes 3932160 | tf_op jit(solution)/shard_map/reshape.16
  277.0 11.8 %fusion.27 = f32[512,60,60]{2,1,0:T(8,128)} fusion(bf16[32,60,512]{1,0,2:T(8,128)(2,1)} %copy.46), kind=kOutput, calls=%fused_computation.60 | convolution fusion | flops 117964800 | bytes 9338880 | tf_op jit(solution)/shard_map/gtaf,gtbf->gabf/dot_general | solution.py:12
  288.8 7.1 %fusion.28 = f32[512,60,60]{2,1,0:T(8,128)} fusion(bf16[32,60,512]{1,0,2:T(8,128)(2,1)S(1)} %copy-done.3, bf16[32,60,512]{1,0,2:T(8,128)(2,1)S(1)} %copy-done.2), kind=kOutput, calls=%fused_computation.61 | convolution fusion | flops 117964800 | bytes 11304960 | tf_op jit(solution)/shard_map/gtaf,gtbf->gabf/dot_general | solution.py:12
  295.9 16.4 %subtract_bitcast_fusion = f32[1,60,60,512]{1,2,3,0:T(8,128)} fusion(f32[512,60,60]{2,1,0:T(8,128)} %fusion.28, bf16[32,60,512]{1,0,2:T(8,128)(2,1)} %copy.48, bf16[32,60,512]{1,0,2:T(8,128)(2,1)} %copy.46), kind=kOutput, calls=%fused_computation.5 | convolution fusion | flops 119808000 | bytes 18677760 | tf_op jit(solution)/shard_map/gtaf,gtbf->gabf/dot_general | solution.py:12
  312.3 13.6 %copy.58 = f32[1,60,60,512]{3,2,1,0:T(8,128)} copy(f32[1,60,60,512]{1,2,3,0:T(8,128)} %subtract_bitcast_fusion) | data formatting | bytes 14745600 | tf_op jit(solution)/shard_map/sub | solution.py:37
  325.8 9.8 %reshape.274 = f32[30,2,30,2,512]{4,3,2,1,0:T(2,128)} reshape(f32[1,60,60,512]{3,2,1,0:T(8,128)} %copy.58) | data formatting | bytes 14745600 | tf_op jit(solution)/shard_map/reshape | solution.py:42
  335.6 16.1 %gather_fusion.4 = f32[435,2,2,512]{3,2,1,0:T(2,128)} fusion(f32[30,2,30,2,512]{4,3,2,1,0:T(2,128)} %reshape.274, s32[435]{0:T(512)S(1)} %bitcast.112), kind=kCustom, calls=%fused_computation.4 | custom fusion | bytes 7130520 | tf_op jit(solution)/shard_map/gather | solution.py:42
  351.7 5.0 copy.59
  356.8 16.4 %add_bitcast_fusion = f32[1,60,60,512]{1,2,3,0:T(8,128)} fusion(f32[512,60,60]{2,1,0:T(8,128)} %fusion.27, bf16[32,60,512]{1,0,2:T(8,128)(2,1)} %copy.48), kind=kOutput, calls=%fused_computation.6 | convolution fusion | flops 119808000 | bytes 16711680 | tf_op jit(solution)/shard_map/gtaf,gtbf->gabf/dot_general | solution.py:12
  373.2 13.6 %copy.50 = f32[1,60,60,512]{3,2,1,0:T(8,128)} copy(f32[1,60,60,512]{1,2,3,0:T(8,128)} %add_bitcast_fusion) | data formatting | bytes 14745600 | tf_op jit(solution)/shard_map/add | solution.py:36
  386.8 9.8 %reshape.238 = f32[30,2,30,2,512]{4,3,2,1,0:T(2,128)} reshape(f32[1,60,60,512]{3,2,1,0:T(8,128)} %copy.50) | data formatting | bytes 14745600 | tf_op jit(solution)/shard_map/reshape | solution.py:41
  396.6 15.8 %gather_fusion = f32[435,2,2,512]{3,2,1,0:T(2,128)} fusion(f32[30,2,30,2,512]{4,3,2,1,0:T(2,128)} %reshape.238, s32[435]{0:T(512)S(1)} %bitcast.113), kind=kCustom, calls=%fused_computation | custom fusion | bytes 7130520 | tf_op jit(solution)/shard_map/gather | solution.py:41
  422.8 147.9 %all-reduce.3.cloned.1.call-done = f32[128,2,4,435]{3,0,2,1:T(8,128)} async-done(((f32[128,2,4,435]{3,0,2,1:T(8,128)}), f32[128,2,4,435]{3,0,2,1:T(8,128)}) %all-reduce.3.cloned.1.call-update) | async-done | bytes 1781776
  (50 shorter events, 27.0 us)
Async XLA Ops:
  6.5 78.7 %copy-start = (f32[64,512]{1,0:T(8,128)S(1)}, f32[64,512]{1,0:T(8,128)}, u32[]{:S(2)}) copy-start(f32[64,512]{1,0:T(8,128)} %param.7) | copy-start | bytes 393220
  77.3 7.8 %copy-start.9 = (s32[1,2,30]{2,1,0:T(2,128)S(1)}, s32[1,2,30]{2,1,0:T(2,128)}, u32[]{:S(2)}) copy-start(s32[1,2,30]{2,1,0:T(2,128)} %param.6) | copy-start | bytes 724
  77.4 8.7 %copy-start.8 = (s32[435,2]{0,1:T(2,128)S(1)}, s32[435,2]{0,1:T(2,128)}, u32[]{:S(2)}) copy-start(s32[435,2]{0,1:T(2,128)} %param.8) | copy-start | bytes 10444
  77.4 80.7 %all-to-all-start = ((bf16[16,2,61440]{2,1,0:T(2,128)(2,1)}), bf16[16,2,61440]{2,1,0:T(2,128)(2,1)}, u32[]{:S(2)}, u32[]{:S(2)}) async-start(bf16[16,2,61440]{2,1,0:T(2,128)(2,1)} %reshape.293), calls=%async_computation | async-start | bytes 7864320 | tf_op jit(solution)/shard_map/all_to_all | solution.py:22
  84.9 485.8 %all-reduce.3.cloned.1.call-start = ((), (), s32[]{:S(2)}) async-start(), calls=%async_computation.1 | async-start | bytes 4194304
  277.0 11.8 %copy-start.2 = (bf16[32,60,512]{1,0,2:T(8,128)(2,1)S(1)}, bf16[32,60,512]{1,0,2:T(8,128)(2,1)}, u32[]{:S(2)}) copy-start(bf16[32,60,512]{1,0,2:T(8,128)(2,1)} %copy.48) | copy-start | bytes 5898244
  277.0 11.8 %copy-start.3 = (bf16[32,60,512]{1,0,2:T(8,128)(2,1)S(1)}, bf16[32,60,512]{1,0,2:T(8,128)(2,1)}, u32[]{:S(2)}) copy-start(bf16[32,60,512]{1,0,2:T(8,128)(2,1)} %copy.46) | copy-start | bytes 5898244
  412.4 3.3 copy-start.4
  412.4 3.3 copy-start.5
  412.4 3.6 copy-start.6
  412.4 3.9 copy-start.7
  416.3 2.5 copy-start.10
  421.0 151.3 %copy-start.1 = (f32[64,512]{1,0:T(8,128)S(1)}, f32[64,512]{1,0:T(8,128)}, u32[]{:S(2)}) copy-start(f32[64,512]{1,0:T(8,128)} %param.7) | copy-start | bytes 393220
Sparse Core Ops, SparseCore 0:
  422.9 147.7 all-reduce.2
where the time goes:
time: 587 us; the launch traced here: 579 us
  local copies, waits for them, and re-layouts  294 us (50%)
  waiting for transfers between devices  180 us (31%)
  matrix products  53.9 us (9%)
  other arithmetic  30 us (5%)
  between operations  13.8 us (2%)
  starting transfers between devices  7.78 us (1%)
    unnamed x2, waiting for transfers between devices  148 us
    unnamed x29, local copies, waits for them, and re-layouts  121 us
    dot_general x4, matrix products, correlate(): jnp.einsum('gtaf,gtbf->gabf', left_part, right_part, preferred_element_ty...  51.6 us
    all_to_all x1, local copies, waits for them, and re-layouts, on_device(): lax.all_to_all(voltage_frequency_samples, 'chan', split_axis=4, concat_ax...  40.6 us
    all_to_all x1, waiting for transfers between devices, on_device(): lax.all_to_all(voltage_frequency_samples, 'chan', split_axis=4, concat_ax...  31.7 us
    cos x1, other arithmetic, on_device(): cosine = jnp.cos(phase_diff)  26.2 us
    another operation x4, local copies, waits for them, and re-layouts  24.5 us
    gather x1, local copies, waits for them, and re-layouts, on_device(): vis_imag.reshape(full_shape)  16.1 us
  transfers between devices with their start and end apart: 2, of which 2 were waited for; matrix products, arithmetic and copies ran while one was open for 7% of the time, Pallas kernels for 0%

commit v1 on v0

v1 whole, which is shorter than its diff:
```python
import functools

import jax
import jax.numpy as jnp
import numpy as np
from jax import lax
from jax.experimental import pallas as pl
from jax.experimental.pallas import tpu as pltpu
from jax.sharding import Mesh
from jax.sharding import PartitionSpec as P

Q = 64
LANES = 128
HALF = 64
ROW = 8
GROUP = 2
TURN = 65536.0
COSINE = (-0.9999992251396179, 19.738981246948242, -64.92865753173828, 85.27162170410156, -58.79049301147461, 21.07110595703125)
VMEM = pl.BlockSpec(memory_space=pltpu.VMEM)
SMEM = pl.BlockSpec(memory_space=pltpu.SMEM)
ANY = pl.BlockSpec(memory_space=pl.ANY)


def iota(shape, dim):
    return lax.broadcasted_iota(jnp.int32, shape, dim)


def params(mib):
    return pltpu.CompilerParams(vmem_limit_bytes=mib * 1024 * 1024)


def pack_kernel(turning_ref, bins_ref, out_ref):
    entries, fine = turning_ref.shape
    rows = fine // 2
    codes = jnp.round(turning_ref[...] * (TURN / (2.0 * np.pi)))
    flipped = codes.T
    pair = jnp.concatenate([flipped[:rows], flipped[rows:]], axis=1)
    out_ref[0:rows, :] = pair.astype(jnp.int32).astype(jnp.int16)
    spare = jnp.zeros((out_ref.shape[0] - rows - bins_ref.shape[0], LANES), jnp.int32)
    out_ref[rows:, :] = jnp.concatenate([bins_ref[...], spare], axis=0).astype(jnp.int16)


def encode(block):
    top = jnp.max(jnp.max(jnp.abs(block), axis=0, keepdims=True), axis=1, keepdims=True)
    power = jnp.floor(jnp.log2(jnp.maximum(top, 1e-30)))
    code = jnp.clip(jnp.round(block * jnp.exp2(14.0 - power)), -32767.0, 32767.0)
    code = jnp.where(iota(block.shape, 0) == 60, power, code)
    return code.astype(jnp.int32).astype(jnp.int16)


def decode(code):
    code = code.astype(jnp.int32).astype(jnp.float32)
    scale = jnp.exp2(code[60:61, 0:1] - 14.0)
    return code * scale


def correlate_kernel(
    place_ref, own_ref, other_ref, entry_ref, *rest, chips, near, far, pairs, spectra, fine
):
    blocks = rest[: 2 * chips]
    outs = rest[2 * chips : 2 * chips + GROUP * near]
    held, raw, even, odd, source_v, source_s, sems, source_sem = rest[2 * chips + GROUP * near :]
    chip = place_ref[0]
    core = place_ref[1]
    slots = raw.shape[1]
    q_here = 2 * far * near * pairs

    def fetch(side, slot):
        ref = (own_ref, other_ref)[side]
        return pltpu.make_async_copy(
            ref.at[:, :, :, :, pl.ds(pl.multiple_of(slot * LANES, LANES), LANES)],
            raw.at[side, slot, :, :, pl.ds(0, ref.shape[2])],
            sems.at[side, slot],
        )

    def start(slot, _):
        for side in range(2):
            raw[side, slot, :, :, 30:32] = jnp.zeros((2, spectra, 2, 2, LANES), jnp.bfloat16)
            fetch(side, slot).start()
        return 0

    lax.fori_loop(0, slots, start, 0)

    above = (iota((fine, fine), 0) < iota((fine, fine), 1)).astype(jnp.bfloat16)
    carry = jnp.zeros((q_here, 1), jnp.float32)
    found = jnp.zeros((2 * q_here, LANES), jnp.float32)
    bases = []
    for index in range(2 * chips):
        owner = (chip ^ (index % chips)) * 2 + (core if index < chips else 1 - core)
        bases.append(owner * fine)
        rows = blocks[index][fine // 2 : fine // 2 + 16, :].astype(jnp.int32)
        bins = jnp.concatenate([rows[r : r + 1, :] for r in range(fine // LANES)], axis=1)
        per = 2 * pairs
        bin_owner = bins // per
        relative = (bin_owner // 2) ^ chip
        label = ((relative % near) * far + relative // near) * per + bins % per
        label = jnp.where(bin_owner % 2 == core, label, -1)
        hit = iota((q_here, fine), 0) == label
        hit_b = hit.astype(jnp.bfloat16)
        before = jnp.dot(hit_b, above, preferred_element_type=jnp.float32)
        rank = jnp.sum(jnp.where(hit, before + carry, 0.0), axis=0, keepdims=True)
        carry = carry + before[:, fine - 1 : fine] + hit_b[:, fine - 1 : fine].astype(jnp.float32)
        at_rank = (iota((LANES, fine), 0) == rank.astype(jnp.int32)).astype(jnp.bfloat16)
        lane = iota((q_here, fine), 1)
        high = jnp.where(hit, owner * (fine // LANES) + lane // LANES, 0)
        low = jnp.where(hit, lane % LANES, 0)
        ids = jnp.concatenate([high, low], axis=0).astype(jnp.float32).astype(jnp.bfloat16)
        found = found + lax.dot_general(
            ids, at_rank, (((1,), (1,)), ((), ())), preferred_element_type=jnp.float32
        )
    source_v[...] = ((found[:q_here] * LANES + found[q_here:]) * ROW).astype(jnp.int32)
    to_scalar = pltpu.make_async_copy(source_v, source_s, source_sem)
    to_scalar.start()

    row = iota((2 * LANES, LANES), 0)
    weight = jnp.where(row < LANES, 2.0**-8, 2.0**-16)
    columns = []
    for half in range(2):
        for centre in range(GROUP):
            wanted = entry_ref[centre : centre + 1, :]
            match = (row % HALF == wanted) & ((row // HALF) % 2 == half)
            columns.append(jnp.where(match, weight, 0.0).astype(jnp.bfloat16))
    spread = jnp.concatenate(columns, axis=1)
    for index in range(2 * chips):
        code = blocks[index][0 : fine // 2, :].astype(jnp.int32).astype(jnp.float32)
        high = jnp.floor(code * (1.0 / 256.0))
        low = code - 256.0 * high
        digits = jnp.concatenate([high, low], axis=1).astype(jnp.bfloat16)
        turns = jnp.dot(digits, spread, preferred_element_type=jnp.float32)
        for half in range(2):
            for centre in range(GROUP):
                column = (half * GROUP + centre) * LANES
                first = (bases[index] + half * (fine // 2)) * ROW + 2 * spectra + centre
                held[pl.ds(first, fine // 2, stride=ROW), :] = turns[:, column : column + LANES]

    eye = (iota((2 * LANES, 2 * LANES), 0) == iota((2 * LANES, 2 * LANES), 1)).astype(jnp.bfloat16)

    def flip(step, _):
        for side in range(2):
            for unit in range(2):
                slot = step * 4 + unit * 2
                fetch(side, slot).wait()
                fetch(side, slot + 1).wait()
                parts = []
                for k in range(2):
                    block = raw[side, slot + k].reshape(2 * spectra * HALF, LANES)
                    parts.append(
                        jnp.concatenate(
                            [
                                block[(part * spectra + t) * HALF : (part * spectra + t + 1) * HALF]
                                for t in range(spectra)
                                for part in range(2)
                            ],
                            axis=0,
                        )
                    )
                flat = jnp.concatenate(parts, axis=1)
                tall = lax.dot_general(
                    eye, flat, (((1,), (1,)), ((), ())), preferred_element_type=jnp.float32
                )
                for t in range(spectra):
                    first = slot * LANES * ROW + side * spectra + t
                    held[pl.ds(first, 2 * LANES, stride=ROW), :] = tall[:, t * LANES : (t + 1) * LANES]
        return 0

    lax.fori_loop(0, slots // 4, flip, 0)
    to_scalar.wait()

    def gather(pair, into):
        for unit in range(2):
            for first in range(0, LANES, 32):
                at = [source_s[2 * pair + unit, first + k] for k in range(32)]
                rows = [held[pl.ds(pl.multiple_of(a, ROW), ROW), :] for a in at]
                for k in range(32):
                    into[pl.ds((unit * LANES + first + k) * ROW, ROW), :] = rows[k]

    lane = iota((LANES, LANES), 1)
    left = lane < HALF
    quarter = jnp.where(left, 0.0, 0.25)
    upper = (iota((HALF, LANES), 1) % HALF) > iota((HALF, LANES), 0)
    left_h = iota((HALF, LANES), 1) < HALF

    def compute(held_rows):
        packed = [[], []]
        for unit in range(2):
            base = unit * LANES * ROW
            volts = [held_rows[pl.ds(base + t, LANES, stride=ROW), :] for t in range(2 * spectra)]
            swapped = [pltpu.roll(v, HALF, 1) for v in volts]
            for centre in range(GROUP):
                turns = held_rows[pl.ds(base + 2 * spectra + centre, LANES, stride=ROW), :]
                z = jnp.abs(turns - quarter) - 0.5
                z = z * z
                wave = jnp.full_like(z, COSINE[-1])
                for coefficient in COSINE[-2::-1]:
                    wave = wave * z + coefficient
                turned = pltpu.roll(wave, HALF, 1)
                cosine = jnp.where(left, wave, turned)
                sine = jnp.where(left, turned, -wave)
                rotated = jnp.concatenate(
                    [v * cosine + s * sine for v, s in zip(volts, swapped)], axis=0
                )
                coarse = rotated.astype(jnp.bfloat16)
                rest_of = (rotated - coarse.astype(jnp.float32)).astype(jnp.bfloat16)
                both = jnp.concatenate([coarse, rest_of], axis=1)
                product = lax.dot_general(
                    coarse, both, (((0,), (0,)), ((), ())), preferred_element_type=jnp.float32
                )
                product = product[:, :LANES] + product[:, LANES:]
                under = pltpu.roll(product[HALF:], HALF, 1)
                packed[centre].append(product[:HALF] + jnp.where(left_h, under, -under))
        results = []
        for centre in range(GROUP):
            first, second = packed[centre]
            first = jnp.where(upper, first, pltpu.roll(first, HALF, 1))
            second = jnp.where(upper, pltpu.roll(second, HALF, 1), second)
            results.append(jnp.where(left_h, first, second))
        return results

    def store(out_ref, at, value):
        if out_ref.dtype == jnp.int16:
            value = encode(value)
        out_ref[pl.ds(pl.multiple_of(at * HALF, HALF), HALF), :] = value

    each = far * pairs
    last = near * each - 1
    gather(0, even)
    for y in range(near):

        def two(step, _):
            pair = y * each + 2 * step
            gather(jnp.minimum(pair + 1, last), odd)
            for centre, value in enumerate(compute(even)):
                store(outs[centre * near + y], 2 * step, value)
            gather(jnp.minimum(pair + 2, last), even)
            for centre, value in enumerate(compute(odd)):
                store(outs[centre * near + y], 2 * step + 1, value)
            return 0

        lax.fori_loop(0, each // 2, two, 0)


def merge_kernel(own_ref, *refs, arrivals, far, pairs):
    own_out = refs[arrivals]
    outs = refs[arrivals + 1 :]
    for z in range(far):
        for pair in range(pairs):
            at = pl.ds((z * pairs + pair) * HALF, HALF)
            total = own_ref[at, :]
            for ref in refs[:arrivals]:
                total = total + decode(ref[at, :])
            to = pl.ds(pair * HALF, HALF)
            if z == 0:
                own_out[to, :] = total
            else:
                outs[z - 1][to, :] = encode(total)


def finish_kernel(members_ref, own_ref, *refs, arrivals, pairs, scale):
    out_ref = refs[arrivals]
    baselines = members_ref.shape[1]
    first = members_ref[0:1, :]
    second = members_ref[1:2, :]
    rising = first < second
    station = iota((HALF, baselines), 0)
    for pair in range(pairs):
        at = pl.ds(pair * HALF, HALF)
        total = own_ref[at, :]
        for ref in refs[:arrivals]:
            total = total + decode(ref[at, :])
        total = total * scale
        total = jnp.where(iota(total.shape, 0) < 60, total, 0.0)
        flipped = total.T
        coarse = flipped.astype(jnp.bfloat16)
        medium = (flipped - coarse.astype(jnp.float32)).astype(jnp.bfloat16)
        fine = (flipped - coarse.astype(jnp.float32) - medium.astype(jnp.float32)).astype(jnp.bfloat16)
        stack = jnp.concatenate([coarse, medium, fine], axis=0)
        picked = {}
        for side, members in enumerate((first, second)):
            for p in range(2):
                choose = (station == 2 * members + p).astype(jnp.bfloat16)
                rows = jnp.dot(stack, choose, preferred_element_type=jnp.float32)
                rows = rows[:LANES] + rows[LANES : 2 * LANES] + rows[2 * LANES :]
                partner = second if side == 0 else first
                for half in range(2):
                    for p2 in range(2):
                        match = station == 2 * partner + p2
                        part = rows[half * HALF : (half + 1) * HALF]
                        picked[side, half, p, p2] = jnp.sum(
                            jnp.where(match, part, 0.0), axis=0, keepdims=True
                        )
        for half in range(2):
            real, imaginary = [], []
            for p in range(2):
                for p2 in range(2):
                    a = picked[0, half, p, p2]
                    b = picked[1, half, p2, p]
                    real.append(jnp.where(rising, a, b))
                    imaginary.append(jnp.where(rising, b, -a))
            out_ref[2 * pair + half, 0] = jnp.concatenate(real, axis=0)
            out_ref[2 * pair + half, 1] = jnp.concatenate(imaginary, axis=0)


def on_device(volts, entry, turning, members, target, *, tm, chips):
    near = max(1, chips // 4)
    far = chips // near
    fine = turning.shape[1]
    spectra = volts.shape[1]
    centres = entry.shape[1]
    per_device = Q // (2 * chips)
    pairs = per_device // 2
    channels = volts.shape[4]

    def across_chips(x, step):
        return lax.ppermute(x, "chip", [(i, i ^ step) for i in range(chips)])

    def across_cores(x):
        return lax.ppermute(x, "core", [(0, 1), (1, 0)])

    other = across_cores(volts)
    block = pl.pallas_call(
        pack_kernel,
        in_specs=[VMEM, VMEM],
        out_specs=VMEM,
        out_shape=jax.ShapeDtypeStruct((fine // 2 + 16, LANES), jnp.int16),
        name="pack",
    )(turning, target.reshape(fine // LANES, LANES))
    gathered = {0: block}
    step = chips // 2
    while step:
        for known in list(gathered):
            gathered[known ^ step] = across_chips(gathered[known], step)
        step //= 2
    mine = [gathered[k] for k in range(chips)]
    theirs = [across_cores(x) for x in mine]

    chip = lax.axis_index("chip")
    core = lax.axis_index("core")
    x = lax.axis_index("tm")
    place = jnp.stack([chip, core]).astype(jnp.int32)
    order = jnp.arange(centres, dtype=jnp.int32) ^ x
    lanes = jnp.repeat(entry[0], 2, axis=1)
    lanes = jnp.pad(lanes, ((0, 0), (0, HALF - lanes.shape[1])), constant_values=-1)
    lanes = jnp.concatenate([lanes, lanes], axis=1)
    lanes = jnp.take(lanes, order, axis=0)

    sums = {}
    for first in range(0, centres, GROUP):
        kinds = [
            jnp.float32 if first + c == 0 and y == 0 else jnp.int16
            for c in range(GROUP)
            for y in range(near)
        ]
        results = pl.pallas_call(
            functools.partial(
                correlate_kernel,
                chips=chips,
                near=near,
                far=far,
                pairs=pairs,
                spectra=spectra,
                fine=fine,
            ),
            in_specs=[SMEM, ANY, ANY, VMEM] + [VMEM] * (2 * chips),
            out_specs=[VMEM] * (GROUP * near),
            out_shape=[
                jax.ShapeDtypeStruct((far * pairs * HALF, LANES), kind) for kind in kinds
            ],
            scratch_shapes=[
                pltpu.VMEM((channels * ROW, LANES), jnp.float32),
                pltpu.VMEM((2, channels // LANES, 2, spectra, 32, 2, LANES), jnp.bfloat16),
                pltpu.VMEM((2 * LANES * ROW, LANES), jnp.float32),
                pltpu.VMEM((2 * LANES * ROW, LANES), jnp.float32),
                pltpu.VMEM((Q // 2, LANES), jnp.int32),
                pltpu.SMEM((Q // 2, LANES), jnp.int32),
                pltpu.SemaphoreType.DMA((2, channels // LANES)),
                pltpu.SemaphoreType.DMA,
            ],
            compiler_params=params(58),
            name="correlate",
        )(place, volts, other, lanes[first : first + GROUP], *mine, *theirs)
        for c in range(GROUP):
            for y in range(near):
                sums[first + c, y] = results[c * near + y]

    flat = [(a, b) for a in range(tm) for b in range(chips)]
    arrived = []
    for c in range(centres):
        for y in range(near):
            if c or y:
                route = [(a * chips + b, (a ^ c) * chips + (b ^ y)) for a, b in flat]
                arrived.append(lax.ppermute(sums[c, y], ("tm", "chip"), route))
    rows = pairs * HALF
    merged = pl.pallas_call(
        functools.partial(merge_kernel, arrivals=len(arrived), far=far, pairs=pairs),
        in_specs=[VMEM] * (1 + len(arrived)),
        out_specs=[VMEM] * far,
        out_shape=[
            jax.ShapeDtypeStruct((rows, LANES), jnp.int16 if z else jnp.float32)
            for z in range(far)
        ],
        name="merge",
    )(sums[0, 0], *arrived)
    final = [across_chips(merged[z], z * near) for z in range(1, far)]
    return pl.pallas_call(
        functools.partial(finish_kernel, arrivals=len(final), pairs=pairs, scale=Q / channels),
        in_specs=[VMEM] * (2 + len(final)),
        out_specs=VMEM,
        out_shape=jax.ShapeDtypeStruct((per_device, 2, 4, members.shape[0]), jnp.float32),
        name="finish",
    )(members.T, merged[0], *final)


def solution(mesh):
    tm = mesh.shape["tm"]
    chips = mesh.shape["chan"] // 2
    inner = Mesh(mesh.devices.reshape(tm, chips, 2), ("tm", "chip", "core"))
    every = ("tm", "chip", "core")
    split = ("chip", "core")
    return jax.shard_map(
        functools.partial(on_device, tm=tm, chips=chips),
        mesh=inner,
        in_specs=(
            P(None, every, None, None, None),
            P("tm", None, None),
            P(None, split),
            P(),
            P(split),
        ),
        out_specs=P(every, None, None, None),
        check_vma=False,
    )
```

time: 587 us -> 91.1 us (0.16); the launches traced: 579 us -> 90.9 us
  local copies, waits for them, and re-layouts: 294 us -> 3.22 us
  waiting for transfers between devices: 180 us -> 15 us
  matrix products: 53.9 us -> 0 us
  Pallas kernels: 0 us -> 49.9 us
  other arithmetic: 30 us -> 1.35 us
  between operations: 13.8 us -> 0.29 us
  starting transfers between devices: 7.78 us -> 21.1 us
    unnamed x2 -> x0, waiting for transfers between devices: 148 us -> none
    unnamed x29 -> x42, local copies, waits for them, and re-layouts: 121 us -> 1.8 us
    dot_general x6 -> x0, matrix products: 53.9 us -> none  [the longest x4 51.6 us: correlate(): jnp.einsum('gtaf,gtbf->gabf', left_part, right_part, preferred_element_ty...]
    pallas_call x0 -> x4, Pallas kernels: none -> 49.9 us  [the longest x1 43.4 us: on_device(): pl.pallas_call(functools.partial(correlate_kernel, chips=chips, near=near...]
    all_to_all x1 -> x0, local copies, waits for them, and re-layouts: 40.6 us -> none  [on_device(): lax.all_to_all(voltage_frequency_samples, 'chan', split_axis=4, concat_ax...]
    gather x6 -> x1, local copies, waits for them, and re-layouts: 40.6 us -> 0.56 us  [on_device(): lanes = jnp.take(lanes, order, axis=0)]
    all_to_all x1 -> x0, waiting for transfers between devices: 31.7 us -> none  [on_device(): lax.all_to_all(voltage_frequency_samples, 'chan', split_axis=4, concat_ax...]
    cos x1 -> x0, other arithmetic: 26.2 us -> none  [on_device(): cosine = jnp.cos(phase_diff)]
  transfers between devices with their start and end apart: 2 -> 22, of which waited for: 2 -> 9; matrix products, arithmetic and copies ran while one was open for 7% -> 3% of each run, Pallas kernels for 0% -> 2%
where the time goes in v1:
time: 91.1 us; the launch traced here: 90.9 us
  Pallas kernels  49.9 us (55%)
  starting transfers between devices  21.1 us (23%)
  waiting for transfers between devices  15 us (16%)
  local copies, waits for them, and re-layouts  3.22 us (4%)
  other arithmetic  1.35 us (1%)
    pallas_call x1, Pallas kernels, on_device(): pl.pallas_call(functools.partial(correlate_kernel, chips=chips, near=near...  43.4 us
    ppermute x10, starting transfers between devices, across_chips(): return lax.ppermute(x, 'chip', [(i, i ^ step) for i in range(chips)])  16.3 us
    ppermute x10, waiting for transfers between devices, across_chips(): return lax.ppermute(x, 'chip', [(i, i ^ step) for i in range(chips)])  8.16 us
    ppermute x3, waiting for transfers between devices, on_device(): arrived.append(lax.ppermute(sums[c, y], ('tm', 'chip'), route))  6.26 us
    ppermute x3, starting transfers between devices, on_device(): arrived.append(lax.ppermute(sums[c, y], ('tm', 'chip'), route))  3.55 us
    pallas_call x1, Pallas kernels, on_device(): pl.pallas_call(functools.partial(finish_kernel, arrivals=len(final), pair...  2.77 us
    pallas_call x1, Pallas kernels, on_device(): pl.pallas_call(functools.partial(merge_kernel, arrivals=len(arrived), far...  1.98 us
  transfers between devices with their start and end apart: 22, of which 9 were waited for; matrix products, arithmetic and copies ran while one was open for 3% of the time, Pallas kernels for 2%

profile of v1, /device:TPU:0, one launch (start us, length us, event | category | flops | bytes accessed | tf_op | source)
XLA Modules:
  0.0 90.9 jit_solution(17072485965401613472)
XLA Ops:
  0.5 1.8 %pack.1.rest_0_ = s16[272,128]{1,0:T(8,128)(2,1)} custom-call(f32[64,512]{1,0:T(8,128)} %turning_ref.1, s32[4,128]{1,0:T(4,128)} %bitcast.8), custom_call_target="tpu_custom_call" | custom-call | tf_op jit(solution)/shard_map/pack/pallas_call | solution.py:320
  2.3 4.0 %collective-permute-start.4 = (s16[272,128]{1,0:T(8,128)(2,1)}, s16[272,128]{1,0:T(8,128)(2,1)S(1)}, u32[]{:S(2)}, u32[]{:S(2)}) collective-permute-start(s16[272,128]{1,0:T(8,128)(2,1)} %pack.1.rest_0_), channel_id=1, source_target_pairs={{0,8},{2,10},{4,12},{6,14},{8,0},{10,2},{12,4},{14,6},{1,9},{3,11}... | collective-permute-start | bytes 208904 | tf_op jit(solution)/shard_map/ppermute | solution.py:314
  6.3 1.6 %collective-permute-start.2 = (s16[272,128]{1,0:T(8,128)(2,1)}, s16[272,128]{1,0:T(8,128)(2,1)S(1)}, u32[]{:S(2)}, u32[]{:S(2)}) collective-permute-start(s16[272,128]{1,0:T(8,128)(2,1)} %pack.1.rest_0_), channel_id=1, source_target_pairs={{0,4},{2,6},{4,0},{6,2},{8,12},{10,14},{12,8},{14,10},{1,5},{3,7},... | collective-permute-start | bytes 208904 | tf_op jit(solution)/shard_map/ppermute | solution.py:314
  7.9 1.5 %collective-permute-start.1 = (s16[272,128]{1,0:T(8,128)(2,1)}, s16[272,128]{1,0:T(8,128)(2,1)S(1)}, u32[]{:S(2)}, u32[]{:S(2)}) collective-permute-start(s16[272,128]{1,0:T(8,128)(2,1)} %pack.1.rest_0_), channel_id=1, source_target_pairs={{0,2},{2,0},{4,6},{6,4},{8,10},{10,8},{12,14},{14,12},{1,3},{3,1},... | collective-permute-start | bytes 208904 | tf_op jit(solution)/shard_map/ppermute | solution.py:314
  9.4 0.7 broadcast_in_dim.14
  11.6 1.3 %collective-permute-start.5 = (s16[272,128]{1,0:T(8,128)(2,1)S(1)}, s16[272,128]{1,0:T(8,128)(2,1)S(1)}, u32[]{:S(2)}, u32[]{:S(2)}) collective-permute-start(s16[272,128]{1,0:T(8,128)(2,1)S(1)} %collective-permute-done.4.rest_4_), channel_id=1, source_target_pairs={{0,2},{2,0},{4,6},{6,4},{8,10},{10,8},{12,14},{14,12},{1,3},{3,1},... | collective-permute-start | bytes 208904 | tf_op jit(solution)/shard_map/ppermute | solution.py:314
  13.0 1.0 %collective-permute-start.3 = (s16[272,128]{1,0:T(8,128)(2,1)S(1)}, s16[272,128]{1,0:T(8,128)(2,1)S(1)}, u32[]{:S(2)}, u32[]{:S(2)}) collective-permute-start(s16[272,128]{1,0:T(8,128)(2,1)S(1)} %collective-permute-done.2.rest_2_), channel_id=1, source_target_pairs={{0,2},{2,0},{4,6},{6,4},{8,10},{10,8},{12,14},{14,12},{1,3},{3,1},... | collective-permute-start | bytes 208904 | tf_op jit(solution)/shard_map/ppermute | solution.py:314
  14.0 1.6 %collective-permute-done.6.rest_6_ = s16[272,128]{1,0:T(8,128)(2,1)S(1)} collective-permute-done((s16[272,128]{1,0:T(8,128)(2,1)S(1)}, s16[272,128]{1,0:T(8,128)(2,1)S(1)}, u32[]{:S(2)}, u32[]{:S(2)}) %collective-permute-start.6) | collective-permute-done | bytes 69664 | tf_op jit(solution)/shard_map/ppermute | solution.py:314
  15.9 1.4 %collective-permute-start.7 = (s16[272,128]{1,0:T(8,128)(2,1)S(1)}, s16[272,128]{1,0:T(8,128)(2,1)S(1)}, u32[]{:S(2)}, u32[]{:S(2)}) collective-permute-start(s16[272,128]{1,0:T(8,128)(2,1)S(1)} %collective-permute-done.6.rest_6_), channel_id=1, source_target_pairs={{0,2},{2,0},{4,6},{6,4},{8,10},{10,8},{12,14},{14,12},{1,3},{3,1},... | collective-permute-start | bytes 208904 | tf_op jit(solution)/shard_map/ppermute | solution.py:314
  18.6 1.7 %collective-permute-done.7.rest_7_ = s16[272,128]{1,0:T(8,128)(2,1)S(1)} collective-permute-done((s16[272,128]{1,0:T(8,128)(2,1)S(1)}, s16[272,128]{1,0:T(8,128)(2,1)S(1)}, u32[]{:S(2)}, u32[]{:S(2)}) %collective-permute-start.7) | collective-permute-done | bytes 69664 | tf_op jit(solution)/shard_map/ppermute | solution.py:314
  22.1 43.4 %correlate.1 = (f32[512,128]{1,0:T(8,128)}, s16[512,128]{1,0:T(8,128)(2,1)}, s16[512,128]{1,0:T(8,128)(2,1)}, s16[512,128]{1,0:T(8,128)(2,1)}) custom-call(s32[2]{0:T(128)} %pad_add_fusion.1.place_ref, bf16[2,2,30,2,8192]{4,3,2,1,0:T(2,128)(2,1)} %own_ref.1, bf16[2,2,30,2,8192]{4,3,2,1,0:T(2,128)(2,1)} %collective-permute-done.other_ref, ...), custom_call_target="tpu_custom_call" | custom-call | tf_op jit(solution)/shard_map/correlate/pallas_call | solution.py:353
  65.5 1.5 %collective-permute-start.16 = (s16[512,128]{1,0:T(8,128)(2,1)}, s16[512,128]{1,0:T(8,128)(2,1)S(1)}, u32[]{:S(2)}, u32[]{:S(2)}) collective-permute-start(s16[512,128]{1,0:T(8,128)(2,1)} %get-tuple-element.14), channel_id=1, source_target_pairs={{0,2},{2,0},{4,6},{6,4},{8,10},{10,8},{12,14},{14,12},{16,18},{18,... | collective-permute-start | bytes 393224 | tf_op jit(solution)/shard_map/ppermute | solution.py:391
  67.0 1.5 %collective-permute-start.17 = (s16[512,128]{1,0:T(8,128)(2,1)}, s16[512,128]{1,0:T(8,128)(2,1)S(1)}, u32[]{:S(2)}, u32[]{:S(2)}) collective-permute-start(s16[512,128]{1,0:T(8,128)(2,1)} %get-tuple-element.15), channel_id=1, source_target_pairs={{0,16},{2,18},{4,20},{6,22},{8,24},{10,26},{12,28},{14,30},{16,0},... | collective-permute-start | bytes 393224 | tf_op jit(solution)/shard_map/ppermute | solution.py:391
  69.1 2.3 %collective-permute-done.16.refs_0_ = s16[512,128]{1,0:T(8,128)(2,1)S(1)} collective-permute-done((s16[512,128]{1,0:T(8,128)(2,1)}, s16[512,128]{1,0:T(8,128)(2,1)S(1)}, u32[]{:S(2)}, u32[]{:S(2)}) %collective-permute-start.16) | collective-permute-done | bytes 131104 | tf_op jit(solution)/shard_map/ppermute | solution.py:391
  71.4 2.2 %collective-permute-done.17.refs_1_ = s16[512,128]{1,0:T(8,128)(2,1)S(1)} collective-permute-done((s16[512,128]{1,0:T(8,128)(2,1)}, s16[512,128]{1,0:T(8,128)(2,1)S(1)}, u32[]{:S(2)}, u32[]{:S(2)}) %collective-permute-start.17) | collective-permute-done | bytes 131104 | tf_op jit(solution)/shard_map/ppermute | solution.py:391
  73.6 1.8 %collective-permute-done.18.refs_2_ = s16[512,128]{1,0:T(8,128)(2,1)S(1)} collective-permute-done((s16[512,128]{1,0:T(8,128)(2,1)}, s16[512,128]{1,0:T(8,128)(2,1)S(1)}, u32[]{:S(2)}, u32[]{:S(2)}) %collective-permute-start.18) | collective-permute-done | bytes 131104 | tf_op jit(solution)/shard_map/ppermute | solution.py:391
  75.4 0.7 copy-done.2
  76.0 2.0 %merge.1 = (f32[128,128]{1,0:T(8,128)}, s16[128,128]{1,0:T(8,128)(2,1)}, s16[128,128]{1,0:T(8,128)(2,1)}, s16[128,128]{1,0:T(8,128)(2,1)}) custom-call(f32[512,128]{1,0:T(8,128)} %get-tuple-element.13.own_ref, s16[512,128]{1,0:T(8,128)(2,1)} %copy-done, s16[512,128]{1,0:T(8,128)(2,1)} %copy-done.1, s16[512,128]{1,0:T(8,128)(2,1)} %copy-done.2), custom_call_target="tpu_custom_call" | custom-call | tf_op jit(solution)/shard_map/merge/pallas_call | solution.py:393
  78.0 1.8 %collective-permute-start.19 = (s16[128,128]{1,0:T(8,128)(2,1)}, s16[128,128]{1,0:T(8,128)(2,1)S(1)}, u32[]{:S(2)}, u32[]{:S(2)}) collective-permute-start(s16[128,128]{1,0:T(8,128)(2,1)} %get-tuple-element.18), channel_id=1, source_target_pairs={{0,4},{2,6},{4,0},{6,2},{8,12},{10,14},{12,8},{14,10},{1,5},{3,7},... | collective-permute-start | bytes 98312 | tf_op jit(solution)/shard_map/ppermute | solution.py:314
  79.8 1.7 %collective-permute-start.20 = (s16[128,128]{1,0:T(8,128)(2,1)}, s16[128,128]{1,0:T(8,128)(2,1)S(1)}, u32[]{:S(2)}, u32[]{:S(2)}) collective-permute-start(s16[128,128]{1,0:T(8,128)(2,1)} %get-tuple-element.19), channel_id=1, source_target_pairs={{0,8},{2,10},{4,12},{6,14},{8,0},{10,2},{12,4},{14,6},{1,9},{3,11}... | collective-permute-start | bytes 98312 | tf_op jit(solution)/shard_map/ppermute | solution.py:314
  81.6 1.3 %collective-permute-start.21 = (s16[128,128]{1,0:T(8,128)(2,1)}, s16[128,128]{1,0:T(8,128)(2,1)S(1)}, u32[]{:S(2)}, u32[]{:S(2)}) collective-permute-start(s16[128,128]{1,0:T(8,128)(2,1)} %get-tuple-element.20), channel_id=1, source_target_pairs={{0,12},{2,14},{4,8},{6,10},{8,4},{10,6},{12,0},{14,2},{1,13},{3,15... | collective-permute-start | bytes 98312 | tf_op jit(solution)/shard_map/ppermute | solution.py:314
  82.9 2.2 %collective-permute-done.20.refs_1_ = s16[128,128]{1,0:T(8,128)(2,1)S(1)} collective-permute-done((s16[128,128]{1,0:T(8,128)(2,1)}, s16[128,128]{1,0:T(8,128)(2,1)S(1)}, u32[]{:S(2)}, u32[]{:S(2)}) %collective-permute-start.20) | collective-permute-done | bytes 32800 | tf_op jit(solution)/shard_map/ppermute | solution.py:314
  85.0 2.4 %collective-permute-done.21.refs_2_ = s16[128,128]{1,0:T(8,128)(2,1)S(1)} collective-permute-done((s16[128,128]{1,0:T(8,128)(2,1)}, s16[128,128]{1,0:T(8,128)(2,1)S(1)}, u32[]{:S(2)}, u32[]{:S(2)}) %collective-permute-start.21) | collective-permute-done | bytes 32800 | tf_op jit(solution)/shard_map/ppermute | solution.py:314
  88.1 2.8 %finish.1 = f32[4,2,4,435]{3,2,1,0:T(4,128)} custom-call(s32[2,435]{1,0:T(2,128)} %bitcast.7, f32[128,128]{1,0:T(8,128)} %get-tuple-element.17.own_ref, s16[128,128]{1,0:T(8,128)(2,1)} %copy-done.18, s16[128,128]{1,0:T(8,128)(2,1)} %copy-done.19, s16[128,128]{1,0:T(8,128)(2,1)} %copy-done.20), custom_call_target="tpu_custom_call" | custom-call | tf_op jit(solution)/shard_map/finish/pallas_call | solution.py:404
  (76 shorter events, 6.4 us)
Async XLA Ops:
  0.0 21.5 %collective-permute-start = (bf16[2,2,30,2,8192]{4,3,2,1,0:T(2,128)(2,1)}, bf16[2,2,30,2,8192]{4,3,2,1,0:T(2,128)(2,1)}, u32[]{:S(2)}, u32[]{:S(2)}) collective-permute-start(bf16[2,2,30,2,8192]{4,3,2,1,0:T(2,128)(2,1)} %own_ref.1), channel_id=1, source_target_pairs={{0,1},{1,0},{2,3},{3,2},{4,5},{5,4},{6,7},{7,6},{8,9},{9,8},{10,11... | collective-permute-start | bytes 11796488 | tf_op jit(solution)/shard_map/ppermute | solution.py:317
  2.2 8.8 %collective-permute-start.8 = (s16[272,128]{1,0:T(8,128)(2,1)}, s16[272,128]{1,0:T(8,128)(2,1)S(1)}, u32[]{:S(2)}, u32[]{:S(2)}) collective-permute-start(s16[272,128]{1,0:T(8,128)(2,1)} %pack.1.rest_0_), channel_id=1, source_target_pairs={{0,1},{1,0},{2,3},{3,2},{4,5},{5,4},{6,7},{7,6},{8,9},{9,8},{10,11... | collective-permute-start | bytes 208904 | tf_op jit(solution)/shard_map/ppermute | solution.py:317
  2.3 8.7 %collective-permute-start.4 = (s16[272,128]{1,0:T(8,128)(2,1)}, s16[272,128]{1,0:T(8,128)(2,1)S(1)}, u32[]{:S(2)}, u32[]{:S(2)}) collective-permute-start(s16[272,128]{1,0:T(8,128)(2,1)} %pack.1.rest_0_), channel_id=1, source_target_pairs={{0,8},{2,10},{4,12},{6,14},{8,0},{10,2},{12,4},{14,6},{1,9},{3,11}... | collective-permute-start | bytes 208904 | tf_op jit(solution)/shard_map/ppermute | solution.py:314
  6.3 5.3 %collective-permute-start.2 = (s16[272,128]{1,0:T(8,128)(2,1)}, s16[272,128]{1,0:T(8,128)(2,1)S(1)}, u32[]{:S(2)}, u32[]{:S(2)}) collective-permute-start(s16[272,128]{1,0:T(8,128)(2,1)} %pack.1.rest_0_), channel_id=1, source_target_pairs={{0,4},{2,6},{4,0},{6,2},{8,12},{10,14},{12,8},{14,10},{1,5},{3,7},... | collective-permute-start | bytes 208904 | tf_op jit(solution)/shard_map/ppermute | solution.py:314
  7.9 5.0 %collective-permute-start.1 = (s16[272,128]{1,0:T(8,128)(2,1)}, s16[272,128]{1,0:T(8,128)(2,1)S(1)}, u32[]{:S(2)}, u32[]{:S(2)}) collective-permute-start(s16[272,128]{1,0:T(8,128)(2,1)} %pack.1.rest_0_), channel_id=1, source_target_pairs={{0,2},{2,0},{4,6},{6,4},{8,10},{10,8},{12,14},{14,12},{1,3},{3,1},... | collective-permute-start | bytes 208904 | tf_op jit(solution)/shard_map/ppermute | solution.py:314
  10.9 10.6 %copy-start.4 = (s16[272,128]{1,0:T(8,128)(2,1)}, s16[272,128]{1,0:T(8,128)(2,1)S(1)}, u32[]{:S(2)}) copy-start(s16[272,128]{1,0:T(8,128)(2,1)S(1)} %collective-permute-done.4.rest_4_) | copy-start | bytes 208900
  11.0 2.0 %collective-permute-start.12 = (s16[272,128]{1,0:T(8,128)(2,1)S(1)}, s16[272,128]{1,0:T(8,128)(2,1)S(1)}, u32[]{:S(2)}, u32[]{:S(2)}) collective-permute-start(s16[272,128]{1,0:T(8,128)(2,1)S(1)} %collective-permute-done.4.rest_4_), channel_id=1, source_target_pairs={{0,1},{1,0},{2,3},{3,2},{4,5},{5,4},{6,7},{7,6},{8,9},{9,8},{10,11... | collective-permute-start | bytes 208904 | tf_op jit(solution)/shard_map/ppermute | solution.py:317
  11.0 10.5 %copy-start.3 = (s16[272,128]{1,0:T(8,128)(2,1)}, s16[272,128]{1,0:T(8,128)(2,1)S(1)}, u32[]{:S(2)}) copy-start(s16[272,128]{1,0:T(8,128)(2,1)S(1)} %collective-permute-done.8.rest_8_) | copy-start | bytes 208900
  11.1 4.6 %collective-permute-start.6 = (s16[272,128]{1,0:T(8,128)(2,1)S(1)}, s16[272,128]{1,0:T(8,128)(2,1)S(1)}, u32[]{:S(2)}, u32[]{:S(2)}) collective-permute-start(s16[272,128]{1,0:T(8,128)(2,1)S(1)} %collective-permute-done.4.rest_4_), channel_id=1, source_target_pairs={{0,4},{2,6},{4,0},{6,2},{8,12},{10,14},{12,8},{14,10},{1,5},{3,7},... | collective-permute-start | bytes 208904 | tf_op jit(solution)/shard_map/ppermute | solution.py:314
  11.6 4.3 %collective-permute-start.5 = (s16[272,128]{1,0:T(8,128)(2,1)S(1)}, s16[272,128]{1,0:T(8,128)(2,1)S(1)}, u32[]{:S(2)}, u32[]{:S(2)}) collective-permute-start(s16[272,128]{1,0:T(8,128)(2,1)S(1)} %collective-permute-done.4.rest_4_), channel_id=1, source_target_pairs={{0,2},{2,0},{4,6},{6,4},{8,10},{10,8},{12,14},{14,12},{1,3},{3,1},... | collective-permute-start | bytes 208904 | tf_op jit(solution)/shard_map/ppermute | solution.py:314
  12.9 5.1 %collective-permute-start.10 = (s16[272,128]{1,0:T(8,128)(2,1)S(1)}, s16[272,128]{1,0:T(8,128)(2,1)S(1)}, u32[]{:S(2)}, u32[]{:S(2)}) collective-permute-start(s16[272,128]{1,0:T(8,128)(2,1)S(1)} %collective-permute-done.2.rest_2_), channel_id=1, source_target_pairs={{0,1},{1,0},{2,3},{3,2},{4,5},{5,4},{6,7},{7,6},{8,9},{9,8},{10,11... | collective-permute-start | bytes 208904 | tf_op jit(solution)/shard_map/ppermute | solution.py:317
  13.0 5.0 %collective-permute-start.3 = (s16[272,128]{1,0:T(8,128)(2,1)S(1)}, s16[272,128]{1,0:T(8,128)(2,1)S(1)}, u32[]{:S(2)}, u32[]{:S(2)}) collective-permute-start(s16[272,128]{1,0:T(8,128)(2,1)S(1)} %collective-permute-done.2.rest_2_), channel_id=1, source_target_pairs={{0,2},{2,0},{4,6},{6,4},{8,10},{10,8},{12,14},{14,12},{1,3},{3,1},... | collective-permute-start | bytes 208904 | tf_op jit(solution)/shard_map/ppermute | solution.py:314
  15.6 2.8 %collective-permute-start.9 = (s16[272,128]{1,0:T(8,128)(2,1)S(1)}, s16[272,128]{1,0:T(8,128)(2,1)S(1)}, u32[]{:S(2)}, u32[]{:S(2)}) collective-permute-start(s16[272,128]{1,0:T(8,128)(2,1)S(1)} %collective-permute-done.1.rest_1_), channel_id=1, source_target_pairs={{0,1},{1,0},{2,3},{3,2},{4,5},{5,4},{6,7},{7,6},{8,9},{9,8},{10,11... | collective-permute-start | bytes 208904 | tf_op jit(solution)/shard_map/ppermute | solution.py:317
  15.9 4.4 %collective-permute-start.7 = (s16[272,128]{1,0:T(8,128)(2,1)S(1)}, s16[272,128]{1,0:T(8,128)(2,1)S(1)}, u32[]{:S(2)}, u32[]{:S(2)}) collective-permute-start(s16[272,128]{1,0:T(8,128)(2,1)S(1)} %collective-permute-done.6.rest_6_), channel_id=1, source_target_pairs={{0,2},{2,0},{4,6},{6,4},{8,10},{10,8},{12,14},{14,12},{1,3},{3,1},... | collective-permute-start | bytes 208904 | tf_op jit(solution)/shard_map/ppermute | solution.py:314
  18.0 2.9 %collective-permute-start.14 = (s16[272,128]{1,0:T(8,128)(2,1)S(1)}, s16[272,128]{1,0:T(8,128)(2,1)S(1)}, u32[]{:S(2)}, u32[]{:S(2)}) collective-permute-start(s16[272,128]{1,0:T(8,128)(2,1)S(1)} %collective-permute-done.6.rest_6_), channel_id=1, source_target_pairs={{0,1},{1,0},{2,3},{3,2},{4,5},{5,4},{6,7},{7,6},{8,9},{9,8},{10,11... | collective-permute-start | bytes 208904 | tf_op jit(solution)/shard_map/ppermute | solution.py:317
  18.0 2.9 %collective-permute-start.13 = (s16[272,128]{1,0:T(8,128)(2,1)S(1)}, s16[272,128]{1,0:T(8,128)(2,1)S(1)}, u32[]{:S(2)}, u32[]{:S(2)}) collective-permute-start(s16[272,128]{1,0:T(8,128)(2,1)S(1)} %collective-permute-done.5.rest_5_), channel_id=1, source_target_pairs={{0,1},{1,0},{2,3},{3,2},{4,5},{5,4},{6,7},{7,6},{8,9},{9,8},{10,11... | collective-permute-start | bytes 208904 | tf_op jit(solution)/shard_map/ppermute | solution.py:317
  18.5 2.4 %collective-permute-start.11 = (s16[272,128]{1,0:T(8,128)(2,1)S(1)}, s16[272,128]{1,0:T(8,128)(2,1)S(1)}, u32[]{:S(2)}, u32[]{:S(2)}) collective-permute-start(s16[272,128]{1,0:T(8,128)(2,1)S(1)} %collective-permute-done.3.rest_3_), channel_id=1, source_target_pairs={{0,1},{1,0},{2,3},{3,2},{4,5},{5,4},{6,7},{7,6},{8,9},{9,8},{10,11... | collective-permute-start | bytes 208904 | tf_op jit(solution)/shard_map/ppermute | solution.py:317
  20.2 1.3 %collective-permute-start.15 = (s16[272,128]{1,0:T(8,128)(2,1)S(1)}, s16[272,128]{1,0:T(8,128)(2,1)S(1)}, u32[]{:S(2)}, u32[]{:S(2)}) collective-permute-start(s16[272,128]{1,0:T(8,128)(2,1)S(1)} %collective-permute-done.7.rest_7_), channel_id=1, source_target_pairs={{0,1},{1,0},{2,3},{3,2},{4,5},{5,4},{6,7},{7,6},{8,9},{9,8},{10,11... | collective-permute-start | bytes 208904 | tf_op jit(solution)/shard_map/ppermute | solution.py:317
  65.5 5.8 %collective-permute-start.16 = (s16[512,128]{1,0:T(8,128)(2,1)}, s16[512,128]{1,0:T(8,128)(2,1)S(1)}, u32[]{:S(2)}, u32[]{:S(2)}) collective-permute-start(s16[512,128]{1,0:T(8,128)(2,1)} %get-tuple-element.14), channel_id=1, source_target_pairs={{0,2},{2,0},{4,6},{6,4},{8,10},{10,8},{12,14},{14,12},{16,18},{18,... | collective-permute-start | bytes 393224 | tf_op jit(solution)/shard_map/ppermute | solution.py:391
  67.0 6.6 %collective-permute-start.17 = (s16[512,128]{1,0:T(8,128)(2,1)}, s16[512,128]{1,0:T(8,128)(2,1)S(1)}, u32[]{:S(2)}, u32[]{:S(2)}) collective-permute-start(s16[512,128]{1,0:T(8,128)(2,1)} %get-tuple-element.15), channel_id=1, source_target_pairs={{0,16},{2,18},{4,20},{6,22},{8,24},{10,26},{12,28},{14,30},{16,0},... | collective-permute-start | bytes 393224 | tf_op jit(solution)/shard_map/ppermute | solution.py:391
  68.5 6.9 %collective-permute-start.18 = (s16[512,128]{1,0:T(8,128)(2,1)}, s16[512,128]{1,0:T(8,128)(2,1)S(1)}, u32[]{:S(2)}, u32[]{:S(2)}) collective-permute-start(s16[512,128]{1,0:T(8,128)(2,1)} %get-tuple-element.16), channel_id=1, source_target_pairs={{0,18},{2,16},{4,22},{6,20},{8,26},{10,24},{12,30},{14,28},{16,2},... | collective-permute-start | bytes 393224 | tf_op jit(solution)/shard_map/ppermute | solution.py:391
  78.0 4.9 %collective-permute-start.19 = (s16[128,128]{1,0:T(8,128)(2,1)}, s16[128,128]{1,0:T(8,128)(2,1)S(1)}, u32[]{:S(2)}, u32[]{:S(2)}) collective-permute-start(s16[128,128]{1,0:T(8,128)(2,1)} %get-tuple-element.18), channel_id=1, source_target_pairs={{0,4},{2,6},{4,0},{6,2},{8,12},{10,14},{12,8},{14,10},{1,5},{3,7},... | collective-permute-start | bytes 98312 | tf_op jit(solution)/shard_map/ppermute | solution.py:314
  79.8 5.2 %collective-permute-start.20 = (s16[128,128]{1,0:T(8,128)(2,1)}, s16[128,128]{1,0:T(8,128)(2,1)S(1)}, u32[]{:S(2)}, u32[]{:S(2)}) collective-permute-start(s16[128,128]{1,0:T(8,128)(2,1)} %get-tuple-element.19), channel_id=1, source_target_pairs={{0,8},{2,10},{4,12},{6,14},{8,0},{10,2},{12,4},{14,6},{1,9},{3,11}... | collective-permute-start | bytes 98312 | tf_op jit(solution)/shard_map/ppermute | solution.py:314
  81.6 5.9 %collective-permute-start.21 = (s16[128,128]{1,0:T(8,128)(2,1)}, s16[128,128]{1,0:T(8,128)(2,1)S(1)}, u32[]{:S(2)}, u32[]{:S(2)}) collective-permute-start(s16[128,128]{1,0:T(8,128)(2,1)} %get-tuple-element.20), channel_id=1, source_target_pairs={{0,12},{2,14},{4,8},{6,10},{8,4},{10,6},{12,0},{14,2},{1,13},{3,15... | collective-permute-start | bytes 98312 | tf_op jit(solution)/shard_map/ppermute | solution.py:314
  (19 other events, 67.5 us)

commit v2 on v0

v2 whole, which is shorter than its diff:
```python
import functools

import jax
import jax.numpy as jnp
import numpy as np
from jax import lax
from jax.experimental import pallas as pl
from jax.experimental.pallas import tpu as pltpu
from jax.sharding import Mesh
from jax.sharding import PartitionSpec as P

Q = 64
LANES = 128
HALF = 64
WIDTH = 256
GROUP = 2
TURN = 65536.0
COSINE = (-0.9999992251396179, 19.738981246948242, -64.92865753173828, 85.27162170410156, -58.79049301147461, 21.07110595703125)
VMEM = pl.BlockSpec(memory_space=pltpu.VMEM)
SMEM = pl.BlockSpec(memory_space=pltpu.SMEM)
ANY = pl.BlockSpec(memory_space=pl.ANY)
HBM = pl.BlockSpec(memory_space=pltpu.HBM)


def iota(shape, dim):
    return lax.broadcasted_iota(jnp.int32, shape, dim)


def params(mib):
    return pltpu.CompilerParams(vmem_limit_bytes=mib * 1024 * 1024)


def cost(microseconds):
    return pl.CostEstimate(
        flops=int(microseconds * 1.0e9), bytes_accessed=int(microseconds * 3.0e6), transcendentals=0
    )


def pack_kernel(turning_hbm, bins_hbm, out_ref, turning_ref, bins_ref, sems):
    entries, fine = turning_ref.shape
    rows = fine // 2
    copies = [
        pltpu.make_async_copy(turning_hbm, turning_ref, sems.at[0]),
        pltpu.make_async_copy(bins_hbm, bins_ref, sems.at[1]),
    ]
    for copy in copies:
        copy.start()
    for copy in copies:
        copy.wait()
    codes = jnp.round(turning_ref[...] * (TURN / (2.0 * np.pi)))
    flipped = codes.T
    pair = jnp.concatenate([flipped[:rows], flipped[rows:]], axis=1)
    out_ref[0:rows, :] = pair.astype(jnp.int32).astype(jnp.int16)
    spare = jnp.zeros((out_ref.shape[0] - rows - bins_ref.shape[0], LANES), jnp.int32)
    out_ref[rows:, :] = jnp.concatenate([bins_ref[...], spare], axis=0).astype(jnp.int16)


def stack_kernel(after_ref, *refs):
    del after_ref
    out_ref = refs[-1]
    size = refs[0].shape[0]
    for k, ref in enumerate(refs[:-1]):
        out_ref[k * size : (k + 1) * size, :] = ref[...]


def encode(block):
    top = jnp.max(jnp.max(jnp.abs(block), axis=0, keepdims=True), axis=1, keepdims=True)
    power = jnp.floor(jnp.log2(jnp.maximum(top, 1e-30)))
    code = jnp.clip(jnp.round(block * jnp.exp2(14.0 - power)), -32767.0, 32767.0)
    code = jnp.where(iota(block.shape, 0) == 60, power, code)
    return code.astype(jnp.int32).astype(jnp.int16)


def decode(code):
    code = code.astype(jnp.int32).astype(jnp.float32)
    scale = jnp.exp2(code[60:61, 0:1] - 14.0)
    return code * scale


def rows_kernel(volts_ref, *rest, first, depth):
    held, raw, sems = rest[-3:]
    parts, spectra, stations = volts_ref.shape[:3]
    width = raw.shape[-1]
    steps = raw.shape[0]
    unroll = 4

    def fetch(step):
        return pltpu.make_async_copy(
            volts_ref.at[:, :, :, :, pl.ds(pl.multiple_of(step * width, width), width)],
            raw.at[step, :, :, pl.ds(0, stations)],
            sems.at[step],
        )

    def start(step, _):
        raw[step, :, :, stations:] = jnp.zeros(
            (parts, spectra, raw.shape[3] - stations, 2, width), jnp.bfloat16
        )
        fetch(step).start()
        return 0

    lax.fori_loop(0, steps, start, 0)

    def flip(group, _):
        for unit in range(unroll):
            fetch(group * unroll + unit).wait()
        for unit in range(unroll):
            step = group * unroll + unit
            for k in range(width // LANES):
                block = raw[step, :, :, :, :, k * LANES : (k + 1) * LANES]
                block = block.reshape(parts * spectra * HALF, LANES)
                for t in range(spectra):
                    both = jnp.concatenate(
                        [
                            block[(part * spectra + t) * HALF : (part * spectra + t + 1) * HALF]
                            for part in range(parts)
                        ],
                        axis=0,
                    )
                    at = (step * width + k * LANES) * depth + first + t
                    held[pl.ds(at, LANES, stride=depth), :] = both.astype(jnp.float32).T
        return 0

    lax.fori_loop(0, steps // unroll, flip, 0)


def prepare_kernel(
    place_ref, entry_ref, after_ref, *rest, columns, started, group, near, far, per, fine
):
    del after_ref
    stacks = rest[: len(columns)]
    rest = rest[len(columns) :]
    if started:
        carry_in, found_in, _ = rest[:3]
        rest = rest[3:]
    carry_ref, found_ref, turns_ref, source_ref = rest
    chip = place_ref[0]
    core = place_ref[1]
    x = place_ref[2]
    q_here = source_ref.shape[0]
    per_bits = per.bit_length() - 1
    near_bits = near.bit_length() - 1
    size = fine // 2 + 16
    blocks = [
        (stack, z * size, (chip ^ (z * near + column)) * 2 + (1 - core if other else core))
        for stack, (column, other) in zip(stacks, columns)
        for z in range(far)
    ]

    stations = entry_ref.shape[2]
    twice = (iota((stations, HALF), 0) == (iota((stations, HALF), 1) >> 1)).astype(jnp.bfloat16)
    entries = jnp.concatenate(
        [
            jnp.dot(
                entry_ref[0, pl.ds((group * GROUP + c) ^ x, 1), :]
                .astype(jnp.float32)
                .astype(jnp.bfloat16),
                twice,
                preferred_element_type=jnp.float32,
            )
            for c in range(GROUP)
        ],
        axis=1,
    ).astype(jnp.int32)
    row = iota((2 * LANES, LANES), 0)
    weight = jnp.where(row < LANES, 2.0**-8, 2.0**-16)
    spread = jnp.concatenate(
        [
            jnp.where(
                ((row & (HALF - 1)) == entries) & (((row >> 6) & 1) == half), weight, 0.0
            ).astype(jnp.bfloat16)
            for half in range(2)
        ],
        axis=1,
    )
    code = jnp.concatenate([stack[at : at + fine // 2, :] for stack, at, _ in blocks], axis=0)
    code = code.astype(jnp.int32).astype(jnp.float32)
    high = jnp.floor(code * (1.0 / 256.0))
    digits = jnp.concatenate([high, code - 256.0 * high], axis=1).astype(jnp.bfloat16)
    turns = jnp.dot(digits, spread, preferred_element_type=jnp.float32)
    for index, (_, _, owner) in enumerate(blocks):
        for half in range(2):
            at = pl.multiple_of((owner * 2 + half) * (fine // 2), fine // 2)
            turns_ref[pl.ds(at, fine // 2), :] = turns[
                index * (fine // 2) : (index + 1) * (fine // 2), half * LANES : (half + 1) * LANES
            ]

    if started:
        carry = carry_in[:, 0:1]
        found = found_in[...]
    else:
        carry = jnp.zeros((q_here, 1), jnp.float32)
        found = jnp.zeros((2 * q_here, LANES), jnp.float32)
    lane = iota((q_here, fine), 1)
    hits = []
    for stack, at, _ in blocks:
        tail = stack[at + fine // 2 : at + size, :].astype(jnp.int32)
        bins = jnp.concatenate([tail[r : r + 1, :] for r in range(fine // LANES)], axis=1)
        bin_owner = bins >> per_bits
        relative = (bin_owner >> 1) ^ chip
        label = ((relative & (near - 1)) * far + (relative >> near_bits)) * per
        label = label + (bins & (per - 1))
        label = jnp.where((bin_owner & 1) == core, label, -1)
        hits.append(jnp.where(iota((q_here, fine), 0) == label, 1.0, 0.0))
    above = (iota((fine, fine), 0) < iota((fine, fine), 1)).astype(jnp.bfloat16)
    every = jnp.concatenate(hits, axis=0).astype(jnp.bfloat16)
    every = jnp.dot(every, above, preferred_element_type=jnp.float32)
    ids, at_rank = [], []
    for index, (hit, (_, _, owner)) in enumerate(zip(hits, blocks)):
        before = every[index * q_here : (index + 1) * q_here]
        rank = jnp.sum(hit * (before + carry), axis=0, keepdims=True)
        carry = carry + before[:, fine - 1 : fine] + hit[:, fine - 1 : fine]
        at_rank.append((iota((LANES, fine), 0) == rank.astype(jnp.int32)).astype(jnp.bfloat16))
        high = hit * (owner * (fine // LANES) + (lane >> 7)).astype(jnp.float32)
        low = hit * (lane & (LANES - 1)).astype(jnp.float32)
        ids.append(jnp.concatenate([high, low], axis=0).astype(jnp.bfloat16))
    found = found + lax.dot_general(
        jnp.concatenate(ids, axis=1),
        jnp.concatenate(at_rank, axis=1),
        (((1,), (1,)), ((), ())),
        preferred_element_type=jnp.float32,
    )
    carry_ref[...] = jnp.broadcast_to(carry, carry_ref.shape)
    found_ref[...] = found
    source_ref[...] = (found[:q_here] * LANES + found[q_here:]).astype(jnp.int32)


def wave(z):
    value = jnp.full_like(z, COSINE[-1])
    for coefficient in COSINE[-2::-1]:
        value = value * z + coefficient
    return value


def correlate_kernel(source_ref, held, turns_ref, *rest, first_pair, pairs, spectra):
    outs = rest[:GROUP]
    even, odd, even_turns, odd_turns, wide_even, wide_odd, kept = rest[GROUP:]
    depth = 2 * spectra

    def gather(unit, into, into_turns):
        for first in range(0, LANES, 32):
            at = [source_ref[unit, first + k] for k in range(32)]
            rows = [held[pl.ds(pl.multiple_of(a * depth, depth), depth), :] for a in at]
            turns = [turns_ref[pl.ds(a, 1), :] for a in at]
            for k in range(32):
                into[(first + k) * depth : (first + k + 1) * depth, :] = rows[k]
                into_turns[first + k : first + k + 1, :] = turns[k]

    upper = (iota((HALF, LANES), 1) & (HALF - 1)) > iota((HALF, LANES), 0)
    left = iota((HALF, LANES), 1) < HALF

    def rotate(rows, turns, wide):
        turns = turns[...].T
        turning = []
        for centre in range(GROUP):
            angle = turns[centre * HALF : (centre + 1) * HALF]
            cosine = jnp.abs(angle) - 0.5
            sine = jnp.abs(angle - 0.25) - 0.5
            turning.append((wave(cosine * cosine), wave(sine * sine)))
        for t in range(2 * spectra):
            volts = rows[pl.ds(t, LANES, stride=depth), :].T
            real, imaginary = volts[:HALF], volts[HALF:]
            columns = slice(t * LANES, (t + 1) * LANES)
            for centre in range(GROUP):
                cosine, sine = turning[centre]
                rotated = (real * cosine + imaginary * sine, imaginary * cosine - real * sine)
                for part, value in enumerate(rotated):
                    coarse = value.astype(jnp.bfloat16)
                    rest_of = (value - coarse.astype(jnp.float32)).astype(jnp.bfloat16)
                    wide[centre, part * HALF : (part + 1) * HALF, columns] = coarse
                    wide[centre, LANES + part * HALF : LANES + (part + 1) * HALF, columns] = rest_of

    def correlate(wide):
        results = []
        for centre in range(GROUP):
            product = lax.dot_general(
                wide[centre],
                wide[centre, :LANES],
                (((1,), (1,)), ((), ())),
                preferred_element_type=jnp.float32,
            )
            product = product[:LANES] + product[LANES:]
            under = pltpu.roll(product[HALF:], HALF, 1)
            results.append(product[:HALF] + jnp.where(left, under, -under))
        return results

    def emit(pair, seconds):
        for centre in range(GROUP):
            first, second = kept[centre], seconds[centre]
            first = jnp.where(upper, first, pltpu.roll(first, HALF, 1))
            second = jnp.where(upper, pltpu.roll(second, HALF, 1), second)
            value = jnp.where(left, first, second)
            out_ref = outs[centre]
            if out_ref.dtype == jnp.int16:
                value = encode(value)
            out_ref[pl.ds(pl.multiple_of(pair * HALF, HALF), HALF), :] = value

    base = 2 * first_pair
    last = base + 2 * pairs - 1
    gather(base, even, even_turns)
    wide_odd[...] = jnp.zeros_like(wide_odd)
    kept[...] = jnp.zeros_like(kept)

    def one(pair, _):
        unit = base + 2 * pair
        gather(unit + 1, odd, odd_turns)
        rotate(even, even_turns, wide_even)
        emit(jnp.maximum(pair - 1, 0), correlate(wide_odd))
        gather(jnp.minimum(unit + 2, last), even, even_turns)
        rotate(odd, odd_turns, wide_odd)
        for centre, value in enumerate(correlate(wide_even)):
            kept[centre] = value
        return 0

    lax.fori_loop(0, pairs, one, 0)
    emit(pairs - 1, correlate(wide_odd))


def merge_kernel(own_ref, *refs, arrivals, far, pairs):
    own_out = refs[arrivals]
    outs = refs[arrivals + 1 :]
    for z in range(far):
        for pair in range(pairs):
            at = pl.ds((z * pairs + pair) * HALF, HALF)
            total = own_ref[at, :]
            for ref in refs[:arrivals]:
                total = total + decode(ref[at, :])
            to = pl.ds(pair * HALF, HALF)
            if z == 0:
                own_out[to, :] = total
            else:
                outs[z - 1][to, :] = encode(total)


def finish_kernel(members_ref, own_ref, *refs, arrivals, pairs, scale):
    out_ref = refs[arrivals]
    baselines = members_ref.shape[1]
    first = members_ref[0:1, :]
    second = members_ref[1:2, :]
    rising = first < second
    station = iota((HALF, baselines), 0)
    for pair in range(pairs):
        at = pl.ds(pair * HALF, HALF)
        total = own_ref[at, :]
        for ref in refs[:arrivals]:
            total = total + decode(ref[at, :])
        total = total * scale
        total = jnp.where(iota(total.shape, 0) < 60, total, 0.0)
        flipped = total.T
        coarse = flipped.astype(jnp.bfloat16)
        medium = (flipped - coarse.astype(jnp.float32)).astype(jnp.bfloat16)
        fine = (flipped - coarse.astype(jnp.float32) - medium.astype(jnp.float32)).astype(jnp.bfloat16)
        stack = jnp.concatenate([coarse, medium, fine], axis=0)
        picked = {}
        for side, members in enumerate((first, second)):
            for p in range(2):
                choose = (station == 2 * members + p).astype(jnp.bfloat16)
                rows = jnp.dot(stack, choose, preferred_element_type=jnp.float32)
                rows = rows[:LANES] + rows[LANES : 2 * LANES] + rows[2 * LANES :]
                partner = second if side == 0 else first
                for half in range(2):
                    for p2 in range(2):
                        match = station == 2 * partner + p2
                        part = rows[half * HALF : (half + 1) * HALF]
                        picked[side, half, p, p2] = jnp.sum(
                            jnp.where(match, part, 0.0), axis=0, keepdims=True
                        )
        for half in range(2):
            real, imaginary = [], []
            for p in range(2):
                for p2 in range(2):
                    a = picked[0, half, p, p2]
                    b = picked[1, half, p2, p]
                    real.append(jnp.where(rising, a, b))
                    imaginary.append(jnp.where(rising, b, -a))
            out_ref[2 * pair + half, 0] = jnp.concatenate(real, axis=0)
            out_ref[2 * pair + half, 1] = jnp.concatenate(imaginary, axis=0)


def on_device(volts, entry, turning, members, target, *, tm, chips):
    near = max(1, chips // 4)
    far = chips // near
    fine = turning.shape[1]
    spectra = volts.shape[1]
    centres = entry.shape[1]
    per_device = Q // (2 * chips)
    pairs = per_device // 2
    channels = volts.shape[4]

    def across_chips(x, step):
        return lax.ppermute(x, "chip", [(i, i ^ step) for i in range(chips)])

    def across_cores(x):
        return lax.ppermute(x, "core", [(0, 1), (1, 0)])

    chip = lax.axis_index("chip")
    core = lax.axis_index("core")
    x = lax.axis_index("tm")
    place = jnp.stack([chip, core, x]).astype(jnp.int32)
    other = across_cores(volts)
    block = pl.pallas_call(
        pack_kernel,
        in_specs=[HBM, HBM],
        out_specs=VMEM,
        out_shape=jax.ShapeDtypeStruct((fine // 2 + 16, LANES), jnp.int16),
        scratch_shapes=[
            pltpu.VMEM(turning.shape, jnp.float32),
            pltpu.VMEM((fine // LANES, LANES), jnp.int32),
            pltpu.SemaphoreType.DMA((2,)),
        ],
        compiler_params=params(56),
        cost_estimate=cost(1),
        name="pack",
    )(turning, target.reshape(fine // LANES, LANES))
    line = [block] + [across_chips(block, z * near) for z in range(1, far)]

    held_type = pltpu.VMEM((channels * 2 * spectra, LANES), jnp.float32)

    def rows(side, *operands):
        return pl.pallas_call(
            functools.partial(rows_kernel, first=side * spectra, depth=2 * spectra),
            in_specs=[HBM, ANY, VMEM][: 2 + side],
            out_specs=VMEM,
            out_shape=held_type,
            scratch_shapes=[
                pltpu.VMEM((channels // WIDTH, 2, spectra, 32, 2, WIDTH), jnp.bfloat16),
                pltpu.SemaphoreType.DMA((channels // WIDTH,)),
            ],
            input_output_aliases={2: 0} if side else {},
            compiler_params=params(44),
            cost_estimate=cost(5),
            name="rows",
        )(*operands)

    held = rows(0, volts, place)
    size = block.shape[0]
    stack = pl.pallas_call(
        stack_kernel,
        in_specs=[ANY] + [VMEM] * far,
        out_specs=VMEM,
        out_shape=jax.ShapeDtypeStruct((far * size, LANES), jnp.int16),
        compiler_params=params(4),
        cost_estimate=cost(1),
        name="stack",
    )(held, *line)
    mine = [stack] + [across_chips(stack, y) for y in range(1, near)]
    theirs = [across_cores(stack)]
    held = rows(1, other, place, held)
    each = far * pairs
    arrived = []
    flat = [(a, b) for a in range(tm) for b in range(chips)]

    def exchange(value, c, y):
        route = [(a * chips + b, (a ^ c) * chips + (b ^ y)) for a, b in flat]
        return lax.ppermute(value, ("tm", "chip"), route)

    for group in range(centres // GROUP):
        state = ()
        for part in range(3 if near > 1 else 1):
            if part == 0:
                columns = [(0, False), (0, True)]
            else:
                columns = [(y, part == 2) for y in range(1, near)]
            if part == 1 and group == 0:
                state, mine = lax.optimization_barrier((state, mine))
                theirs += [across_cores(value) for value in mine[1:]]
            stacks = [(theirs if across else mine)[y] for y, across in columns]
            *state, source = pl.pallas_call(
                functools.partial(
                    prepare_kernel,
                    columns=columns,
                    started=part > 0,
                    group=group,
                    near=near,
                    far=far,
                    per=per_device,
                    fine=fine,
                ),
                in_specs=[SMEM, VMEM, ANY] + [VMEM] * (len(stacks) + len(state)),
                out_specs=[VMEM] * 4,
                out_shape=[
                    jax.ShapeDtypeStruct((Q // 2, LANES), jnp.float32),
                    jax.ShapeDtypeStruct((Q, LANES), jnp.float32),
                    pltpu.VMEM((channels, LANES), jnp.float32),
                    jax.ShapeDtypeStruct((Q // 2, LANES), jnp.int32),
                ],
                input_output_aliases={3 + len(stacks) + 2: 2} if part else {},
                compiler_params=params(16),
                cost_estimate=cost(2),
                name="prepare",
            )(place, entry, held, *stacks, *state)
        turns = state[2]
        for y, count in ((1, near - 1), (0, 1)):
            if not count:
                continue
            kinds = [jnp.float32 if group + c + y == 0 else jnp.int16 for c in range(GROUP)]
            results = pl.pallas_call(
                functools.partial(
                    correlate_kernel, first_pair=y * each, pairs=count * each, spectra=spectra
                ),
                in_specs=[SMEM, VMEM, VMEM],
                out_specs=[VMEM] * GROUP,
                out_shape=[
                    jax.ShapeDtypeStruct((count * each * HALF, LANES), kind) for kind in kinds
                ],
                scratch_shapes=[
                    pltpu.VMEM((LANES * 2 * spectra, LANES), jnp.float32),
                    pltpu.VMEM((LANES * 2 * spectra, LANES), jnp.float32),
                    pltpu.VMEM((LANES, LANES), jnp.float32),
                    pltpu.VMEM((LANES, LANES), jnp.float32),
                    pltpu.VMEM((GROUP, 2 * LANES, 2 * spectra * LANES), jnp.bfloat16),
                    pltpu.VMEM((GROUP, 2 * LANES, 2 * spectra * LANES), jnp.bfloat16),
                    pltpu.VMEM((GROUP, HALF, LANES), jnp.float32),
                ],
                compiler_params=params(12),
                cost_estimate=cost(9 * count),
                name="correlate",
            )(source, held, turns)
            for c in range(GROUP):
                for k in range(count):
                    value = results[c]
                    if count > 1:
                        value = value[k * each * HALF : (k + 1) * each * HALF]
                    if group + c + y == 0:
                        total = value
                    else:
                        arrived.append(exchange(value, group * GROUP + c, y + k))
    rows = pairs * HALF
    merged = pl.pallas_call(
        functools.partial(merge_kernel, arrivals=len(arrived), far=far, pairs=pairs),
        in_specs=[VMEM] * (1 + len(arrived)),
        out_specs=[VMEM] * far,
        out_shape=[
            jax.ShapeDtypeStruct((rows, LANES), jnp.int16 if z else jnp.float32)
            for z in range(far)
        ],
        compiler_params=params(6),
        cost_estimate=cost(1),
        name="merge",
    )(total, *arrived)
    final = [across_chips(merged[z], z * near) for z in range(1, far)]
    return pl.pallas_call(
        functools.partial(finish_kernel, arrivals=len(final), pairs=pairs, scale=Q / channels),
        in_specs=[VMEM] * (2 + len(final)),
        out_specs=VMEM,
        out_shape=jax.ShapeDtypeStruct((per_device, 2, 4, members.shape[0]), jnp.float32),
        compiler_params=params(6),
        cost_estimate=cost(2),
        name="finish",
    )(members.T, merged[0], *final)


def solution(mesh):
    tm = mesh.shape["tm"]
    chips = mesh.shape["chan"] // 2
    inner = Mesh(mesh.devices.reshape(tm, chips, 2), ("tm", "chip", "core"))
    every = ("tm", "chip", "core")
    split = ("chip", "core")
    return jax.shard_map(
        functools.partial(on_device, tm=tm, chips=chips),
        mesh=inner,
        in_specs=(
            P(None, every, None, None, None),
            P("tm", None, None),
            P(None, split),
            P(),
            P(split),
        ),
        out_specs=P(every, None, None, None),
        check_vma=False,
    )
```

time: 587 us -> 66.7 us (0.11); the launches traced: 579 us -> 66.6 us
  local copies, waits for them, and re-layouts: 294 us -> 0.02 us
  waiting for transfers between devices: 180 us -> 11.6 us
  matrix products: 53.9 us -> 0 us
  Pallas kernels: 0 us -> 38.3 us
  other arithmetic: 30 us -> 0.59 us
  between operations: 13.8 us -> 0.12 us
  starting transfers between devices: 7.78 us -> 15.9 us
    unnamed x2 -> x0, waiting for transfers between devices: 148 us -> none
    unnamed x29 -> x8, local copies, waits for them, and re-layouts: 121 us -> 0.02 us
    dot_general x6 -> x0, matrix products: 53.9 us -> none  [the longest x4 51.6 us: correlate(): jnp.einsum('gtaf,gtbf->gabf', left_part, right_part, preferred_element_ty...]
    all_to_all x1 -> x0, local copies, waits for them, and re-layouts: 40.6 us -> none  [on_device(): lax.all_to_all(voltage_frequency_samples, 'chan', split_axis=4, concat_ax...]
    gather x6 -> x0, local copies, waits for them, and re-layouts: 40.6 us -> none  [the longest x1 16.1 us: on_device(): vis_imag.reshape(full_shape)]
    pallas_call x0 -> x11, Pallas kernels: none -> 38.3 us  [the longest x2 18.9 us: on_device(): pl.pallas_call(functools.partial(correlate_kernel, first_pair=y * each, p...]
    all_to_all x1 -> x0, waiting for transfers between devices: 31.7 us -> none  [on_device(): lax.all_to_all(voltage_frequency_samples, 'chan', split_axis=4, concat_ax...]
    cos x1 -> x0, other arithmetic: 26.2 us -> none  [on_device(): cosine = jnp.cos(phase_diff)]
  transfers between devices with their start and end apart: 2 -> 13, of which waited for: 2 -> 5; matrix products, arithmetic and copies ran while one was open for 7% -> 1% of each run, Pallas kernels for 0% -> 23%
where the time goes in v2:
time: 66.7 us; the launch traced here: 66.6 us
  Pallas kernels  38.3 us (57%)
  starting transfers between devices  15.9 us (24%)
  waiting for transfers between devices  11.6 us (17%)
    pallas_call x2, Pallas kernels, on_device(): pl.pallas_call(functools.partial(correlate_kernel, first_pair=y * each, p...  18.9 us
    ppermute x7, starting transfers between devices, across_chips(): return lax.ppermute(x, 'chip', [(i, i ^ step) for i in range(chips)])  11.3 us
    pallas_call x2, Pallas kernels, rows(): pl.pallas_call(functools.partial(rows_kernel, first=side * spectra, depth...  8.74 us
    pallas_call x3, Pallas kernels, on_device(): pl.pallas_call(functools.partial(prepare_kernel, columns=columns, started...  6.69 us
    ppermute x3, waiting for transfers between devices, exchange(): return lax.ppermute(value, ('tm', 'chip'), route)  5.93 us
    ppermute x7, waiting for transfers between devices, across_chips(): return lax.ppermute(x, 'chip', [(i, i ^ step) for i in range(chips)])  5.69 us
    ppermute x3, starting transfers between devices, exchange(): return lax.ppermute(value, ('tm', 'chip'), route)  3.55 us
    pallas_call x1, Pallas kernels, on_device(): pl.pallas_call(functools.partial(finish_kernel, arrivals=len(final), pair...  1.92 us
  transfers between devices with their start and end apart: 13, of which 5 were waited for; matrix products, arithmetic and copies ran while one was open for 1% of the time, Pallas kernels for 23%

profile of v2, /device:TPU:0, one launch (start us, length us, event | category | flops | bytes accessed | tf_op | source)
XLA Modules:
  0.0 66.6 jit_solution(12984349886071893451)
XLA Ops:
  0.5 1.8 %pack.1.refs_0_ = s16[272,128]{1,0:T(8,128)(2,1)} custom-call(f32[64,512]{1,0:T(8,128)} %turning_hbm.1, s32[4,128]{1,0:T(4,128)} %bitcast.6), custom_call_target="tpu_custom_call" | custom-call | flops 1000000000 | bytes 3000000 | tf_op jit(solution)/shard_map/pack/pallas_call | solution.py:400
  2.2 4.7 %collective-permute-start.3 = (s16[272,128]{1,0:T(8,128)(2,1)}, s16[272,128]{1,0:T(8,128)(2,1)S(1)}, u32[]{:S(2)}, u32[]{:S(2)}) collective-permute-start(s16[272,128]{1,0:T(8,128)(2,1)} %pack.1.refs_0_), channel_id=1, source_target_pairs={{0,12},{2,14},{4,8},{6,10},{8,4},{10,6},{12,0},{14,2},{1,13},{3,15... | collective-permute-start | bytes 208904 | tf_op jit(solution)/shard_map/ppermute | solution.py:390
  6.9 0.6 collective-permute-start.1
  7.5 0.6 pad_add_fusion.rest_0_.place_ref
  8.1 4.4 %rows.2.rest_1_.after_ref = f32[32768,128]{1,0:T(8,128)S(1)} custom-call(bf16[2,2,30,2,8192]{4,3,2,1,0:T(2,128)(2,1)} %volts_ref.1, s32[3]{0:T(128)} %pad_add_fusion.rest_0_.place_ref), custom_call_target="tpu_custom_call" | custom-call | flops 5000000000 | bytes 15000000 | tf_op jit(solution)/shard_map/rows/pallas_call | solution.py:419
  12.5 1.1 %collective-permute-done.2.refs_2_ = s16[272,128]{1,0:T(8,128)(2,1)S(1)} collective-permute-done((s16[272,128]{1,0:T(8,128)(2,1)}, s16[272,128]{1,0:T(8,128)(2,1)S(1)}, u32[]{:S(2)}, u32[]{:S(2)}) %collective-permute-start.2) | collective-permute-done | bytes 69664 | tf_op jit(solution)/shard_map/ppermute | solution.py:390
  13.6 1.6 %collective-permute-start.5 = (s16[1088,128]{1,0:T(8,128)(2,1)S(1)}, s16[1088,128]{1,0:T(8,128)(2,1)S(1)}, u32[]{:S(2)}, u32[]{:S(2)}) collective-permute-start(s16[1088,128]{1,0:T(8,128)(2,1)S(1)} %stack.17.rest_0_), channel_id=1, source_target_pairs={{0,2},{2,0},{4,6},{6,4},{8,10},{10,8},{12,14},{14,12},{1,3},{3,1},... | collective-permute-start | bytes 835592 | tf_op jit(solution)/shard_map/ppermute | solution.py:390
  15.2 4.4 %rows.3.after_ref.held = f32[32768,128]{1,0:T(8,128)S(1)} custom-call(bf16[2,2,30,2,8192]{4,3,2,1,0:T(2,128)(2,1)} %collective-permute-done.volts_ref, s32[3]{0:T(128)} %pad_add_fusion.rest_0_.place_ref, f32[32768,128]{1,0:T(8,128)S(1)} %rows.2.rest_1_.after_ref), custom_call_target="tpu_custom_call", output_to_operand_aliasing={{}: (2, {})} | custom-call | flops 5000000000 | bytes 15000000 | tf_op jit(solution)/shard_map/rows/pallas_call | solution.py:419
  19.6 2.9 %prepare.3 = (f32[32,128]{1,0:T(8,128)S(1)}, f32[64,128]{1,0:T(8,128)S(1)}, f32[8192,128]{1,0:T(8,128)S(1)}, s32[32,128]{1,0:T(8,128)}) custom-call(s32[3]{0:T(128)S(1)} %copy-done.1, s32[1,2,30]{2,1,0:T(2,128)S(1)} %copy-done.2, f32[32768,128]{1,0:T(8,128)S(1)} %rows.3.after_ref.held, s16[1088,128]{1,0:T(8,128)(2,1)S(1)} %stack.17.rest_0_, ...), custom_call_target="tpu_custom_call" | custom-call | flops 2000000000 | bytes 6000000 | tf_op jit(solution)/shard_map/prepare/pallas_call | solution.py:467
  23.1 1.9 %prepare.4 = (f32[32,128]{1,0:T(8,128)S(1)}, f32[64,128]{1,0:T(8,128)S(1)}, f32[8192,128]{1,0:T(8,128)S(1)}, s32[32,128]{1,0:T(8,128)}) custom-call(s32[3]{0:T(128)S(1)} %copy-done.1, s32[1,2,30]{2,1,0:T(2,128)S(1)} %copy-done.2, f32[32768,128]{1,0:T(8,128)S(1)} %rows.3.after_ref.held, ...), custom_call_target="tpu_custom_call", output_to_operand_aliasing={{2}: (6, {})} | custom-call | flops 2000000000 | bytes 6000000 | tf_op jit(solution)/shard_map/prepare/pallas_call | solution.py:467
  25.0 1.9 %prepare.5 = (f32[32,128]{1,0:T(8,128)}, f32[64,128]{1,0:T(8,128)}, f32[8192,128]{1,0:T(8,128)S(1)}, s32[32,128]{1,0:T(8,128)S(1)}) custom-call(s32[3]{0:T(128)S(1)} %copy-done.1, s32[1,2,30]{2,1,0:T(2,128)S(1)} %copy-done.2, f32[32768,128]{1,0:T(8,128)S(1)} %rows.3.after_ref.held, ...), custom_call_target="tpu_custom_call", output_to_operand_aliasing={{2}: (6, {})} | custom-call | flops 2000000000 | bytes 6000000 | tf_op jit(solution)/shard_map/prepare/pallas_call | solution.py:467
  26.8 9.5 %correlate.3 = (s16[512,128]{1,0:T(8,128)(2,1)S(1)}, s16[512,128]{1,0:T(8,128)(2,1)S(1)}) custom-call(s32[32,128]{1,0:T(8,128)S(1)} %get-tuple-element.35.source_ref, f32[32768,128]{1,0:T(8,128)S(1)} %rows.3.after_ref.held, f32[8192,128]{1,0:T(8,128)S(1)} %get-tuple-element.36.turns_ref), custom_call_target="tpu_custom_call" | custom-call | flops 8999999488 | bytes 27000000 | tf_op jit(solution)/shard_map/correlate/pallas_call | solution.py:496
  36.3 9.5 %correlate.2 = (f32[512,128]{1,0:T(8,128)S(1)}, s16[512,128]{1,0:T(8,128)(2,1)S(1)}) custom-call(s32[32,128]{1,0:T(8,128)S(1)} %get-tuple-element.35.source_ref, f32[32768,128]{1,0:T(8,128)S(1)} %rows.3.after_ref.held, f32[8192,128]{1,0:T(8,128)S(1)} %get-tuple-element.36.turns_ref), custom_call_target="tpu_custom_call" | custom-call | flops 8999999488 | bytes 27000000 | tf_op jit(solution)/shard_map/correlate/pallas_call | solution.py:496
  45.8 0.6 collective-permute-start.7
  46.4 2.4 %collective-permute-start.8 = (s16[512,128]{1,0:T(8,128)(2,1)S(1)}, s16[512,128]{1,0:T(8,128)(2,1)S(1)}, u32[]{:S(2)}, u32[]{:S(2)}) collective-permute-start(s16[512,128]{1,0:T(8,128)(2,1)S(1)} %get-tuple-element.39), channel_id=1, source_target_pairs={{0,18},{2,16},{4,22},{6,20},{8,26},{10,24},{12,30},{14,28},{16,2},... | collective-permute-start | bytes 393224 | tf_op jit(solution)/shard_map/ppermute | solution.py:454
  48.8 0.5 collective-permute-start.9
  49.4 4.7 %collective-permute-done.7.refs_0_ = s16[512,128]{1,0:T(8,128)(2,1)S(1)} collective-permute-done((s16[512,128]{1,0:T(8,128)(2,1)S(1)}, s16[512,128]{1,0:T(8,128)(2,1)S(1)}, u32[]{:S(2)}, u32[]{:S(2)}) %collective-permute-start.7) | collective-permute-done | bytes 131104 | tf_op jit(solution)/shard_map/ppermute | solution.py:454
  54.1 1.2 %collective-permute-done.9.refs_2_ = s16[512,128]{1,0:T(8,128)(2,1)S(1)} collective-permute-done((s16[512,128]{1,0:T(8,128)(2,1)S(1)}, s16[512,128]{1,0:T(8,128)(2,1)S(1)}, u32[]{:S(2)}, u32[]{:S(2)}) %collective-permute-start.9) | collective-permute-done | bytes 131104 | tf_op jit(solution)/shard_map/ppermute | solution.py:454
  55.6 1.2 %collective-permute-start.10 = (s16[128,128]{1,0:T(8,128)(2,1)S(1)}, s16[128,128]{1,0:T(8,128)(2,1)S(1)}, u32[]{:S(2)}, u32[]{:S(2)}) collective-permute-start(s16[128,128]{1,0:T(8,128)(2,1)S(1)} %get-tuple-element.42), channel_id=1, source_target_pairs={{0,4},{2,6},{4,0},{6,2},{8,12},{10,14},{12,8},{14,10},{1,5},{3,7},... | collective-permute-start | bytes 98312 | tf_op jit(solution)/shard_map/ppermute | solution.py:390
  56.8 2.2 %collective-permute-start.11 = (s16[128,128]{1,0:T(8,128)(2,1)S(1)}, s16[128,128]{1,0:T(8,128)(2,1)S(1)}, u32[]{:S(2)}, u32[]{:S(2)}) collective-permute-start(s16[128,128]{1,0:T(8,128)(2,1)S(1)} %get-tuple-element.43), channel_id=1, source_target_pairs={{0,8},{2,10},{4,12},{6,14},{8,0},{10,2},{12,4},{14,6},{1,9},{3,11}... | collective-permute-start | bytes 98312 | tf_op jit(solution)/shard_map/ppermute | solution.py:390
  58.9 1.1 %collective-permute-start.12 = (s16[128,128]{1,0:T(8,128)(2,1)S(1)}, s16[128,128]{1,0:T(8,128)(2,1)S(1)}, u32[]{:S(2)}, u32[]{:S(2)}) collective-permute-start(s16[128,128]{1,0:T(8,128)(2,1)S(1)} %get-tuple-element.44), channel_id=1, source_target_pairs={{0,12},{2,14},{4,8},{6,10},{8,4},{10,6},{12,0},{14,2},{1,13},{3,15... | collective-permute-start | bytes 98312 | tf_op jit(solution)/shard_map/ppermute | solution.py:390
  60.0 1.6 %collective-permute-done.11.refs_1_ = s16[128,128]{1,0:T(8,128)(2,1)S(1)} collective-permute-done((s16[128,128]{1,0:T(8,128)(2,1)S(1)}, s16[128,128]{1,0:T(8,128)(2,1)S(1)}, u32[]{:S(2)}, u32[]{:S(2)}) %collective-permute-start.11) | collective-permute-done | bytes 32800 | tf_op jit(solution)/shard_map/ppermute | solution.py:390
  61.6 3.1 %collective-permute-done.12.refs_2_ = s16[128,128]{1,0:T(8,128)(2,1)S(1)} collective-permute-done((s16[128,128]{1,0:T(8,128)(2,1)S(1)}, s16[128,128]{1,0:T(8,128)(2,1)S(1)}, u32[]{:S(2)}, u32[]{:S(2)}) %collective-permute-start.12) | collective-permute-done | bytes 32800 | tf_op jit(solution)/shard_map/ppermute | solution.py:390
  64.6 1.9 %finish.1 = f32[4,2,4,435]{3,2,1,0:T(4,128)} custom-call(s32[2,435]{1,0:T(2,128)S(1)} %bitcast.5, f32[128,128]{1,0:T(8,128)S(1)} %get-tuple-element.41.own_ref, s16[128,128]{1,0:T(8,128)(2,1)S(1)} %collective-permute-done.10.refs_0_, s16[128,128]{1,0:T(8,128)(2,1)S(1)} %collective-permute-done.11.refs_1_, s16[128,128]{1,0:T(8,128)(2,1)S(1)} %collective-permute-done.12.refs_2_), custom_call_target="tpu_custom_call" | custom-call | flops 2000000000 | bytes 6000000 | tf_op jit(solution)/shard_map/finish/pallas_call | solution.py:541
  (22 shorter events, 1.3 us)
Async XLA Ops:
  0.0 15.2 %collective-permute-start = (bf16[2,2,30,2,8192]{4,3,2,1,0:T(2,128)(2,1)}, bf16[2,2,30,2,8192]{4,3,2,1,0:T(2,128)(2,1)}, u32[]{:S(2)}, u32[]{:S(2)}) collective-permute-start(bf16[2,2,30,2,8192]{4,3,2,1,0:T(2,128)(2,1)} %volts_ref.1), channel_id=1, source_target_pairs={{0,1},{1,0},{2,3},{3,2},{4,5},{5,4},{6,7},{7,6},{8,9},{9,8},{10,11... | collective-permute-start | bytes 11796488 | tf_op jit(solution)/shard_map/ppermute | solution.py:393
  2.2 10.3 %collective-permute-start.3 = (s16[272,128]{1,0:T(8,128)(2,1)}, s16[272,128]{1,0:T(8,128)(2,1)S(1)}, u32[]{:S(2)}, u32[]{:S(2)}) collective-permute-start(s16[272,128]{1,0:T(8,128)(2,1)} %pack.1.refs_0_), channel_id=1, source_target_pairs={{0,12},{2,14},{4,8},{6,10},{8,4},{10,6},{12,0},{14,2},{1,13},{3,15... | collective-permute-start | bytes 208904 | tf_op jit(solution)/shard_map/ppermute | solution.py:390
  6.9 6.7 %collective-permute-start.2 = (s16[272,128]{1,0:T(8,128)(2,1)}, s16[272,128]{1,0:T(8,128)(2,1)S(1)}, u32[]{:S(2)}, u32[]{:S(2)}) collective-permute-start(s16[272,128]{1,0:T(8,128)(2,1)} %pack.1.refs_0_), channel_id=1, source_target_pairs={{0,8},{2,10},{4,12},{6,14},{8,0},{10,2},{12,4},{14,6},{1,9},{3,11}... | collective-permute-start | bytes 208904 | tf_op jit(solution)/shard_map/ppermute | solution.py:390
  6.9 6.7 %collective-permute-start.1 = (s16[272,128]{1,0:T(8,128)(2,1)}, s16[272,128]{1,0:T(8,128)(2,1)S(1)}, u32[]{:S(2)}, u32[]{:S(2)}) collective-permute-start(s16[272,128]{1,0:T(8,128)(2,1)} %pack.1.refs_0_), channel_id=1, source_target_pairs={{0,4},{2,6},{4,0},{6,2},{8,12},{10,14},{12,8},{14,10},{1,5},{3,7},... | collective-permute-start | bytes 208904 | tf_op jit(solution)/shard_map/ppermute | solution.py:390
  8.1 5.5 %copy-start = (s16[272,128]{1,0:T(8,128)(2,1)S(1)}, s16[272,128]{1,0:T(8,128)(2,1)}, u32[]{:S(2)}) copy-start(s16[272,128]{1,0:T(8,128)(2,1)} %pack.1.refs_0_) | copy-start | bytes 208900
  13.6 6.0 %copy-start.1 = (s32[3]{0:T(128)S(1)}, s32[3]{0:T(128)}, u32[]{:S(2)}) copy-start(s32[3]{0:T(128)} %pad_add_fusion.rest_0_.place_ref) | copy-start | bytes 40
  13.6 6.0 %copy-start.2 = (s32[1,2,30]{2,1,0:T(2,128)S(1)}, s32[1,2,30]{2,1,0:T(2,128)}, u32[]{:S(2)}) copy-start(s32[1,2,30]{2,1,0:T(2,128)} %entry_ref.5) | copy-start | bytes 724
  13.6 8.9 %collective-permute-start.5 = (s16[1088,128]{1,0:T(8,128)(2,1)S(1)}, s16[1088,128]{1,0:T(8,128)(2,1)S(1)}, u32[]{:S(2)}, u32[]{:S(2)}) collective-permute-start(s16[1088,128]{1,0:T(8,128)(2,1)S(1)} %stack.17.rest_0_), channel_id=1, source_target_pairs={{0,2},{2,0},{4,6},{6,4},{8,10},{10,8},{12,14},{14,12},{1,3},{3,1},... | collective-permute-start | bytes 835592 | tf_op jit(solution)/shard_map/ppermute | solution.py:390
  15.2 4.4 %collective-permute-start.4 = (s16[1088,128]{1,0:T(8,128)(2,1)S(1)}, s16[1088,128]{1,0:T(8,128)(2,1)S(1)}, u32[]{:S(2)}, u32[]{:S(2)}) collective-permute-start(s16[1088,128]{1,0:T(8,128)(2,1)S(1)} %stack.17.rest_0_), channel_id=1, source_target_pairs={{0,1},{1,0},{2,3},{3,2},{4,5},{5,4},{6,7},{7,6},{8,9},{9,8},{10,11... | collective-permute-start | bytes 835592 | tf_op jit(solution)/shard_map/ppermute | solution.py:393
  22.6 2.4 %collective-permute-start.6 = (s16[1088,128]{1,0:T(8,128)(2,1)S(1)}, s16[1088,128]{1,0:T(8,128)(2,1)S(1)}, u32[]{:S(2)}, u32[]{:S(2)}) collective-permute-start(s16[1088,128]{1,0:T(8,128)(2,1)S(1)} %collective-permute-done.5.rest_0_), channel_id=1, source_target_pairs={{0,1},{1,0},{2,3},{3,2},{4,5},{5,4},{6,7},{7,6},{8,9},{9,8},{10,11... | collective-permute-start | bytes 835592 | tf_op jit(solution)/shard_map/ppermute | solution.py:393
  36.3 28.3 %copy-start.3 = (s32[435,2]{0,1:T(2,128)S(1)}, s32[435,2]{0,1:T(2,128)}, u32[]{:S(2)}) copy-start(s32[435,2]{0,1:T(2,128)} %param.8) | copy-start | bytes 10444
  45.8 8.3 %collective-permute-start.7 = (s16[512,128]{1,0:T(8,128)(2,1)S(1)}, s16[512,128]{1,0:T(8,128)(2,1)S(1)}, u32[]{:S(2)}, u32[]{:S(2)}) collective-permute-start(s16[512,128]{1,0:T(8,128)(2,1)S(1)} %get-tuple-element.38), channel_id=1, source_target_pairs={{0,2},{2,0},{4,6},{6,4},{8,10},{10,8},{12,14},{14,12},{16,18},{18,... | collective-permute-start | bytes 393224 | tf_op jit(solution)/shard_map/ppermute | solution.py:454
  46.4 7.7 %collective-permute-start.8 = (s16[512,128]{1,0:T(8,128)(2,1)S(1)}, s16[512,128]{1,0:T(8,128)(2,1)S(1)}, u32[]{:S(2)}, u32[]{:S(2)}) collective-permute-start(s16[512,128]{1,0:T(8,128)(2,1)S(1)} %get-tuple-element.39), channel_id=1, source_target_pairs={{0,18},{2,16},{4,22},{6,20},{8,26},{10,24},{12,30},{14,28},{16,2},... | collective-permute-start | bytes 393224 | tf_op jit(solution)/shard_map/ppermute | solution.py:454
  48.8 6.5 %collective-permute-start.9 = (s16[512,128]{1,0:T(8,128)(2,1)S(1)}, s16[512,128]{1,0:T(8,128)(2,1)S(1)}, u32[]{:S(2)}, u32[]{:S(2)}) collective-permute-start(s16[512,128]{1,0:T(8,128)(2,1)S(1)} %get-tuple-element.40), channel_id=1, source_target_pairs={{0,16},{2,18},{4,20},{6,22},{8,24},{10,26},{12,28},{14,30},{16,0},... | collective-permute-start | bytes 393224 | tf_op jit(solution)/shard_map/ppermute | solution.py:454
  55.6 4.5 %collective-permute-start.10 = (s16[128,128]{1,0:T(8,128)(2,1)S(1)}, s16[128,128]{1,0:T(8,128)(2,1)S(1)}, u32[]{:S(2)}, u32[]{:S(2)}) collective-permute-start(s16[128,128]{1,0:T(8,128)(2,1)S(1)} %get-tuple-element.42), channel_id=1, source_target_pairs={{0,4},{2,6},{4,0},{6,2},{8,12},{10,14},{12,8},{14,10},{1,5},{3,7},... | collective-permute-start | bytes 98312 | tf_op jit(solution)/shard_map/ppermute | solution.py:390
  56.8 4.8 %collective-permute-start.11 = (s16[128,128]{1,0:T(8,128)(2,1)S(1)}, s16[128,128]{1,0:T(8,128)(2,1)S(1)}, u32[]{:S(2)}, u32[]{:S(2)}) collective-permute-start(s16[128,128]{1,0:T(8,128)(2,1)S(1)} %get-tuple-element.43), channel_id=1, source_target_pairs={{0,8},{2,10},{4,12},{6,14},{8,0},{10,2},{12,4},{14,6},{1,9},{3,11}... | collective-permute-start | bytes 98312 | tf_op jit(solution)/shard_map/ppermute | solution.py:390
  58.9 5.7 %collective-permute-start.12 = (s16[128,128]{1,0:T(8,128)(2,1)S(1)}, s16[128,128]{1,0:T(8,128)(2,1)S(1)}, u32[]{:S(2)}, u32[]{:S(2)}) collective-permute-start(s16[128,128]{1,0:T(8,128)(2,1)S(1)} %get-tuple-element.44), channel_id=1, source_target_pairs={{0,12},{2,14},{4,8},{6,10},{8,4},{10,6},{12,0},{14,2},{1,13},{3,15... | collective-permute-start | bytes 98312 | tf_op jit(solution)/shard_map/ppermute | solution.py:390

commit v3 on v2

--- a/solution.py
+++ b/solution.py
@@ -12,7 +12,8 @@
 Q = 64
 LANES = 128
 HALF = 64
-WIDTH = 256
+WIDTH = 1024
+ROW = 8
 GROUP = 2
 TURN = 65536.0
 COSINE = (-0.9999992251396179, 19.738981246948242, -64.92865753173828, 85.27162170410156, -58.79049301147461, 21.07110595703125)
@@ -77,12 +78,12 @@
     return code * scale
 
 
-def rows_kernel(volts_ref, *rest, first, depth):
+def rows_kernel(volts_ref, *rest, first, pitch):
     held, raw, sems = rest[-3:]
     parts, spectra, stations = volts_ref.shape[:3]
     width = raw.shape[-1]
     steps = raw.shape[0]
-    unroll = 4
+    unroll = 2
 
     def fetch(step):
         return pltpu.make_async_copy(
@@ -116,23 +117,23 @@
                         ],
                         axis=0,
                     )
-                    at = (step * width + k * LANES) * depth + first + t
-                    held[pl.ds(at, LANES, stride=depth), :] = both.astype(jnp.float32).T
+                    at = (step * width + k * LANES) * pitch + first + t
+                    held[pl.ds(at, LANES, stride=pitch), :] = both.astype(jnp.float32).T
         return 0
 
     lax.fori_loop(0, steps // unroll, flip, 0)
 
 
 def prepare_kernel(
-    place_ref, entry_ref, after_ref, *rest, columns, started, group, near, far, per, fine
+    place_ref, entry_ref, after_ref, held_in, *rest, columns, started, group, near, far, per, fine, pitch
 ):
-    del after_ref
+    del after_ref, held_in
     stacks = rest[: len(columns)]
     rest = rest[len(columns) :]
     if started:
-        carry_in, found_in, _ = rest[:3]
-        rest = rest[3:]
-    carry_ref, found_ref, turns_ref, source_ref = rest
+        carry_in, found_in = rest[:2]
+        rest = rest[2:]
+    held, carry_ref, found_ref, source_ref = rest
     chip = place_ref[0]
     core = place_ref[1]
     x = place_ref[2]
@@ -179,8 +180,8 @@
     turns = jnp.dot(digits, spread, preferred_element_type=jnp.float32)
     for index, (_, _, owner) in enumerate(blocks):
         for half in range(2):
-            at = pl.multiple_of((owner * 2 + half) * (fine // 2), fine // 2)
-            turns_ref[pl.ds(at, fine // 2), :] = turns[
+            at = (owner * 2 + half) * (fine // 2) * pitch + pitch - 1
+            held[pl.ds(at, fine // 2, stride=pitch), :] = turns[
                 index * (fine // 2) : (index + 1) * (fine // 2), half * LANES : (half + 1) * LANES
             ]
 
@@ -221,7 +222,7 @@
     )
     carry_ref[...] = jnp.broadcast_to(carry, carry_ref.shape)
     found_ref[...] = found
-    source_ref[...] = (found[:q_here] * LANES + found[q_here:]).astype(jnp.int32)
+    source_ref[...] = ((found[:q_here] * LANES + found[q_here:]) * pitch).astype(jnp.int32)
 
 
 def wave(z):
@@ -231,25 +232,23 @@
     return value
 
 
-def correlate_kernel(source_ref, held, turns_ref, *rest, first_pair, pairs, spectra):
-    outs = rest[:GROUP]
-    even, odd, even_turns, odd_turns, wide_even, wide_odd, kept = rest[GROUP:]
-    depth = 2 * spectra
-
-    def gather(unit, into, into_turns):
+def correlate_kernel(source_ref, held, *rest, first_pair, pairs, spectra, sent):
+    outs = rest[: 1 if sent else GROUP]
+    rest = rest[len(outs) :]
+    even, odd, wide_even, wide_odd, kept = rest
+
+    def gather(unit, into):
         for first in range(0, LANES, 32):
             at = [source_ref[unit, first + k] for k in range(32)]
-            rows = [held[pl.ds(pl.multiple_of(a * depth, depth), depth), :] for a in at]
-            turns = [turns_ref[pl.ds(a, 1), :] for a in at]
+            rows = [held[pl.ds(a, ROW), :] for a in at]
             for k in range(32):
-                into[(first + k) * depth : (first + k + 1) * depth, :] = rows[k]
-                into_turns[first + k : first + k + 1, :] = turns[k]
+                into[(first + k) * ROW : (first + k + 1) * ROW, :] = rows[k]
 
     upper = (iota((HALF, LANES), 1) & (HALF - 1)) > iota((HALF, LANES), 0)
     left = iota((HALF, LANES), 1) < HALF
 
-    def rotate(rows, turns, wide):
-        turns = turns[...].T
+    def rotate(rows, wide):
+        turns = rows[pl.ds(2 * spectra, LANES, stride=ROW), :].T
         turning = []
         for centre in range(GROUP):
             angle = turns[centre * HALF : (centre + 1) * HALF]
@@ -257,7 +256,7 @@
             sine = jnp.abs(angle - 0.25) - 0.5
             turning.append((wave(cosine * cosine), wave(sine * sine)))
         for t in range(2 * spectra):
-            volts = rows[pl.ds(t, LANES, stride=depth), :].T
+            volts = rows[pl.ds(t, LANES, stride=ROW), :].T
             real, imaginary = volts[:HALF], volts[HALF:]
             columns = slice(t * LANES, (t + 1) * LANES)
             for centre in range(GROUP):
@@ -289,30 +288,42 @@
             first = jnp.where(upper, first, pltpu.roll(first, HALF, 1))
             second = jnp.where(upper, pltpu.roll(second, HALF, 1), second)
             value = jnp.where(left, first, second)
-            out_ref = outs[centre]
-            if out_ref.dtype == jnp.int16:
+            at = pl.ds(pl.multiple_of(pair * HALF, HALF), HALF)
+            if outs[0].dtype == jnp.int16:
                 value = encode(value)
-            out_ref[pl.ds(pl.multiple_of(pair * HALF, HALF), HALF), :] = value
+                outs[0][centre, at, :] = value
+            else:
+                outs[centre][at, :] = value
 
     base = 2 * first_pair
     last = base + 2 * pairs - 1
-    gather(base, even, even_turns)
+    gather(base, even)
     wide_odd[...] = jnp.zeros_like(wide_odd)
     kept[...] = jnp.zeros_like(kept)
 
     def one(pair, _):
         unit = base + 2 * pair
-        gather(unit + 1, odd, odd_turns)
-        rotate(even, even_turns, wide_even)
+        gather(unit + 1, odd)
+        rotate(even, wide_even)
         emit(jnp.maximum(pair - 1, 0), correlate(wide_odd))
-        gather(jnp.minimum(unit + 2, last), even, even_turns)
-        rotate(odd, odd_turns, wide_odd)
+        gather(jnp.minimum(unit + 2, last), even)
+        rotate(odd, wide_odd)
         for centre, value in enumerate(correlate(wide_even)):
             kept[centre] = value
         return 0
 
     lax.fori_loop(0, pairs, one, 0)
     emit(pairs - 1, correlate(wide_odd))
+
+
+def join_kernel(*refs, arrivals):
+    owns, arrived, outs = refs[:GROUP], refs[GROUP : GROUP + arrivals], refs[GROUP + arrivals :]
+    for at in range(0, owns[0].shape[0], HALF):
+        for c in range(GROUP):
+            value = owns[c][at : at + HALF, :]
+            for ref in arrived:
+                value = value + decode(ref[c, at : at + HALF, :])
+            outs[c][at : at + HALF, :] = encode(value) if outs[c].dtype == jnp.int16 else value
 
 
 def merge_kernel(own_ref, *refs, arrivals, far, pairs):
@@ -348,14 +359,13 @@
         flipped = total.T
         coarse = flipped.astype(jnp.bfloat16)
         medium = (flipped - coarse.astype(jnp.float32)).astype(jnp.bfloat16)
-        fine = (flipped - coarse.astype(jnp.float32) - medium.astype(jnp.float32)).astype(jnp.bfloat16)
-        stack = jnp.concatenate([coarse, medium, fine], axis=0)
+        stack = jnp.concatenate([coarse, medium], axis=0)
         picked = {}
         for side, members in enumerate((first, second)):
             for p in range(2):
                 choose = (station == 2 * members + p).astype(jnp.bfloat16)
                 rows = jnp.dot(stack, choose, preferred_element_type=jnp.float32)
-                rows = rows[:LANES] + rows[LANES : 2 * LANES] + rows[2 * LANES :]
+                rows = rows[:LANES] + rows[LANES:]
                 partner = second if side == 0 else first
                 for half in range(2):
                     for p2 in range(2):
@@ -413,11 +423,12 @@
     )(turning, target.reshape(fine // LANES, LANES))
     line = [block] + [across_chips(block, z * near) for z in range(1, far)]
 
-    held_type = pltpu.VMEM((channels * 2 * spectra, LANES), jnp.float32)
+    pitch = 2 * spectra + 1
+    held_type = pltpu.VMEM((channels * pitch + ROW, LANES), jnp.float32)
 
     def rows(side, *operands):
         return pl.pallas_call(
-            functools.partial(rows_kernel, first=side * spectra, depth=2 * spectra),
+            functools.partial(rows_kernel, first=side * spectra, pitch=pitch),
             in_specs=[HBM, ANY, VMEM][: 2 + side],
             out_specs=VMEM,
             out_shape=held_type,
@@ -426,7 +437,7 @@
                 pltpu.SemaphoreType.DMA((channels // WIDTH,)),
             ],
             input_output_aliases={2: 0} if side else {},
-            compiler_params=params(44),
+            compiler_params=params(40),
             cost_estimate=cost(5),
             name="rows",
         )(*operands)
@@ -447,12 +458,7 @@
     held = rows(1, other, place, held)
     each = far * pairs
     arrived = []
-    flat = [(a, b) for a in range(tm) for b in range(chips)]
-
-    def exchange(value, c, y):
-        route = [(a * chips + b, (a ^ c) * chips + (b ^ y)) for a, b in flat]
-        return lax.ppermute(value, ("tm", "chip"), route)
-
+    after = place
     for group in range(centres // GROUP):
         state = ()
         for part in range(3 if near > 1 else 1):
@@ -464,7 +470,7 @@
                 state, mine = lax.optimization_barrier((state, mine))
                 theirs += [across_cores(value) for value in mine[1:]]
             stacks = [(theirs if across else mine)[y] for y, across in columns]
-            *state, source = pl.pallas_call(
+            held, *state, source = pl.pallas_call(
                 functools.partial(
                     prepare_kernel,
                     columns=columns,
@@ -474,56 +480,72 @@
                     far=far,
                     per=per_device,
                     fine=fine,
+                    pitch=pitch,
                 ),
-                in_specs=[SMEM, VMEM, ANY] + [VMEM] * (len(stacks) + len(state)),
+                in_specs=[SMEM, VMEM, ANY] + [VMEM] * (1 + len(stacks) + len(state)),
                 out_specs=[VMEM] * 4,
                 out_shape=[
+                    held_type,
                     jax.ShapeDtypeStruct((Q // 2, LANES), jnp.float32),
                     jax.ShapeDtypeStruct((Q, LANES), jnp.float32),
-                    pltpu.VMEM((channels, LANES), jnp.float32),
                     jax.ShapeDtypeStruct((Q // 2, LANES), jnp.int32),
                 ],
-                input_output_aliases={3 + len(stacks) + 2: 2} if part else {},
+                input_output_aliases={3: 0},
                 compiler_params=params(16),
                 cost_estimate=cost(2),
                 name="prepare",
-            )(place, entry, held, *stacks, *state)
-        turns = state[2]
-        for y, count in ((1, near - 1), (0, 1)):
-            if not count:
-                continue
-            kinds = [jnp.float32 if group + c + y == 0 else jnp.int16 for c in range(GROUP)]
-            results = pl.pallas_call(
+            )(place, entry, after, held, *stacks, *state)
+        def correlate(first_pair, out_types, source=source, held=held):
+            return pl.pallas_call(
                 functools.partial(
-                    correlate_kernel, first_pair=y * each, pairs=count * each, spectra=spectra
+                    correlate_kernel,
+                    first_pair=first_pair,
+                    pairs=each,
+                    spectra=spectra,
+                    sent=len(out_types) == 1,
                 ),
-                in_specs=[SMEM, VMEM, VMEM],
-                out_specs=[VMEM] * GROUP,
-                out_shape=[
-                    jax.ShapeDtypeStruct((count * each * HALF, LANES), kind) for kind in kinds
-                ],
+                in_specs=[SMEM, VMEM],
+                out_specs=[VMEM] * len(out_types),
+                out_shape=out_types,
                 scratch_shapes=[
-                    pltpu.VMEM((LANES * 2 * spectra, LANES), jnp.float32),
-                    pltpu.VMEM((LANES * 2 * spectra, LANES), jnp.float32),
-                    pltpu.VMEM((LANES, LANES), jnp.float32),
-                    pltpu.VMEM((LANES, LANES), jnp.float32),
+                    pltpu.VMEM((LANES * ROW, LANES), jnp.float32),
+                    pltpu.VMEM((LANES * ROW, LANES), jnp.float32),
                     pltpu.VMEM((GROUP, 2 * LANES, 2 * spectra * LANES), jnp.bfloat16),
                     pltpu.VMEM((GROUP, 2 * LANES, 2 * spectra * LANES), jnp.bfloat16),
                     pltpu.VMEM((GROUP, HALF, LANES), jnp.float32),
                 ],
                 compiler_params=params(12),
-                cost_estimate=cost(9 * count),
+                cost_estimate=cost(9),
                 name="correlate",
-            )(source, held, turns)
-            for c in range(GROUP):
-                for k in range(count):
-                    value = results[c]
-                    if count > 1:
-                        value = value[k * each * HALF : (k + 1) * each * HALF]
-                    if group + c + y == 0:
-                        total = value
-                    else:
-                        arrived.append(exchange(value, group * GROUP + c, y + k))
+            )(source, held)
+
+        columns_in = []
+        for y in range(1, near):
+            sent = correlate(
+                y * each, [jax.ShapeDtypeStruct((GROUP, each * HALF, LANES), jnp.int16)]
+            )[0]
+            columns_in.append(across_chips(sent, y))
+        own = correlate(0, [jax.ShapeDtypeStruct((each * HALF, LANES), jnp.float32)] * GROUP)
+        after = own[0]
+        if columns_in:
+            kinds = [jnp.int16 if group + c else jnp.float32 for c in range(GROUP)]
+            own = pl.pallas_call(
+                functools.partial(join_kernel, arrivals=len(columns_in)),
+                in_specs=[VMEM] * (GROUP + len(columns_in)),
+                out_specs=[VMEM] * GROUP,
+                out_shape=[jax.ShapeDtypeStruct((each * HALF, LANES), kind) for kind in kinds],
+                compiler_params=params(8),
+                cost_estimate=cost(1),
+                name="join",
+            )(*own, *columns_in)
+        for c in range(GROUP):
+            centre = group * GROUP + c
+            if centre == 0:
+                total = own[c]
+            else:
+                arrived.append(
+                    lax.ppermute(own[c], "tm", [(i, i ^ centre) for i in range(tm)])
+                )
     rows = pairs * HALF
     merged = pl.pallas_call(
         functools.partial(merge_kernel, arrivals=len(arrived), far=far, pairs=pairs),

time: 66.7 us -> 60.2 us (0.903)
  Pallas kernels: 38.3 us -> 34.1 us
  waiting for transfers between devices: 11.6 us -> 10.2 us
  starting transfers between devices: 15.9 us -> 14.9 us
    pallas_call x4 -> x5, Pallas kernels: 27.7 us -> 23.8 us  [the longest x2 16.1 us: correlate(): pl.pallas_call(functools.partial(correlate_kernel, first_pair=first_pair,...]
    ppermute x3 -> x1, starting transfers between devices: 3.55 us -> 1.55 us  [on_device(): lax.ppermute(own[c], 'tm', [(i, i ^ centre) for i in range(tm)])]
    ppermute x3 -> x1, waiting for transfers between devices: 5.93 us -> 4.15 us  [on_device(): lax.ppermute(own[c], 'tm', [(i, i ^ centre) for i in range(tm)])]
    ppermute x7 -> x8, starting transfers between devices: 11.3 us -> 12.5 us  [across_chips(): return lax.ppermute(x, 'chip', [(i, i ^ step) for i in range(chips)])]
    ppermute x7 -> x8, waiting for transfers between devices: 5.69 us -> 6.05 us  [across_chips(): return lax.ppermute(x, 'chip', [(i, i ^ step) for i in range(chips)])]
  transfers between devices with their start and end apart: 13 -> 12, of which waited for: 5 -> 4; matrix products, arithmetic and copies ran while one was open for 1% -> 1% of each run, Pallas kernels for 23% -> 36%
where the time goes in v3:
time: 60.2 us; the launch traced here: 60.1 us
  Pallas kernels  34.1 us (57%)
  starting transfers between devices  14.9 us (25%)
  waiting for transfers between devices  10.2 us (17%)
  other arithmetic  0.65 us (1%)
    pallas_call x2, Pallas kernels, correlate(): pl.pallas_call(functools.partial(correlate_kernel, first_pair=first_pair,...  16.1 us
    ppermute x8, starting transfers between devices, across_chips(): return lax.ppermute(x, 'chip', [(i, i ^ step) for i in range(chips)])  12.5 us
    pallas_call x2, Pallas kernels, rows(): pl.pallas_call(functools.partial(rows_kernel, first=side * spectra, pitch...  7.47 us
    pallas_call x3, Pallas kernels, on_device(): pl.pallas_call(functools.partial(prepare_kernel, columns=columns, started...  6.7 us
    ppermute x8, waiting for transfers between devices, across_chips(): return lax.ppermute(x, 'chip', [(i, i ^ step) for i in range(chips)])  6.05 us
    ppermute x1, waiting for transfers between devices, on_device(): lax.ppermute(own[c], 'tm', [(i, i ^ centre) for i in range(tm)])  4.15 us
    pallas_call x1, Pallas kernels, on_device(): pl.pallas_call(pack_kernel, in_specs=[HBM, HBM], out_specs=VMEM, out_shap...  1.76 us
    pallas_call x1, Pallas kernels, on_device(): pl.pallas_call(functools.partial(finish_kernel, arrivals=len(final), pair...  1.62 us
  transfers between devices with their start and end apart: 12, of which 4 were waited for; matrix products, arithmetic and copies ran while one was open for 1% of the time, Pallas kernels for 36%

profile of v3, /device:TPU:0, one launch (start us, length us, event | category | flops | bytes accessed | tf_op | source)
XLA Modules:
  0.0 60.1 jit_solution(5024974017611484991)
XLA Ops:
  0.0 0.5 collective-permute-start
  0.5 1.8 %pack.1.refs_0_ = s16[272,128]{1,0:T(8,128)(2,1)} custom-call(f32[64,512]{1,0:T(8,128)} %turning_hbm.1, s32[4,128]{1,0:T(4,128)} %bitcast.6), custom_call_target="tpu_custom_call" | custom-call | flops 1000000000 | bytes 3000000 | tf_op jit(solution)/shard_map/pack/pallas_call | solution.py:410
  2.2 4.7 %collective-permute-start.3 = (s16[272,128]{1,0:T(8,128)(2,1)}, s16[272,128]{1,0:T(8,128)(2,1)S(1)}, u32[]{:S(2)}, u32[]{:S(2)}) collective-permute-start(s16[272,128]{1,0:T(8,128)(2,1)} %pack.1.refs_0_), channel_id=1, source_target_pairs={{0,12},{2,14},{4,8},{6,10},{8,4},{10,6},{12,0},{14,2},{1,13},{3,15... | collective-permute-start | bytes 208904 | tf_op jit(solution)/shard_map/ppermute | solution.py:400
  6.9 0.6 %collective-permute-start.1 = (s16[272,128]{1,0:T(8,128)(2,1)}, s16[272,128]{1,0:T(8,128)(2,1)S(1)}, u32[]{:S(2)}, u32[]{:S(2)}) collective-permute-start(s16[272,128]{1,0:T(8,128)(2,1)} %pack.1.refs_0_), channel_id=1, source_target_pairs={{0,4},{2,6},{4,0},{6,2},{8,12},{10,14},{12,8},{14,10},{1,5},{3,7},... | collective-permute-start | bytes 208904 | tf_op jit(solution)/shard_map/ppermute | solution.py:400
  7.5 0.7 %pad_add_fusion.rest_0_.place_ref.after_ref = s32[3]{0:T(128)} fusion(s32[1]{0:T(128)} %bitcast.3, s32[1]{0:T(128)} %bitcast.2, s32[1]{0:T(128)} %bitcast.1), kind=kLoop, calls=%fused_computation | loop fusion | flops 6 | bytes 24 | tf_op jit(solution)/shard_map/stack | solution.py:408
  8.2 3.7 %rows.2.rest_1_.after_ref = f32[40968,128]{1,0:T(8,128)S(1)} custom-call(bf16[2,2,30,2,8192]{4,3,2,1,0:T(2,128)(2,1)} %volts_ref.1, s32[3]{0:T(128)} %pad_add_fusion.rest_0_.place_ref.after_ref), custom_call_target="tpu_custom_call" | custom-call | flops 5000000000 | bytes 15000000 | tf_op jit(solution)/shard_map/rows/pallas_call | solution.py:430
  11.9 1.6 %collective-permute-done.2.refs_2_ = s16[272,128]{1,0:T(8,128)(2,1)S(1)} collective-permute-done((s16[272,128]{1,0:T(8,128)(2,1)}, s16[272,128]{1,0:T(8,128)(2,1)S(1)}, u32[]{:S(2)}, u32[]{:S(2)}) %collective-permute-start.2) | collective-permute-done | bytes 69664 | tf_op jit(solution)/shard_map/ppermute | solution.py:400
  13.6 1.6 %collective-permute-start.5 = (s16[1088,128]{1,0:T(8,128)(2,1)S(1)}, s16[1088,128]{1,0:T(8,128)(2,1)S(1)}, u32[]{:S(2)}, u32[]{:S(2)}) collective-permute-start(s16[1088,128]{1,0:T(8,128)(2,1)S(1)} %stack.17.rest_0_), channel_id=1, source_target_pairs={{0,2},{2,0},{4,6},{6,4},{8,10},{10,8},{12,14},{14,12},{1,3},{3,1},... | collective-permute-start | bytes 835592 | tf_op jit(solution)/shard_map/ppermute | solution.py:400
  15.2 3.7 %rows.3.held_in = f32[40968,128]{1,0:T(8,128)S(1)} custom-call(bf16[2,2,30,2,8192]{4,3,2,1,0:T(2,128)(2,1)} %collective-permute-done.volts_ref, s32[3]{0:T(128)} %pad_add_fusion.rest_0_.place_ref.after_ref, f32[40968,128]{1,0:T(8,128)S(1)} %rows.2.rest_1_.after_ref), custom_call_target="tpu_custom_call", output_to_operand_aliasing={{}: (2, {})} | custom-call | flops 5000000000 | bytes 15000000 | tf_op jit(solution)/shard_map/rows/pallas_call | solution.py:430
  19.0 2.9 %prepare.3 = (f32[40968,128]{1,0:T(8,128)S(1)}, f32[32,128]{1,0:T(8,128)S(1)}, f32[64,128]{1,0:T(8,128)S(1)}, s32[32,128]{1,0:T(8,128)}) custom-call(s32[3]{0:T(128)S(1)} %copy-done.1, s32[1,2,30]{2,1,0:T(2,128)S(1)} %copy-done.2, s32[3]{0:T(128)S(1)} %copy-done.1, f32[40968,128]{1,0:T(8,128)S(1)} %rows.3.held_in, ...), custom_call_target="tpu_custom_call", output_to_operand_aliasing={{0}: (3, {})} | custom-call | flops 2000000000 | bytes 6000000 | tf_op jit(solution)/shard_map/prepare/pallas_call | solution.py:473
  22.0 0.5 collective-permute-start.6
  22.5 1.9 %prepare.4 = (f32[40968,128]{1,0:T(8,128)S(1)}, f32[32,128]{1,0:T(8,128)S(1)}, f32[64,128]{1,0:T(8,128)S(1)}, s32[32,128]{1,0:T(8,128)}) custom-call(s32[3]{0:T(128)S(1)} %copy-done.1, s32[1,2,30]{2,1,0:T(2,128)S(1)} %copy-done.2, s32[3]{0:T(128)S(1)} %copy-done.1, f32[40968,128]{1,0:T(8,128)S(1)} %get-tuple-element.24.held_in, ...), custom_call_target="tpu_custom_call", output_to_operand_aliasing={{0}: (3, {})} | custom-call | flops 2000000000 | bytes 6000000 | tf_op jit(solution)/shard_map/prepare/pallas_call | solution.py:473
  24.3 1.9 %prepare.5 = (f32[40968,128]{1,0:T(8,128)S(1)}, f32[32,128]{1,0:T(8,128)}, f32[64,128]{1,0:T(8,128)}, s32[32,128]{1,0:T(8,128)S(1)}) custom-call(s32[3]{0:T(128)S(1)} %copy-done.1, s32[1,2,30]{2,1,0:T(2,128)S(1)} %copy-done.2, s32[3]{0:T(128)S(1)} %copy-done.1, f32[40968,128]{1,0:T(8,128)S(1)} %get-tuple-element.30.held_in, ...), custom_call_target="tpu_custom_call", output_to_operand_aliasing={{0}: (3, {})} | custom-call | flops 2000000000 | bytes 6000000 | tf_op jit(solution)/shard_map/prepare/pallas_call | solution.py:473
  26.2 8.4 %correlate.3 = s16[2,512,128]{2,1,0:T(8,128)(2,1)S(1)} custom-call(s32[32,128]{1,0:T(8,128)S(1)} %get-tuple-element.33.source_ref, f32[40968,128]{1,0:T(8,128)S(1)} %get-tuple-element.34.held), custom_call_target="tpu_custom_call" | custom-call | flops 8999999488 | bytes 27000000 | tf_op jit(solution)/shard_map/correlate/pallas_call | solution.py:499
  34.7 1.1 %collective-permute-start.7 = (s16[2,512,128]{2,1,0:T(8,128)(2,1)S(1)}, s16[2,512,128]{2,1,0:T(8,128)(2,1)S(1)}, u32[]{:S(2)}, u32[]{:S(2)}) collective-permute-start(s16[2,512,128]{2,1,0:T(8,128)(2,1)S(1)} %correlate.3), channel_id=1, source_target_pairs={{0,2},{2,0},{4,6},{6,4},{8,10},{10,8},{12,14},{14,12},{1,3},{3,1},... | collective-permute-start | bytes 786440 | tf_op jit(solution)/shard_map/ppermute | solution.py:400
  35.8 7.7 %correlate.2 = (f32[512,128]{1,0:T(8,128)S(1)}, f32[512,128]{1,0:T(8,128)S(1)}) custom-call(s32[32,128]{1,0:T(8,128)S(1)} %get-tuple-element.33.source_ref, f32[40968,128]{1,0:T(8,128)S(1)} %get-tuple-element.34.held), custom_call_target="tpu_custom_call" | custom-call | flops 8999999488 | bytes 27000000 | tf_op jit(solution)/shard_map/correlate/pallas_call | solution.py:499
  43.8 1.6 %collective-permute-start.8 = (s16[512,128]{1,0:T(8,128)(2,1)S(1)}, s16[512,128]{1,0:T(8,128)(2,1)S(1)}, u32[]{:S(2)}, u32[]{:S(2)}) collective-permute-start(s16[512,128]{1,0:T(8,128)(2,1)S(1)} %get-tuple-element.38), channel_id=1, source_target_pairs={{0,16},{16,0},{1,17},{17,1},{2,18},{18,2},{3,19},{19,3},{4,20},{20... | collective-permute-start | bytes 393224 | tf_op jit(solution)/shard_map/ppermute | solution.py:547
  45.3 4.2 %collective-permute-done.8.refs_0_ = s16[512,128]{1,0:T(8,128)(2,1)S(1)} collective-permute-done((s16[512,128]{1,0:T(8,128)(2,1)S(1)}, s16[512,128]{1,0:T(8,128)(2,1)S(1)}, u32[]{:S(2)}, u32[]{:S(2)}) %collective-permute-start.8) | collective-permute-done | bytes 131104 | tf_op jit(solution)/shard_map/ppermute | solution.py:547
  49.7 1.2 %collective-permute-start.9 = (s16[128,128]{1,0:T(8,128)(2,1)S(1)}, s16[128,128]{1,0:T(8,128)(2,1)S(1)}, u32[]{:S(2)}, u32[]{:S(2)}) collective-permute-start(s16[128,128]{1,0:T(8,128)(2,1)S(1)} %get-tuple-element.40), channel_id=1, source_target_pairs={{0,4},{2,6},{4,0},{6,2},{8,12},{10,14},{12,8},{14,10},{1,5},{3,7},... | collective-permute-start | bytes 98312 | tf_op jit(solution)/shard_map/ppermute | solution.py:400
  50.8 1.9 %collective-permute-start.10 = (s16[128,128]{1,0:T(8,128)(2,1)S(1)}, s16[128,128]{1,0:T(8,128)(2,1)S(1)}, u32[]{:S(2)}, u32[]{:S(2)}) collective-permute-start(s16[128,128]{1,0:T(8,128)(2,1)S(1)} %get-tuple-element.41), channel_id=1, source_target_pairs={{0,8},{2,10},{4,12},{6,14},{8,0},{10,2},{12,4},{14,6},{1,9},{3,11}... | collective-permute-start | bytes 98312 | tf_op jit(solution)/shard_map/ppermute | solution.py:400
  52.8 1.4 %collective-permute-start.11 = (s16[128,128]{1,0:T(8,128)(2,1)S(1)}, s16[128,128]{1,0:T(8,128)(2,1)S(1)}, u32[]{:S(2)}, u32[]{:S(2)}) collective-permute-start(s16[128,128]{1,0:T(8,128)(2,1)S(1)} %get-tuple-element.42), channel_id=1, source_target_pairs={{0,12},{2,14},{4,8},{6,10},{8,4},{10,6},{12,0},{14,2},{1,13},{3,15... | collective-permute-start | bytes 98312 | tf_op jit(solution)/shard_map/ppermute | solution.py:400
  54.1 1.5 %collective-permute-done.10.refs_1_ = s16[128,128]{1,0:T(8,128)(2,1)S(1)} collective-permute-done((s16[128,128]{1,0:T(8,128)(2,1)S(1)}, s16[128,128]{1,0:T(8,128)(2,1)S(1)}, u32[]{:S(2)}, u32[]{:S(2)}) %collective-permute-start.10) | collective-permute-done | bytes 32800 | tf_op jit(solution)/shard_map/ppermute | solution.py:400
  55.6 2.8 %collective-permute-done.11.refs_2_ = s16[128,128]{1,0:T(8,128)(2,1)S(1)} collective-permute-done((s16[128,128]{1,0:T(8,128)(2,1)S(1)}, s16[128,128]{1,0:T(8,128)(2,1)S(1)}, u32[]{:S(2)}, u32[]{:S(2)}) %collective-permute-start.11) | collective-permute-done | bytes 32800 | tf_op jit(solution)/shard_map/ppermute | solution.py:400
  58.5 1.6 %finish.1 = f32[4,2,4,435]{3,2,1,0:T(4,128)} custom-call(s32[2,435]{1,0:T(2,128)S(1)} %bitcast.5, f32[128,128]{1,0:T(8,128)S(1)} %get-tuple-element.39.own_ref, s16[128,128]{1,0:T(8,128)(2,1)S(1)} %collective-permute-done.9.refs_0_, s16[128,128]{1,0:T(8,128)(2,1)S(1)} %collective-permute-done.10.refs_1_, s16[128,128]{1,0:T(8,128)(2,1)S(1)} %collective-permute-done.11.refs_2_), custom_call_target="tpu_custom_call" | custom-call | flops 2000000000 | bytes 6000000 | tf_op jit(solution)/shard_map/finish/pallas_call | solution.py:563
  (21 shorter events, 0.5 us)
Async XLA Ops:
  0.0 15.2 %collective-permute-start = (bf16[2,2,30,2,8192]{4,3,2,1,0:T(2,128)(2,1)}, bf16[2,2,30,2,8192]{4,3,2,1,0:T(2,128)(2,1)}, u32[]{:S(2)}, u32[]{:S(2)}) collective-permute-start(bf16[2,2,30,2,8192]{4,3,2,1,0:T(2,128)(2,1)} %volts_ref.1), channel_id=1, source_target_pairs={{0,1},{1,0},{2,3},{3,2},{4,5},{5,4},{6,7},{7,6},{8,9},{9,8},{10,11... | collective-permute-start | bytes 11796488 | tf_op jit(solution)/shard_map/ppermute | solution.py:403
  2.2 11.4 %copy-start = (s16[272,128]{1,0:T(8,128)(2,1)S(1)}, s16[272,128]{1,0:T(8,128)(2,1)}, u32[]{:S(2)}) copy-start(s16[272,128]{1,0:T(8,128)(2,1)} %pack.1.refs_0_) | copy-start | bytes 208900
  2.2 9.7 %collective-permute-start.3 = (s16[272,128]{1,0:T(8,128)(2,1)}, s16[272,128]{1,0:T(8,128)(2,1)S(1)}, u32[]{:S(2)}, u32[]{:S(2)}) collective-permute-start(s16[272,128]{1,0:T(8,128)(2,1)} %pack.1.refs_0_), channel_id=1, source_target_pairs={{0,12},{2,14},{4,8},{6,10},{8,4},{10,6},{12,0},{14,2},{1,13},{3,15... | collective-permute-start | bytes 208904 | tf_op jit(solution)/shard_map/ppermute | solution.py:400
  6.9 6.7 %collective-permute-start.2 = (s16[272,128]{1,0:T(8,128)(2,1)}, s16[272,128]{1,0:T(8,128)(2,1)S(1)}, u32[]{:S(2)}, u32[]{:S(2)}) collective-permute-start(s16[272,128]{1,0:T(8,128)(2,1)} %pack.1.refs_0_), channel_id=1, source_target_pairs={{0,8},{2,10},{4,12},{6,14},{8,0},{10,2},{12,4},{14,6},{1,9},{3,11}... | collective-permute-start | bytes 208904 | tf_op jit(solution)/shard_map/ppermute | solution.py:400
  6.9 6.7 %collective-permute-start.1 = (s16[272,128]{1,0:T(8,128)(2,1)}, s16[272,128]{1,0:T(8,128)(2,1)S(1)}, u32[]{:S(2)}, u32[]{:S(2)}) collective-permute-start(s16[272,128]{1,0:T(8,128)(2,1)} %pack.1.refs_0_), channel_id=1, source_target_pairs={{0,4},{2,6},{4,0},{6,2},{8,12},{10,14},{12,8},{14,10},{1,5},{3,7},... | collective-permute-start | bytes 208904 | tf_op jit(solution)/shard_map/ppermute | solution.py:400
  13.6 5.4 %copy-start.1 = (s32[3]{0:T(128)S(1)}, s32[3]{0:T(128)}, u32[]{:S(2)}) copy-start(s32[3]{0:T(128)} %pad_add_fusion.rest_0_.place_ref.after_ref) | copy-start | bytes 40
  13.6 5.4 %copy-start.2 = (s32[1,2,30]{2,1,0:T(2,128)S(1)}, s32[1,2,30]{2,1,0:T(2,128)}, u32[]{:S(2)}) copy-start(s32[1,2,30]{2,1,0:T(2,128)} %entry_ref.5) | copy-start | bytes 724
  13.6 8.4 %collective-permute-start.5 = (s16[1088,128]{1,0:T(8,128)(2,1)S(1)}, s16[1088,128]{1,0:T(8,128)(2,1)S(1)}, u32[]{:S(2)}, u32[]{:S(2)}) collective-permute-start(s16[1088,128]{1,0:T(8,128)(2,1)S(1)} %stack.17.rest_0_), channel_id=1, source_target_pairs={{0,2},{2,0},{4,6},{6,4},{8,10},{10,8},{12,14},{14,12},{1,3},{3,1},... | collective-permute-start | bytes 835592 | tf_op jit(solution)/shard_map/ppermute | solution.py:400
  15.2 3.8 %collective-permute-start.4 = (s16[1088,128]{1,0:T(8,128)(2,1)S(1)}, s16[1088,128]{1,0:T(8,128)(2,1)S(1)}, u32[]{:S(2)}, u32[]{:S(2)}) collective-permute-start(s16[1088,128]{1,0:T(8,128)(2,1)S(1)} %stack.17.rest_0_), channel_id=1, source_target_pairs={{0,1},{1,0},{2,3},{3,2},{4,5},{5,4},{6,7},{7,6},{8,9},{9,8},{10,11... | collective-permute-start | bytes 835592 | tf_op jit(solution)/shard_map/ppermute | solution.py:403
  22.0 2.3 %collective-permute-start.6 = (s16[1088,128]{1,0:T(8,128)(2,1)S(1)}, s16[1088,128]{1,0:T(8,128)(2,1)S(1)}, u32[]{:S(2)}, u32[]{:S(2)}) collective-permute-start(s16[1088,128]{1,0:T(8,128)(2,1)S(1)} %collective-permute-done.5.rest_0_), channel_id=1, source_target_pairs={{0,1},{1,0},{2,3},{3,2},{4,5},{5,4},{6,7},{7,6},{8,9},{9,8},{10,11... | collective-permute-start | bytes 835592 | tf_op jit(solution)/shard_map/ppermute | solution.py:403
  34.7 23.8 %copy-start.3 = (s32[435,2]{0,1:T(2,128)S(1)}, s32[435,2]{0,1:T(2,128)}, u32[]{:S(2)}) copy-start(s32[435,2]{0,1:T(2,128)} %param.8) | copy-start | bytes 10444
  34.7 8.8 %collective-permute-start.7 = (s16[2,512,128]{2,1,0:T(8,128)(2,1)S(1)}, s16[2,512,128]{2,1,0:T(8,128)(2,1)S(1)}, u32[]{:S(2)}, u32[]{:S(2)}) collective-permute-start(s16[2,512,128]{2,1,0:T(8,128)(2,1)S(1)} %correlate.3), channel_id=1, source_target_pairs={{0,2},{2,0},{4,6},{6,4},{8,10},{10,8},{12,14},{14,12},{1,3},{3,1},... | collective-permute-start | bytes 786440 | tf_op jit(solution)/shard_map/ppermute | solution.py:400
  43.8 5.7 %collective-permute-start.8 = (s16[512,128]{1,0:T(8,128)(2,1)S(1)}, s16[512,128]{1,0:T(8,128)(2,1)S(1)}, u32[]{:S(2)}, u32[]{:S(2)}) collective-permute-start(s16[512,128]{1,0:T(8,128)(2,1)S(1)} %get-tuple-element.38), channel_id=1, source_target_pairs={{0,16},{16,0},{1,17},{17,1},{2,18},{18,2},{3,19},{19,3},{4,20},{20... | collective-permute-start | bytes 393224 | tf_op jit(solution)/shard_map/ppermute | solution.py:547
  49.7 4.5 %collective-permute-start.9 = (s16[128,128]{1,0:T(8,128)(2,1)S(1)}, s16[128,128]{1,0:T(8,128)(2,1)S(1)}, u32[]{:S(2)}, u32[]{:S(2)}) collective-permute-start(s16[128,128]{1,0:T(8,128)(2,1)S(1)} %get-tuple-element.40), channel_id=1, source_target_pairs={{0,4},{2,6},{4,0},{6,2},{8,12},{10,14},{12,8},{14,10},{1,5},{3,7},... | collective-permute-start | bytes 98312 | tf_op jit(solution)/shard_map/ppermute | solution.py:400
  50.8 4.8 %collective-permute-start.10 = (s16[128,128]{1,0:T(8,128)(2,1)S(1)}, s16[128,128]{1,0:T(8,128)(2,1)S(1)}, u32[]{:S(2)}, u32[]{:S(2)}) collective-permute-start(s16[128,128]{1,0:T(8,128)(2,1)S(1)} %get-tuple-element.41), channel_id=1, source_target_pairs={{0,8},{2,10},{4,12},{6,14},{8,0},{10,2},{12,4},{14,6},{1,9},{3,11}... | collective-permute-start | bytes 98312 | tf_op jit(solution)/shard_map/ppermute | solution.py:400
  52.8 5.7 %collective-permute-start.11 = (s16[128,128]{1,0:T(8,128)(2,1)S(1)}, s16[128,128]{1,0:T(8,128)(2,1)S(1)}, u32[]{:S(2)}, u32[]{:S(2)}) collective-permute-start(s16[128,128]{1,0:T(8,128)(2,1)S(1)} %get-tuple-element.42), channel_id=1, source_target_pairs={{0,12},{2,14},{4,8},{6,10},{8,4},{10,6},{12,0},{14,2},{1,13},{3,15... | collective-permute-start | bytes 98312 | tf_op jit(solution)/shard_map/ppermute | solution.py:400

commit v4 on v3

--- a/solution.py
+++ b/solution.py
@@ -125,7 +125,7 @@
 
 
 def prepare_kernel(
-    place_ref, entry_ref, after_ref, held_in, *rest, columns, started, group, near, far, per, fine, pitch
+    chip_ref, core_ref, x_ref, entry_ref, after_ref, held_in, *rest, columns, started, group, near, far, per, fine, pitch
 ):
     del after_ref, held_in
     stacks = rest[: len(columns)]
@@ -134,9 +134,9 @@
         carry_in, found_in = rest[:2]
         rest = rest[2:]
     held, carry_ref, found_ref, source_ref = rest
-    chip = place_ref[0]
-    core = place_ref[1]
-    x = place_ref[2]
+    chip = chip_ref[0]
+    core = core_ref[0]
+    x = x_ref[0]
     q_here = source_ref.shape[0]
     per_bits = per.bit_length() - 1
     near_bits = near.bit_length() - 1
@@ -235,7 +235,8 @@
 def correlate_kernel(source_ref, held, *rest, first_pair, pairs, spectra, sent):
     outs = rest[: 1 if sent else GROUP]
     rest = rest[len(outs) :]
-    even, odd, wide_even, wide_odd, kept = rest
+    even, odd, wide_even, wide_odd, kept = rest[:5]
+    sums = rest[5:] if sent else outs
 
     def gather(unit, into):
         for first in range(0, LANES, 32):
@@ -289,17 +290,11 @@
             second = jnp.where(upper, pltpu.roll(second, HALF, 1), second)
             value = jnp.where(left, first, second)
             at = pl.ds(pl.multiple_of(pair * HALF, HALF), HALF)
-            if outs[0].dtype == jnp.int16:
-                value = encode(value)
-                outs[0][centre, at, :] = value
-            else:
-                outs[centre][at, :] = value
+            sums[centre][at, :] = value
 
     base = 2 * first_pair
     last = base + 2 * pairs - 1
     gather(base, even)
-    wide_odd[...] = jnp.zeros_like(wide_odd)
-    kept[...] = jnp.zeros_like(kept)
 
     def one(pair, _):
         unit = base + 2 * pair
@@ -314,6 +309,11 @@
 
     lax.fori_loop(0, pairs, one, 0)
     emit(pairs - 1, correlate(wide_odd))
+    if sent:
+        for centre in range(GROUP):
+            for pair in range(pairs):
+                at = slice(pair * HALF, (pair + 1) * HALF)
+                outs[0][centre, at, :] = encode(sums[centre][at, :])
 
 
 def join_kernel(*refs, arrivals):
@@ -405,7 +405,7 @@
     chip = lax.axis_index("chip")
     core = lax.axis_index("core")
     x = lax.axis_index("tm")
-    place = jnp.stack([chip, core, x]).astype(jnp.int32)
+    place = [value.astype(jnp.int32).reshape(1) for value in (chip, core, x)]
     other = across_cores(volts)
     block = pl.pallas_call(
         pack_kernel,
@@ -429,20 +429,20 @@
     def rows(side, *operands):
         return pl.pallas_call(
             functools.partial(rows_kernel, first=side * spectra, pitch=pitch),
-            in_specs=[HBM, ANY, VMEM][: 2 + side],
+            in_specs=[HBM, SMEM, SMEM, SMEM, VMEM][: 4 + side],
             out_specs=VMEM,
             out_shape=held_type,
             scratch_shapes=[
                 pltpu.VMEM((channels // WIDTH, 2, spectra, 32, 2, WIDTH), jnp.bfloat16),
                 pltpu.SemaphoreType.DMA((channels // WIDTH,)),
             ],
-            input_output_aliases={2: 0} if side else {},
+            input_output_aliases={4: 0} if side else {},
             compiler_params=params(40),
             cost_estimate=cost(5),
             name="rows",
         )(*operands)
 
-    held = rows(0, volts, place)
+    held = rows(0, volts, *place)
     size = block.shape[0]
     stack = pl.pallas_call(
         stack_kernel,
@@ -455,10 +455,10 @@
     )(held, *line)
     mine = [stack] + [across_chips(stack, y) for y in range(1, near)]
     theirs = [across_cores(stack)]
-    held = rows(1, other, place, held)
+    held = rows(1, other, *place, held)
     each = far * pairs
     arrived = []
-    after = place
+    after = entry
     for group in range(centres // GROUP):
         state = ()
         for part in range(3 if near > 1 else 1):
@@ -482,7 +482,7 @@
                     fine=fine,
                     pitch=pitch,
                 ),
-                in_specs=[SMEM, VMEM, ANY] + [VMEM] * (1 + len(stacks) + len(state)),
+                in_specs=[SMEM, SMEM, SMEM, VMEM, ANY] + [VMEM] * (1 + len(stacks) + len(state)),
                 out_specs=[VMEM] * 4,
                 out_shape=[
                     held_type,
@@ -490,11 +490,11 @@
                     jax.ShapeDtypeStruct((Q, LANES), jnp.float32),
                     jax.ShapeDtypeStruct((Q // 2, LANES), jnp.int32),
                 ],
-                input_output_aliases={3: 0},
+                input_output_aliases={5: 0},
                 compiler_params=params(16),
                 cost_estimate=cost(2),
                 name="prepare",
-            )(place, entry, after, held, *stacks, *state)
+            )(*place, entry, after, held, *stacks, *state)
         def correlate(first_pair, out_types, source=source, held=held):
             return pl.pallas_call(
                 functools.partial(
@@ -513,7 +513,8 @@
                     pltpu.VMEM((GROUP, 2 * LANES, 2 * spectra * LANES), jnp.bfloat16),
                     pltpu.VMEM((GROUP, 2 * LANES, 2 * spectra * LANES), jnp.bfloat16),
                     pltpu.VMEM((GROUP, HALF, LANES), jnp.float32),
-                ],
+                ]
+                + [pltpu.VMEM((each * HALF, LANES), jnp.float32)] * (GROUP if len(out_types) == 1 else 0),
                 compiler_params=params(12),
                 cost_estimate=cost(9),
                 name="correlate",

time: 60.2 us -> 58.5 us (0.972)
  Pallas kernels: 34.1 us -> 31.9 us
  waiting for transfers between devices: 10.2 us -> 11.4 us
  other arithmetic: 0.65 us -> 0 us
    pallas_call x3, Pallas kernels: 6.7 us -> 5.08 us  [on_device(): pl.pallas_call(functools.partial(prepare_kernel, columns=columns, started...]
    ppermute x8, waiting for transfers between devices: 6.05 us -> 7.28 us  [across_chips(): return lax.ppermute(x, 'chip', [(i, i ^ step) for i in range(chips)])]
    another operation x1 -> x0, other arithmetic: 0.65 us -> none  [on_device(): place = jnp.stack([chip, core, x]).astype(jnp.int32)]
    pallas_call x2, Pallas kernels: 16.1 us -> 15.5 us  [correlate(): pl.pallas_call(functools.partial(correlate_kernel, first_pair=first_pair,...]
  transfers between devices with their start and end apart: 12 -> 12, of which waited for: 4 -> 6; matrix products, arithmetic and copies ran while one was open for 1% -> 0% of each run, Pallas kernels for 36% -> 35%
where the time goes in v4:
time: 58.5 us; the launch traced here: 58.4 us
  Pallas kernels  31.9 us (55%)
  starting transfers between devices  14.9 us (25%)
  waiting for transfers between devices  11.4 us (19%)
    pallas_call x2, Pallas kernels, correlate(): pl.pallas_call(functools.partial(correlate_kernel, first_pair=first_pair,...  15.5 us
    ppermute x8, starting transfers between devices, across_chips(): return lax.ppermute(x, 'chip', [(i, i ^ step) for i in range(chips)])  12.9 us
    pallas_call x2, Pallas kernels, rows(): pl.pallas_call(functools.partial(rows_kernel, first=side * spectra, pitch...  7.47 us
    ppermute x8, waiting for transfers between devices, across_chips(): return lax.ppermute(x, 'chip', [(i, i ^ step) for i in range(chips)])  7.28 us
    pallas_call x3, Pallas kernels, on_device(): pl.pallas_call(functools.partial(prepare_kernel, columns=columns, started...  5.08 us
    ppermute x1, waiting for transfers between devices, on_device(): lax.ppermute(own[c], 'tm', [(i, i ^ centre) for i in range(tm)])  3.91 us
    pallas_call x1, Pallas kernels, on_device(): pl.pallas_call(pack_kernel, in_specs=[HBM, HBM], out_specs=VMEM, out_shap...  1.77 us
    pallas_call x1, Pallas kernels, on_device(): pl.pallas_call(functools.partial(finish_kernel, arrivals=len(final), pair...  1.63 us
  transfers between devices with their start and end apart: 12, of which 6 were waited for; matrix products, arithmetic and copies ran while one was open for 0% of the time, Pallas kernels for 35%

profile of v4, /device:TPU:0, one launch (start us, length us, event | category | flops | bytes accessed | tf_op | source)
XLA Modules:
  0.0 58.4 jit_solution(6520668424819932628)
XLA Ops:
  0.0 0.5 collective-permute-start
  0.5 1.8 %pack.1.refs_0_ = s16[272,128]{1,0:T(8,128)(2,1)} custom-call(f32[64,512]{1,0:T(8,128)} %turning_hbm.1, s32[4,128]{1,0:T(4,128)} %bitcast.6), custom_call_target="tpu_custom_call" | custom-call | flops 1000000000 | bytes 3000000 | tf_op jit(solution)/shard_map/pack/pallas_call | solution.py:410
  2.2 4.7 %collective-permute-start.3 = (s16[272,128]{1,0:T(8,128)(2,1)}, s16[272,128]{1,0:T(8,128)(2,1)S(1)}, u32[]{:S(2)}, u32[]{:S(2)}) collective-permute-start(s16[272,128]{1,0:T(8,128)(2,1)} %pack.1.refs_0_), channel_id=1, source_target_pairs={{0,12},{2,14},{4,8},{6,10},{8,4},{10,6},{12,0},{14,2},{1,13},{3,15... | collective-permute-start | bytes 208904 | tf_op jit(solution)/shard_map/ppermute | solution.py:400
  6.9 0.6 %collective-permute-start.1 = (s16[272,128]{1,0:T(8,128)(2,1)}, s16[272,128]{1,0:T(8,128)(2,1)S(1)}, u32[]{:S(2)}, u32[]{:S(2)}) collective-permute-start(s16[272,128]{1,0:T(8,128)(2,1)} %pack.1.refs_0_), channel_id=1, source_target_pairs={{0,4},{2,6},{4,0},{6,2},{8,12},{10,14},{12,8},{14,10},{1,5},{3,7},... | collective-permute-start | bytes 208904 | tf_op jit(solution)/shard_map/ppermute | solution.py:400
  7.6 3.7 %rows.2.rest_3_.after_ref = f32[40968,128]{1,0:T(8,128)S(1)} custom-call(bf16[2,2,30,2,8192]{4,3,2,1,0:T(2,128)(2,1)} %volts_ref.1, s32[1]{0:T(128)} %bitcast.1.rest_0_.chip_ref, s32[1]{0:T(128)} %bitcast.2.rest_1_.core_ref, s32[1]{0:T(128)} %bitcast.3.rest_2_.x_ref), custom_call_target="tpu_custom_call" | custom-call | flops 5000000000 | bytes 15000000 | tf_op jit(solution)/shard_map/rows/pallas_call | solution.py:430
  11.3 2.3 %collective-permute-done.2.refs_2_ = s16[272,128]{1,0:T(8,128)(2,1)S(1)} collective-permute-done((s16[272,128]{1,0:T(8,128)(2,1)}, s16[272,128]{1,0:T(8,128)(2,1)S(1)}, u32[]{:S(2)}, u32[]{:S(2)}) %collective-permute-start.2) | collective-permute-done | bytes 69664 | tf_op jit(solution)/shard_map/ppermute | solution.py:400
  13.6 1.6 %collective-permute-start.5 = (s16[1088,128]{1,0:T(8,128)(2,1)S(1)}, s16[1088,128]{1,0:T(8,128)(2,1)S(1)}, u32[]{:S(2)}, u32[]{:S(2)}) collective-permute-start(s16[1088,128]{1,0:T(8,128)(2,1)S(1)} %stack.1.rest_0_), channel_id=1, source_target_pairs={{0,2},{2,0},{4,6},{6,4},{8,10},{10,8},{12,14},{14,12},{1,3},{3,1},... | collective-permute-start | bytes 835592 | tf_op jit(solution)/shard_map/ppermute | solution.py:400
  15.2 3.7 %rows.3.held_in = f32[40968,128]{1,0:T(8,128)S(1)} custom-call(bf16[2,2,30,2,8192]{4,3,2,1,0:T(2,128)(2,1)} %collective-permute-done.volts_ref, s32[1]{0:T(128)} %bitcast.1.rest_0_.chip_ref, s32[1]{0:T(128)} %bitcast.2.rest_1_.core_ref, s32[1]{0:T(128)} %bitcast.3.rest_2_.x_ref, f32[40968,128]{1,0:T(8,128)S(1)} %rows.2.rest_3_.after_ref), custom_call_target="tpu_custom_call", output_to_operand_aliasing={{}: (4, {})} | custom-call | flops 5000000000 | bytes 15000000 | tf_op jit(solution)/shard_map/rows/pallas_call | solution.py:430
  19.0 2.4 %prepare.3 = (f32[40968,128]{1,0:T(8,128)S(1)}, f32[32,128]{1,0:T(8,128)S(1)}, f32[64,128]{1,0:T(8,128)S(1)}, s32[32,128]{1,0:T(8,128)}) custom-call(s32[1]{0:T(128)} %bitcast.1.rest_0_.chip_ref, s32[1]{0:T(128)} %bitcast.2.rest_1_.core_ref, s32[1]{0:T(128)} %bitcast.3.rest_2_.x_ref, s32[1,2,30]{2,1,0:T(2,128)S(1)} %copy-done.1, ...), custom_call_target="tpu_custom_call", output_to_operand_aliasing={{0}: (5, {})} | custom-call | flops 2000000000 | bytes 6000000 | tf_op jit(solution)/shard_map/prepare/pallas_call | solution.py:473
  21.4 0.6 %collective-permute-done.5.rest_0_ = s16[1088,128]{1,0:T(8,128)(2,1)S(1)} collective-permute-done((s16[1088,128]{1,0:T(8,128)(2,1)S(1)}, s16[1088,128]{1,0:T(8,128)(2,1)S(1)}, u32[]{:S(2)}, u32[]{:S(2)}) %collective-permute-start.5) | collective-permute-done | bytes 278560 | tf_op jit(solution)/shard_map/ppermute | solution.py:400
  22.0 1.3 %prepare.4 = (f32[40968,128]{1,0:T(8,128)S(1)}, f32[32,128]{1,0:T(8,128)S(1)}, f32[64,128]{1,0:T(8,128)S(1)}, s32[32,128]{1,0:T(8,128)}) custom-call(s32[1]{0:T(128)} %bitcast.1.rest_0_.chip_ref, s32[1]{0:T(128)} %bitcast.2.rest_1_.core_ref, s32[1]{0:T(128)} %bitcast.3.rest_2_.x_ref, s32[1,2,30]{2,1,0:T(2,128)S(1)} %copy-done.1, ...), custom_call_target="tpu_custom_call", output_to_operand_aliasing={{0}: (5, {})} | custom-call | flops 2000000000 | bytes 6000000 | tf_op jit(solution)/shard_map/prepare/pallas_call | solution.py:473
  23.6 1.3 %prepare.5 = (f32[40968,128]{1,0:T(8,128)S(1)}, f32[32,128]{1,0:T(8,128)}, f32[64,128]{1,0:T(8,128)}, s32[32,128]{1,0:T(8,128)S(1)}) custom-call(s32[1]{0:T(128)} %bitcast.1.rest_0_.chip_ref, s32[1]{0:T(128)} %bitcast.2.rest_1_.core_ref, s32[1]{0:T(128)} %bitcast.3.rest_2_.x_ref, s32[1,2,30]{2,1,0:T(2,128)S(1)} %copy-done.1, ...), custom_call_target="tpu_custom_call", output_to_operand_aliasing={{0}: (5, {})} | custom-call | flops 2000000000 | bytes 6000000 | tf_op jit(solution)/shard_map/prepare/pallas_call | solution.py:473
  24.9 7.8 %correlate.3 = s16[2,512,128]{2,1,0:T(8,128)(2,1)S(1)} custom-call(s32[32,128]{1,0:T(8,128)S(1)} %get-tuple-element.33.source_ref, f32[40968,128]{1,0:T(8,128)S(1)} %get-tuple-element.34.held), custom_call_target="tpu_custom_call" | custom-call | flops 8999999488 | bytes 27000000 | tf_op jit(solution)/shard_map/correlate/pallas_call | solution.py:499
  32.7 1.6 %collective-permute-start.7 = (s16[2,512,128]{2,1,0:T(8,128)(2,1)S(1)}, s16[2,512,128]{2,1,0:T(8,128)(2,1)S(1)}, u32[]{:S(2)}, u32[]{:S(2)}) collective-permute-start(s16[2,512,128]{2,1,0:T(8,128)(2,1)S(1)} %correlate.3), channel_id=1, source_target_pairs={{0,2},{2,0},{4,6},{6,4},{8,10},{10,8},{12,14},{14,12},{1,3},{3,1},... | collective-permute-start | bytes 786440 | tf_op jit(solution)/shard_map/ppermute | solution.py:400
  34.3 7.7 %correlate.2 = (f32[512,128]{1,0:T(8,128)S(1)}, f32[512,128]{1,0:T(8,128)S(1)}) custom-call(s32[32,128]{1,0:T(8,128)S(1)} %get-tuple-element.33.source_ref, f32[40968,128]{1,0:T(8,128)S(1)} %get-tuple-element.34.held), custom_call_target="tpu_custom_call" | custom-call | flops 8999999488 | bytes 27000000 | tf_op jit(solution)/shard_map/correlate/pallas_call | solution.py:499
  42.0 0.2 join.1
  42.3 1.6 %collective-permute-start.8 = (s16[512,128]{1,0:T(8,128)(2,1)S(1)}, s16[512,128]{1,0:T(8,128)(2,1)S(1)}, u32[]{:S(2)}, u32[]{:S(2)}) collective-permute-start(s16[512,128]{1,0:T(8,128)(2,1)S(1)} %get-tuple-element.38), channel_id=1, source_target_pairs={{0,16},{16,0},{1,17},{17,1},{2,18},{18,2},{3,19},{19,3},{4,20},{20... | collective-permute-start | bytes 393224 | tf_op jit(solution)/shard_map/ppermute | solution.py:548
  43.8 3.9 %collective-permute-done.8.refs_0_ = s16[512,128]{1,0:T(8,128)(2,1)S(1)} collective-permute-done((s16[512,128]{1,0:T(8,128)(2,1)S(1)}, s16[512,128]{1,0:T(8,128)(2,1)S(1)}, u32[]{:S(2)}, u32[]{:S(2)}) %collective-permute-start.8) | collective-permute-done | bytes 131104 | tf_op jit(solution)/shard_map/ppermute | solution.py:548
  47.9 1.2 %collective-permute-start.9 = (s16[128,128]{1,0:T(8,128)(2,1)S(1)}, s16[128,128]{1,0:T(8,128)(2,1)S(1)}, u32[]{:S(2)}, u32[]{:S(2)}) collective-permute-start(s16[128,128]{1,0:T(8,128)(2,1)S(1)} %get-tuple-element.40), channel_id=1, source_target_pairs={{0,4},{2,6},{4,0},{6,2},{8,12},{10,14},{12,8},{14,10},{1,5},{3,7},... | collective-permute-start | bytes 98312 | tf_op jit(solution)/shard_map/ppermute | solution.py:400
  49.1 1.9 %collective-permute-start.10 = (s16[128,128]{1,0:T(8,128)(2,1)S(1)}, s16[128,128]{1,0:T(8,128)(2,1)S(1)}, u32[]{:S(2)}, u32[]{:S(2)}) collective-permute-start(s16[128,128]{1,0:T(8,128)(2,1)S(1)} %get-tuple-element.41), channel_id=1, source_target_pairs={{0,8},{2,10},{4,12},{6,14},{8,0},{10,2},{12,4},{14,6},{1,9},{3,11}... | collective-permute-start | bytes 98312 | tf_op jit(solution)/shard_map/ppermute | solution.py:400
  51.0 1.3 %collective-permute-start.11 = (s16[128,128]{1,0:T(8,128)(2,1)S(1)}, s16[128,128]{1,0:T(8,128)(2,1)S(1)}, u32[]{:S(2)}, u32[]{:S(2)}) collective-permute-start(s16[128,128]{1,0:T(8,128)(2,1)S(1)} %get-tuple-element.42), channel_id=1, source_target_pairs={{0,12},{2,14},{4,8},{6,10},{8,4},{10,6},{12,0},{14,2},{1,13},{3,15... | collective-permute-start | bytes 98312 | tf_op jit(solution)/shard_map/ppermute | solution.py:400
  52.4 1.6 %collective-permute-done.10.refs_1_ = s16[128,128]{1,0:T(8,128)(2,1)S(1)} collective-permute-done((s16[128,128]{1,0:T(8,128)(2,1)S(1)}, s16[128,128]{1,0:T(8,128)(2,1)S(1)}, u32[]{:S(2)}, u32[]{:S(2)}) %collective-permute-start.10) | collective-permute-done | bytes 32800 | tf_op jit(solution)/shard_map/ppermute | solution.py:400
  54.0 2.8 %collective-permute-done.11.refs_2_ = s16[128,128]{1,0:T(8,128)(2,1)S(1)} collective-permute-done((s16[128,128]{1,0:T(8,128)(2,1)S(1)}, s16[128,128]{1,0:T(8,128)(2,1)S(1)}, u32[]{:S(2)}, u32[]{:S(2)}) %collective-permute-start.11) | collective-permute-done | bytes 32800 | tf_op jit(solution)/shard_map/ppermute | solution.py:400
  56.8 1.6 %finish.1 = f32[4,2,4,435]{3,2,1,0:T(4,128)} custom-call(s32[2,435]{1,0:T(2,128)S(1)} %bitcast.5, f32[128,128]{1,0:T(8,128)S(1)} %get-tuple-element.39.own_ref, s16[128,128]{1,0:T(8,128)(2,1)S(1)} %collective-permute-done.9.refs_0_, s16[128,128]{1,0:T(8,128)(2,1)S(1)} %collective-permute-done.10.refs_1_, s16[128,128]{1,0:T(8,128)(2,1)S(1)} %collective-permute-done.11.refs_2_), custom_call_target="tpu_custom_call" | custom-call | flops 2000000000 | bytes 6000000 | tf_op jit(solution)/shard_map/finish/pallas_call | solution.py:564
  (18 shorter events, 0.5 us)
Async XLA Ops:
  0.0 15.2 %collective-permute-start = (bf16[2,2,30,2,8192]{4,3,2,1,0:T(2,128)(2,1)}, bf16[2,2,30,2,8192]{4,3,2,1,0:T(2,128)(2,1)}, u32[]{:S(2)}, u32[]{:S(2)}) collective-permute-start(bf16[2,2,30,2,8192]{4,3,2,1,0:T(2,128)(2,1)} %volts_ref.1), channel_id=1, source_target_pairs={{0,1},{1,0},{2,3},{3,2},{4,5},{5,4},{6,7},{7,6},{8,9},{9,8},{10,11... | collective-permute-start | bytes 11796488 | tf_op jit(solution)/shard_map/ppermute | solution.py:403
  2.2 11.4 %copy-start = (s16[272,128]{1,0:T(8,128)(2,1)S(1)}, s16[272,128]{1,0:T(8,128)(2,1)}, u32[]{:S(2)}) copy-start(s16[272,128]{1,0:T(8,128)(2,1)} %pack.1.refs_0_) | copy-start | bytes 208900
  2.2 9.1 %collective-permute-start.3 = (s16[272,128]{1,0:T(8,128)(2,1)}, s16[272,128]{1,0:T(8,128)(2,1)S(1)}, u32[]{:S(2)}, u32[]{:S(2)}) collective-permute-start(s16[272,128]{1,0:T(8,128)(2,1)} %pack.1.refs_0_), channel_id=1, source_target_pairs={{0,12},{2,14},{4,8},{6,10},{8,4},{10,6},{12,0},{14,2},{1,13},{3,15... | collective-permute-start | bytes 208904 | tf_op jit(solution)/shard_map/ppermute | solution.py:400
  6.9 6.7 %collective-permute-start.2 = (s16[272,128]{1,0:T(8,128)(2,1)}, s16[272,128]{1,0:T(8,128)(2,1)S(1)}, u32[]{:S(2)}, u32[]{:S(2)}) collective-permute-start(s16[272,128]{1,0:T(8,128)(2,1)} %pack.1.refs_0_), channel_id=1, source_target_pairs={{0,8},{2,10},{4,12},{6,14},{8,0},{10,2},{12,4},{14,6},{1,9},{3,11}... | collective-permute-start | bytes 208904 | tf_op jit(solution)/shard_map/ppermute | solution.py:400
  6.9 6.7 %collective-permute-start.1 = (s16[272,128]{1,0:T(8,128)(2,1)}, s16[272,128]{1,0:T(8,128)(2,1)S(1)}, u32[]{:S(2)}, u32[]{:S(2)}) collective-permute-start(s16[272,128]{1,0:T(8,128)(2,1)} %pack.1.refs_0_), channel_id=1, source_target_pairs={{0,4},{2,6},{4,0},{6,2},{8,12},{10,14},{12,8},{14,10},{1,5},{3,7},... | collective-permute-start | bytes 208904 | tf_op jit(solution)/shard_map/ppermute | solution.py:400
  13.6 5.4 %copy-start.1 = (s32[1,2,30]{2,1,0:T(2,128)S(1)}, s32[1,2,30]{2,1,0:T(2,128)}, u32[]{:S(2)}) copy-start(s32[1,2,30]{2,1,0:T(2,128)} %after_ref.5) | copy-start | bytes 724
  13.6 8.4 %collective-permute-start.5 = (s16[1088,128]{1,0:T(8,128)(2,1)S(1)}, s16[1088,128]{1,0:T(8,128)(2,1)S(1)}, u32[]{:S(2)}, u32[]{:S(2)}) collective-permute-start(s16[1088,128]{1,0:T(8,128)(2,1)S(1)} %stack.1.rest_0_), channel_id=1, source_target_pairs={{0,2},{2,0},{4,6},{6,4},{8,10},{10,8},{12,14},{14,12},{1,3},{3,1},... | collective-permute-start | bytes 835592 | tf_op jit(solution)/shard_map/ppermute | solution.py:400
  15.2 3.8 %collective-permute-start.4 = (s16[1088,128]{1,0:T(8,128)(2,1)S(1)}, s16[1088,128]{1,0:T(8,128)(2,1)S(1)}, u32[]{:S(2)}, u32[]{:S(2)}) collective-permute-start(s16[1088,128]{1,0:T(8,128)(2,1)S(1)} %stack.1.rest_0_), channel_id=1, source_target_pairs={{0,1},{1,0},{2,3},{3,2},{4,5},{5,4},{6,7},{7,6},{8,9},{9,8},{10,11... | collective-permute-start | bytes 835592 | tf_op jit(solution)/shard_map/ppermute | solution.py:403
  22.0 1.6 %collective-permute-start.6 = (s16[1088,128]{1,0:T(8,128)(2,1)S(1)}, s16[1088,128]{1,0:T(8,128)(2,1)S(1)}, u32[]{:S(2)}, u32[]{:S(2)}) collective-permute-start(s16[1088,128]{1,0:T(8,128)(2,1)S(1)} %collective-permute-done.5.rest_0_), channel_id=1, source_target_pairs={{0,1},{1,0},{2,3},{3,2},{4,5},{5,4},{6,7},{7,6},{8,9},{9,8},{10,11... | collective-permute-start | bytes 835592 | tf_op jit(solution)/shard_map/ppermute | solution.py:403
  32.7 24.0 %copy-start.2 = (s32[435,2]{0,1:T(2,128)S(1)}, s32[435,2]{0,1:T(2,128)}, u32[]{:S(2)}) copy-start(s32[435,2]{0,1:T(2,128)} %param.8) | copy-start | bytes 10444
  32.7 9.3 %collective-permute-start.7 = (s16[2,512,128]{2,1,0:T(8,128)(2,1)S(1)}, s16[2,512,128]{2,1,0:T(8,128)(2,1)S(1)}, u32[]{:S(2)}, u32[]{:S(2)}) collective-permute-start(s16[2,512,128]{2,1,0:T(8,128)(2,1)S(1)} %correlate.3), channel_id=1, source_target_pairs={{0,2},{2,0},{4,6},{6,4},{8,10},{10,8},{12,14},{14,12},{1,3},{3,1},... | collective-permute-start | bytes 786440 | tf_op jit(solution)/shard_map/ppermute | solution.py:400
  42.3 5.5 %collective-permute-start.8 = (s16[512,128]{1,0:T(8,128)(2,1)S(1)}, s16[512,128]{1,0:T(8,128)(2,1)S(1)}, u32[]{:S(2)}, u32[]{:S(2)}) collective-permute-start(s16[512,128]{1,0:T(8,128)(2,1)S(1)} %get-tuple-element.38), channel_id=1, source_target_pairs={{0,16},{16,0},{1,17},{17,1},{2,18},{18,2},{3,19},{19,3},{4,20},{20... | collective-permute-start | bytes 393224 | tf_op jit(solution)/shard_map/ppermute | solution.py:548
  47.9 4.5 %collective-permute-start.9 = (s16[128,128]{1,0:T(8,128)(2,1)S(1)}, s16[128,128]{1,0:T(8,128)(2,1)S(1)}, u32[]{:S(2)}, u32[]{:S(2)}) collective-permute-start(s16[128,128]{1,0:T(8,128)(2,1)S(1)} %get-tuple-element.40), channel_id=1, source_target_pairs={{0,4},{2,6},{4,0},{6,2},{8,12},{10,14},{12,8},{14,10},{1,5},{3,7},... | collective-permute-start | bytes 98312 | tf_op jit(solution)/shard_map/ppermute | solution.py:400
  49.1 4.8 %collective-permute-start.10 = (s16[128,128]{1,0:T(8,128)(2,1)S(1)}, s16[128,128]{1,0:T(8,128)(2,1)S(1)}, u32[]{:S(2)}, u32[]{:S(2)}) collective-permute-start(s16[128,128]{1,0:T(8,128)(2,1)S(1)} %get-tuple-element.41), channel_id=1, source_target_pairs={{0,8},{2,10},{4,12},{6,14},{8,0},{10,2},{12,4},{14,6},{1,9},{3,11}... | collective-permute-start | bytes 98312 | tf_op jit(solution)/shard_map/ppermute | solution.py:400
  51.0 5.7 %collective-permute-start.11 = (s16[128,128]{1,0:T(8,128)(2,1)S(1)}, s16[128,128]{1,0:T(8,128)(2,1)S(1)}, u32[]{:S(2)}, u32[]{:S(2)}) collective-permute-start(s16[128,128]{1,0:T(8,128)(2,1)S(1)} %get-tuple-element.42), channel_id=1, source_target_pairs={{0,12},{2,14},{4,8},{6,10},{8,4},{10,6},{12,0},{14,2},{1,13},{3,15... | collective-permute-start | bytes 98312 | tf_op jit(solution)/shard_map/ppermute | solution.py:400

commit v5 on v4

--- a/solution.py
+++ b/solution.py
@@ -560,7 +560,7 @@
         cost_estimate=cost(1),
         name="merge",
     )(total, *arrived)
-    final = [across_chips(merged[z], z * near) for z in range(1, far)]
+    final = [across_chips(merged[z], z * near) for z in range(far - 1, 0, -1)]
     return pl.pallas_call(
         functools.partial(finish_kernel, arrivals=len(final), pairs=pairs, scale=Q / channels),
         in_specs=[VMEM] * (2 + len(final)),

time: 58.5 us -> 57 us (0.974)
  waiting for transfers between devices: 11.4 us -> 9.9 us
    ppermute x8, waiting for transfers between devices: 7.28 us -> 5.78 us  [across_chips(): return lax.ppermute(x, 'chip', [(i, i ^ step) for i in range(chips)])]
  transfers between devices with their start and end apart: 12 -> 12, of which waited for: 6 -> 6; matrix products, arithmetic and copies ran while one was open for 0% -> 0% of each run, Pallas kernels for 35% -> 36%
where the time goes in v5:
time: 57 us; the launch traced here: 56.9 us
  Pallas kernels  31.9 us (56%)
  starting transfers between devices  14.9 us (26%)
  waiting for transfers between devices  9.9 us (17%)
    pallas_call x2, Pallas kernels, correlate(): pl.pallas_call(functools.partial(correlate_kernel, first_pair=first_pair,...  15.5 us
    ppermute x8, starting transfers between devices, across_chips(): return lax.ppermute(x, 'chip', [(i, i ^ step) for i in range(chips)])  12.9 us
    pallas_call x2, Pallas kernels, rows(): pl.pallas_call(functools.partial(rows_kernel, first=side * spectra, pitch...  7.47 us
    ppermute x8, waiting for transfers between devices, across_chips(): return lax.ppermute(x, 'chip', [(i, i ^ step) for i in range(chips)])  5.78 us
    pallas_call x3, Pallas kernels, on_device(): pl.pallas_call(functools.partial(prepare_kernel, columns=columns, started...  5.08 us
    ppermute x1, waiting for transfers between devices, on_device(): lax.ppermute(own[c], 'tm', [(i, i ^ centre) for i in range(tm)])  3.91 us
    pallas_call x1, Pallas kernels, on_device(): pl.pallas_call(pack_kernel, in_specs=[HBM, HBM], out_specs=VMEM, out_shap...  1.77 us
    pallas_call x1, Pallas kernels, on_device(): pl.pallas_call(functools.partial(finish_kernel, arrivals=len(final), pair...  1.62 us
  transfers between devices with their start and end apart: 12, of which 6 were waited for; matrix products, arithmetic and copies ran while one was open for 0% of the time, Pallas kernels for 36%

profile of v5, /device:TPU:0, one launch (start us, length us, event | category | flops | bytes accessed | tf_op | source)
XLA Modules:
  0.0 56.9 jit_solution(5909975956659470116)
XLA Ops:
  0.0 0.5 collective-permute-start
  0.5 1.8 %pack.1.refs_0_ = s16[272,128]{1,0:T(8,128)(2,1)} custom-call(f32[64,512]{1,0:T(8,128)} %turning_hbm.1, s32[4,128]{1,0:T(4,128)} %bitcast.6), custom_call_target="tpu_custom_call" | custom-call | flops 1000000000 | bytes 3000000 | tf_op jit(solution)/shard_map/pack/pallas_call | solution.py:410
  2.2 4.7 %collective-permute-start.3 = (s16[272,128]{1,0:T(8,128)(2,1)}, s16[272,128]{1,0:T(8,128)(2,1)S(1)}, u32[]{:S(2)}, u32[]{:S(2)}) collective-permute-start(s16[272,128]{1,0:T(8,128)(2,1)} %pack.1.refs_0_), channel_id=1, source_target_pairs={{0,12},{2,14},{4,8},{6,10},{8,4},{10,6},{12,0},{14,2},{1,13},{3,15... | collective-permute-start | bytes 208904 | tf_op jit(solution)/shard_map/ppermute | solution.py:400
  6.9 0.6 %collective-permute-start.1 = (s16[272,128]{1,0:T(8,128)(2,1)}, s16[272,128]{1,0:T(8,128)(2,1)S(1)}, u32[]{:S(2)}, u32[]{:S(2)}) collective-permute-start(s16[272,128]{1,0:T(8,128)(2,1)} %pack.1.refs_0_), channel_id=1, source_target_pairs={{0,4},{2,6},{4,0},{6,2},{8,12},{10,14},{12,8},{14,10},{1,5},{3,7},... | collective-permute-start | bytes 208904 | tf_op jit(solution)/shard_map/ppermute | solution.py:400
  7.6 3.7 %rows.2.rest_3_.after_ref = f32[40968,128]{1,0:T(8,128)S(1)} custom-call(bf16[2,2,30,2,8192]{4,3,2,1,0:T(2,128)(2,1)} %volts_ref.1, s32[1]{0:T(128)} %bitcast.1.rest_0_.chip_ref, s32[1]{0:T(128)} %bitcast.2.rest_1_.core_ref, s32[1]{0:T(128)} %bitcast.3.rest_2_.x_ref), custom_call_target="tpu_custom_call" | custom-call | flops 5000000000 | bytes 15000000 | tf_op jit(solution)/shard_map/rows/pallas_call | solution.py:430
  11.3 2.3 %collective-permute-done.2.refs_2_ = s16[272,128]{1,0:T(8,128)(2,1)S(1)} collective-permute-done((s16[272,128]{1,0:T(8,128)(2,1)}, s16[272,128]{1,0:T(8,128)(2,1)S(1)}, u32[]{:S(2)}, u32[]{:S(2)}) %collective-permute-start.2) | collective-permute-done | bytes 69664 | tf_op jit(solution)/shard_map/ppermute | solution.py:400
  13.6 1.6 %collective-permute-start.5 = (s16[1088,128]{1,0:T(8,128)(2,1)S(1)}, s16[1088,128]{1,0:T(8,128)(2,1)S(1)}, u32[]{:S(2)}, u32[]{:S(2)}) collective-permute-start(s16[1088,128]{1,0:T(8,128)(2,1)S(1)} %stack.1.rest_0_), channel_id=1, source_target_pairs={{0,2},{2,0},{4,6},{6,4},{8,10},{10,8},{12,14},{14,12},{1,3},{3,1},... | collective-permute-start | bytes 835592 | tf_op jit(solution)/shard_map/ppermute | solution.py:400
  15.2 3.7 %rows.3.held_in = f32[40968,128]{1,0:T(8,128)S(1)} custom-call(bf16[2,2,30,2,8192]{4,3,2,1,0:T(2,128)(2,1)} %collective-permute-done.volts_ref, s32[1]{0:T(128)} %bitcast.1.rest_0_.chip_ref, s32[1]{0:T(128)} %bitcast.2.rest_1_.core_ref, s32[1]{0:T(128)} %bitcast.3.rest_2_.x_ref, f32[40968,128]{1,0:T(8,128)S(1)} %rows.2.rest_3_.after_ref), custom_call_target="tpu_custom_call", output_to_operand_aliasing={{}: (4, {})} | custom-call | flops 5000000000 | bytes 15000000 | tf_op jit(solution)/shard_map/rows/pallas_call | solution.py:430
  19.0 2.4 %prepare.3 = (f32[40968,128]{1,0:T(8,128)S(1)}, f32[32,128]{1,0:T(8,128)S(1)}, f32[64,128]{1,0:T(8,128)S(1)}, s32[32,128]{1,0:T(8,128)}) custom-call(s32[1]{0:T(128)} %bitcast.1.rest_0_.chip_ref, s32[1]{0:T(128)} %bitcast.2.rest_1_.core_ref, s32[1]{0:T(128)} %bitcast.3.rest_2_.x_ref, s32[1,2,30]{2,1,0:T(2,128)S(1)} %copy-done.1, ...), custom_call_target="tpu_custom_call", output_to_operand_aliasing={{0}: (5, {})} | custom-call | flops 2000000000 | bytes 6000000 | tf_op jit(solution)/shard_map/prepare/pallas_call | solution.py:473
  21.4 0.6 %collective-permute-done.5.rest_0_ = s16[1088,128]{1,0:T(8,128)(2,1)S(1)} collective-permute-done((s16[1088,128]{1,0:T(8,128)(2,1)S(1)}, s16[1088,128]{1,0:T(8,128)(2,1)S(1)}, u32[]{:S(2)}, u32[]{:S(2)}) %collective-permute-start.5) | collective-permute-done | bytes 278560 | tf_op jit(solution)/shard_map/ppermute | solution.py:400
  22.0 1.3 %prepare.4 = (f32[40968,128]{1,0:T(8,128)S(1)}, f32[32,128]{1,0:T(8,128)S(1)}, f32[64,128]{1,0:T(8,128)S(1)}, s32[32,128]{1,0:T(8,128)}) custom-call(s32[1]{0:T(128)} %bitcast.1.rest_0_.chip_ref, s32[1]{0:T(128)} %bitcast.2.rest_1_.core_ref, s32[1]{0:T(128)} %bitcast.3.rest_2_.x_ref, s32[1,2,30]{2,1,0:T(2,128)S(1)} %copy-done.1, ...), custom_call_target="tpu_custom_call", output_to_operand_aliasing={{0}: (5, {})} | custom-call | flops 2000000000 | bytes 6000000 | tf_op jit(solution)/shard_map/prepare/pallas_call | solution.py:473
  23.3 0.2 collective-permute-done.6.rest_0_
  23.6 1.3 %prepare.5 = (f32[40968,128]{1,0:T(8,128)S(1)}, f32[32,128]{1,0:T(8,128)}, f32[64,128]{1,0:T(8,128)}, s32[32,128]{1,0:T(8,128)S(1)}) custom-call(s32[1]{0:T(128)} %bitcast.1.rest_0_.chip_ref, s32[1]{0:T(128)} %bitcast.2.rest_1_.core_ref, s32[1]{0:T(128)} %bitcast.3.rest_2_.x_ref, s32[1,2,30]{2,1,0:T(2,128)S(1)} %copy-done.1, ...), custom_call_target="tpu_custom_call", output_to_operand_aliasing={{0}: (5, {})} | custom-call | flops 2000000000 | bytes 6000000 | tf_op jit(solution)/shard_map/prepare/pallas_call | solution.py:473
  24.9 7.8 %correlate.3 = s16[2,512,128]{2,1,0:T(8,128)(2,1)S(1)} custom-call(s32[32,128]{1,0:T(8,128)S(1)} %get-tuple-element.33.source_ref, f32[40968,128]{1,0:T(8,128)S(1)} %get-tuple-element.34.held), custom_call_target="tpu_custom_call" | custom-call | flops 8999999488 | bytes 27000000 | tf_op jit(solution)/shard_map/correlate/pallas_call | solution.py:499
  32.7 1.6 %collective-permute-start.7 = (s16[2,512,128]{2,1,0:T(8,128)(2,1)S(1)}, s16[2,512,128]{2,1,0:T(8,128)(2,1)S(1)}, u32[]{:S(2)}, u32[]{:S(2)}) collective-permute-start(s16[2,512,128]{2,1,0:T(8,128)(2,1)S(1)} %correlate.3), channel_id=1, source_target_pairs={{0,2},{2,0},{4,6},{6,4},{8,10},{10,8},{12,14},{14,12},{1,3},{3,1},... | collective-permute-start | bytes 786440 | tf_op jit(solution)/shard_map/ppermute | solution.py:400
  34.3 7.7 %correlate.2 = (f32[512,128]{1,0:T(8,128)S(1)}, f32[512,128]{1,0:T(8,128)S(1)}) custom-call(s32[32,128]{1,0:T(8,128)S(1)} %get-tuple-element.33.source_ref, f32[40968,128]{1,0:T(8,128)S(1)} %get-tuple-element.34.held), custom_call_target="tpu_custom_call" | custom-call | flops 8999999488 | bytes 27000000 | tf_op jit(solution)/shard_map/correlate/pallas_call | solution.py:499
  42.0 0.2 join.1
  42.3 1.6 %collective-permute-start.8 = (s16[512,128]{1,0:T(8,128)(2,1)S(1)}, s16[512,128]{1,0:T(8,128)(2,1)S(1)}, u32[]{:S(2)}, u32[]{:S(2)}) collective-permute-start(s16[512,128]{1,0:T(8,128)(2,1)S(1)} %get-tuple-element.38), channel_id=1, source_target_pairs={{0,16},{16,0},{1,17},{17,1},{2,18},{18,2},{3,19},{19,3},{4,20},{20... | collective-permute-start | bytes 393224 | tf_op jit(solution)/shard_map/ppermute | solution.py:548
  43.8 3.9 %collective-permute-done.8.refs_0_ = s16[512,128]{1,0:T(8,128)(2,1)S(1)} collective-permute-done((s16[512,128]{1,0:T(8,128)(2,1)S(1)}, s16[512,128]{1,0:T(8,128)(2,1)S(1)}, u32[]{:S(2)}, u32[]{:S(2)}) %collective-permute-start.8) | collective-permute-done | bytes 131104 | tf_op jit(solution)/shard_map/ppermute | solution.py:548
  47.9 2.5 %collective-permute-start.9 = (s16[128,128]{1,0:T(8,128)(2,1)S(1)}, s16[128,128]{1,0:T(8,128)(2,1)S(1)}, u32[]{:S(2)}, u32[]{:S(2)}) collective-permute-start(s16[128,128]{1,0:T(8,128)(2,1)S(1)} %get-tuple-element.40), channel_id=1, source_target_pairs={{0,12},{2,14},{4,8},{6,10},{8,4},{10,6},{12,0},{14,2},{1,13},{3,15... | collective-permute-start | bytes 98312 | tf_op jit(solution)/shard_map/ppermute | solution.py:400
  50.6 1.8 %collective-permute-start.11 = (s16[128,128]{1,0:T(8,128)(2,1)S(1)}, s16[128,128]{1,0:T(8,128)(2,1)S(1)}, u32[]{:S(2)}, u32[]{:S(2)}) collective-permute-start(s16[128,128]{1,0:T(8,128)(2,1)S(1)} %get-tuple-element.42), channel_id=1, source_target_pairs={{0,4},{2,6},{4,0},{6,2},{8,12},{10,14},{12,8},{14,10},{1,5},{3,7},... | collective-permute-start | bytes 98312 | tf_op jit(solution)/shard_map/ppermute | solution.py:400
  52.4 1.3 %collective-permute-done.9.refs_0_ = s16[128,128]{1,0:T(8,128)(2,1)S(1)} collective-permute-done((s16[128,128]{1,0:T(8,128)(2,1)S(1)}, s16[128,128]{1,0:T(8,128)(2,1)S(1)}, u32[]{:S(2)}, u32[]{:S(2)}) %collective-permute-start.9) | collective-permute-done | bytes 32800 | tf_op jit(solution)/shard_map/ppermute | solution.py:400
  53.7 1.5 %collective-permute-done.10.refs_1_ = s16[128,128]{1,0:T(8,128)(2,1)S(1)} collective-permute-done((s16[128,128]{1,0:T(8,128)(2,1)S(1)}, s16[128,128]{1,0:T(8,128)(2,1)S(1)}, u32[]{:S(2)}, u32[]{:S(2)}) %collective-permute-start.10) | collective-permute-done | bytes 32800 | tf_op jit(solution)/shard_map/ppermute | solution.py:400
  55.3 1.6 %finish.1 = f32[4,2,4,435]{3,2,1,0:T(4,128)} custom-call(s32[2,435]{1,0:T(2,128)S(1)} %bitcast.5, f32[128,128]{1,0:T(8,128)S(1)} %get-tuple-element.39.own_ref, s16[128,128]{1,0:T(8,128)(2,1)S(1)} %collective-permute-done.9.refs_0_, s16[128,128]{1,0:T(8,128)(2,1)S(1)} %collective-permute-done.10.refs_1_, s16[128,128]{1,0:T(8,128)(2,1)S(1)} %collective-permute-done.11.refs_2_), custom_call_target="tpu_custom_call" | custom-call | flops 2000000000 | bytes 6000000 | tf_op jit(solution)/shard_map/finish/pallas_call | solution.py:564
  (18 shorter events, 0.4 us)
Async XLA Ops:
  0.0 15.2 %collective-permute-start = (bf16[2,2,30,2,8192]{4,3,2,1,0:T(2,128)(2,1)}, bf16[2,2,30,2,8192]{4,3,2,1,0:T(2,128)(2,1)}, u32[]{:S(2)}, u32[]{:S(2)}) collective-permute-start(bf16[2,2,30,2,8192]{4,3,2,1,0:T(2,128)(2,1)} %volts_ref.1), channel_id=1, source_target_pairs={{0,1},{1,0},{2,3},{3,2},{4,5},{5,4},{6,7},{7,6},{8,9},{9,8},{10,11... | collective-permute-start | bytes 11796488 | tf_op jit(solution)/shard_map/ppermute | solution.py:403
  2.2 11.4 %copy-start = (s16[272,128]{1,0:T(8,128)(2,1)S(1)}, s16[272,128]{1,0:T(8,128)(2,1)}, u32[]{:S(2)}) copy-start(s16[272,128]{1,0:T(8,128)(2,1)} %pack.1.refs_0_) | copy-start | bytes 208900
  2.2 9.1 %collective-permute-start.3 = (s16[272,128]{1,0:T(8,128)(2,1)}, s16[272,128]{1,0:T(8,128)(2,1)S(1)}, u32[]{:S(2)}, u32[]{:S(2)}) collective-permute-start(s16[272,128]{1,0:T(8,128)(2,1)} %pack.1.refs_0_), channel_id=1, source_target_pairs={{0,12},{2,14},{4,8},{6,10},{8,4},{10,6},{12,0},{14,2},{1,13},{3,15... | collective-permute-start | bytes 208904 | tf_op jit(solution)/shard_map/ppermute | solution.py:400
  6.9 6.7 %collective-permute-start.2 = (s16[272,128]{1,0:T(8,128)(2,1)}, s16[272,128]{1,0:T(8,128)(2,1)S(1)}, u32[]{:S(2)}, u32[]{:S(2)}) collective-permute-start(s16[272,128]{1,0:T(8,128)(2,1)} %pack.1.refs_0_), channel_id=1, source_target_pairs={{0,8},{2,10},{4,12},{6,14},{8,0},{10,2},{12,4},{14,6},{1,9},{3,11}... | collective-permute-start | bytes 208904 | tf_op jit(solution)/shard_map/ppermute | solution.py:400
  6.9 6.7 %collective-permute-start.1 = (s16[272,128]{1,0:T(8,128)(2,1)}, s16[272,128]{1,0:T(8,128)(2,1)S(1)}, u32[]{:S(2)}, u32[]{:S(2)}) collective-permute-start(s16[272,128]{1,0:T(8,128)(2,1)} %pack.1.refs_0_), channel_id=1, source_target_pairs={{0,4},{2,6},{4,0},{6,2},{8,12},{10,14},{12,8},{14,10},{1,5},{3,7},... | collective-permute-start | bytes 208904 | tf_op jit(solution)/shard_map/ppermute | solution.py:400
  13.6 5.4 %copy-start.1 = (s32[1,2,30]{2,1,0:T(2,128)S(1)}, s32[1,2,30]{2,1,0:T(2,128)}, u32[]{:S(2)}) copy-start(s32[1,2,30]{2,1,0:T(2,128)} %after_ref.5) | copy-start | bytes 724
  13.6 8.4 %collective-permute-start.5 = (s16[1088,128]{1,0:T(8,128)(2,1)S(1)}, s16[1088,128]{1,0:T(8,128)(2,1)S(1)}, u32[]{:S(2)}, u32[]{:S(2)}) collective-permute-start(s16[1088,128]{1,0:T(8,128)(2,1)S(1)} %stack.1.rest_0_), channel_id=1, source_target_pairs={{0,2},{2,0},{4,6},{6,4},{8,10},{10,8},{12,14},{14,12},{1,3},{3,1},... | collective-permute-start | bytes 835592 | tf_op jit(solution)/shard_map/ppermute | solution.py:400
  15.2 3.8 %collective-permute-start.4 = (s16[1088,128]{1,0:T(8,128)(2,1)S(1)}, s16[1088,128]{1,0:T(8,128)(2,1)S(1)}, u32[]{:S(2)}, u32[]{:S(2)}) collective-permute-start(s16[1088,128]{1,0:T(8,128)(2,1)S(1)} %stack.1.rest_0_), channel_id=1, source_target_pairs={{0,1},{1,0},{2,3},{3,2},{4,5},{5,4},{6,7},{7,6},{8,9},{9,8},{10,11... | collective-permute-start | bytes 835592 | tf_op jit(solution)/shard_map/ppermute | solution.py:403
  22.0 1.6 %collective-permute-start.6 = (s16[1088,128]{1,0:T(8,128)(2,1)S(1)}, s16[1088,128]{1,0:T(8,128)(2,1)S(1)}, u32[]{:S(2)}, u32[]{:S(2)}) collective-permute-start(s16[1088,128]{1,0:T(8,128)(2,1)S(1)} %collective-permute-done.5.rest_0_), channel_id=1, source_target_pairs={{0,1},{1,0},{2,3},{3,2},{4,5},{5,4},{6,7},{7,6},{8,9},{9,8},{10,11... | collective-permute-start | bytes 835592 | tf_op jit(solution)/shard_map/ppermute | solution.py:403
  32.7 22.5 %copy-start.2 = (s32[435,2]{0,1:T(2,128)S(1)}, s32[435,2]{0,1:T(2,128)}, u32[]{:S(2)}) copy-start(s32[435,2]{0,1:T(2,128)} %param.8) | copy-start | bytes 10444
  32.7 9.3 %collective-permute-start.7 = (s16[2,512,128]{2,1,0:T(8,128)(2,1)S(1)}, s16[2,512,128]{2,1,0:T(8,128)(2,1)S(1)}, u32[]{:S(2)}, u32[]{:S(2)}) collective-permute-start(s16[2,512,128]{2,1,0:T(8,128)(2,1)S(1)} %correlate.3), channel_id=1, source_target_pairs={{0,2},{2,0},{4,6},{6,4},{8,10},{10,8},{12,14},{14,12},{1,3},{3,1},... | collective-permute-start | bytes 786440 | tf_op jit(solution)/shard_map/ppermute | solution.py:400
  42.3 5.5 %collective-permute-start.8 = (s16[512,128]{1,0:T(8,128)(2,1)S(1)}, s16[512,128]{1,0:T(8,128)(2,1)S(1)}, u32[]{:S(2)}, u32[]{:S(2)}) collective-permute-start(s16[512,128]{1,0:T(8,128)(2,1)S(1)} %get-tuple-element.38), channel_id=1, source_target_pairs={{0,16},{16,0},{1,17},{17,1},{2,18},{18,2},{3,19},{19,3},{4,20},{20... | collective-permute-start | bytes 393224 | tf_op jit(solution)/shard_map/ppermute | solution.py:548
  47.9 5.8 %collective-permute-start.9 = (s16[128,128]{1,0:T(8,128)(2,1)S(1)}, s16[128,128]{1,0:T(8,128)(2,1)S(1)}, u32[]{:S(2)}, u32[]{:S(2)}) collective-permute-start(s16[128,128]{1,0:T(8,128)(2,1)S(1)} %get-tuple-element.40), channel_id=1, source_target_pairs={{0,12},{2,14},{4,8},{6,10},{8,4},{10,6},{12,0},{14,2},{1,13},{3,15... | collective-permute-start | bytes 98312 | tf_op jit(solution)/shard_map/ppermute | solution.py:400
  50.5 4.8 %collective-permute-start.10 = (s16[128,128]{1,0:T(8,128)(2,1)S(1)}, s16[128,128]{1,0:T(8,128)(2,1)S(1)}, u32[]{:S(2)}, u32[]{:S(2)}) collective-permute-start(s16[128,128]{1,0:T(8,128)(2,1)S(1)} %get-tuple-element.41), channel_id=1, source_target_pairs={{0,8},{2,10},{4,12},{6,14},{8,0},{10,2},{12,4},{14,6},{1,9},{3,11}... | collective-permute-start | bytes 98312 | tf_op jit(solution)/shard_map/ppermute | solution.py:400
  50.6 4.7 %collective-permute-start.11 = (s16[128,128]{1,0:T(8,128)(2,1)S(1)}, s16[128,128]{1,0:T(8,128)(2,1)S(1)}, u32[]{:S(2)}, u32[]{:S(2)}) collective-permute-start(s16[128,128]{1,0:T(8,128)(2,1)S(1)} %get-tuple-element.42), channel_id=1, source_target_pairs={{0,4},{2,6},{4,0},{6,2},{8,12},{10,14},{12,8},{14,10},{1,5},{3,7},... | collective-permute-start | bytes 98312 | tf_op jit(solution)/shard_map/ppermute | solution.py:400

commit v6 on v5

--- a/solution.py
+++ b/solution.py
@@ -508,8 +508,8 @@
                 out_specs=[VMEM] * len(out_types),
                 out_shape=out_types,
                 scratch_shapes=[
-                    pltpu.VMEM((LANES * ROW, LANES), jnp.float32),
-                    pltpu.VMEM((LANES * ROW, LANES), jnp.float32),
+                    pltpu.VMEM((LANES * ROW + ROW, LANES), jnp.float32),
+                    pltpu.VMEM((LANES * ROW + ROW, LANES), jnp.float32),
                     pltpu.VMEM((GROUP, 2 * LANES, 2 * spectra * LANES), jnp.bfloat16),
                     pltpu.VMEM((GROUP, 2 * LANES, 2 * spectra * LANES), jnp.bfloat16),
                     pltpu.VMEM((GROUP, HALF, LANES), jnp.float32),

time: 57 us -> 57.1 us (level)
  no operation moved by 1% of the time
where the time goes in v6:
time: 57.1 us; the launch traced here: 56.9 us
  Pallas kernels  31.9 us (56%)
  starting transfers between devices  14.9 us (26%)
  waiting for transfers between devices  9.96 us (17%)
    pallas_call x2, Pallas kernels, correlate(): pl.pallas_call(functools.partial(correlate_kernel, first_pair=first_pair,...  15.5 us
    ppermute x8, starting transfers between devices, across_chips(): return lax.ppermute(x, 'chip', [(i, i ^ step) for i in range(chips)])  12.9 us
    pallas_call x2, Pallas kernels, rows(): pl.pallas_call(functools.partial(rows_kernel, first=side * spectra, pitch...  7.47 us
    ppermute x8, waiting for transfers between devices, across_chips(): return lax.ppermute(x, 'chip', [(i, i ^ step) for i in range(chips)])  5.81 us
    pallas_call x3, Pallas kernels, on_device(): pl.pallas_call(functools.partial(prepare_kernel, columns=columns, started...  5.08 us
    ppermute x1, waiting for transfers between devices, on_device(): lax.ppermute(own[c], 'tm', [(i, i ^ centre) for i in range(tm)])  3.93 us
    pallas_call x1, Pallas kernels, on_device(): pl.pallas_call(pack_kernel, in_specs=[HBM, HBM], out_specs=VMEM, out_shap...  1.77 us
    pallas_call x1, Pallas kernels, on_device(): pl.pallas_call(functools.partial(finish_kernel, arrivals=len(final), pair...  1.62 us
  transfers between devices with their start and end apart: 12, of which 6 were waited for; matrix products, arithmetic and copies ran while one was open for 0% of the time, Pallas kernels for 36%

profile of v6, /device:TPU:0, one launch (start us, length us, event | category | flops | bytes accessed | tf_op | source)
XLA Modules:
  0.0 56.9 jit_solution(2868796864513821016)
XLA Ops:
  0.0 0.5 collective-permute-start
  0.5 1.8 %pack.1.refs_0_ = s16[272,128]{1,0:T(8,128)(2,1)} custom-call(f32[64,512]{1,0:T(8,128)} %turning_hbm.1, s32[4,128]{1,0:T(4,128)} %bitcast.6), custom_call_target="tpu_custom_call" | custom-call | flops 1000000000 | bytes 3000000 | tf_op jit(solution)/shard_map/pack/pallas_call | solution.py:410
  2.2 4.7 %collective-permute-start.3 = (s16[272,128]{1,0:T(8,128)(2,1)}, s16[272,128]{1,0:T(8,128)(2,1)S(1)}, u32[]{:S(2)}, u32[]{:S(2)}) collective-permute-start(s16[272,128]{1,0:T(8,128)(2,1)} %pack.1.refs_0_), channel_id=1, source_target_pairs={{0,12},{2,14},{4,8},{6,10},{8,4},{10,6},{12,0},{14,2},{1,13},{3,15... | collective-permute-start | bytes 208904 | tf_op jit(solution)/shard_map/ppermute | solution.py:400
  6.9 0.6 %collective-permute-start.1 = (s16[272,128]{1,0:T(8,128)(2,1)}, s16[272,128]{1,0:T(8,128)(2,1)S(1)}, u32[]{:S(2)}, u32[]{:S(2)}) collective-permute-start(s16[272,128]{1,0:T(8,128)(2,1)} %pack.1.refs_0_), channel_id=1, source_target_pairs={{0,4},{2,6},{4,0},{6,2},{8,12},{10,14},{12,8},{14,10},{1,5},{3,7},... | collective-permute-start | bytes 208904 | tf_op jit(solution)/shard_map/ppermute | solution.py:400
  7.6 3.7 %rows.2.rest_3_.after_ref = f32[40968,128]{1,0:T(8,128)S(1)} custom-call(bf16[2,2,30,2,8192]{4,3,2,1,0:T(2,128)(2,1)} %volts_ref.1, s32[1]{0:T(128)} %bitcast.1.rest_0_.chip_ref, s32[1]{0:T(128)} %bitcast.2.rest_1_.core_ref, s32[1]{0:T(128)} %bitcast.3.rest_2_.x_ref), custom_call_target="tpu_custom_call" | custom-call | flops 5000000000 | bytes 15000000 | tf_op jit(solution)/shard_map/rows/pallas_call | solution.py:430
  11.3 2.3 %collective-permute-done.2.refs_2_ = s16[272,128]{1,0:T(8,128)(2,1)S(1)} collective-permute-done((s16[272,128]{1,0:T(8,128)(2,1)}, s16[272,128]{1,0:T(8,128)(2,1)S(1)}, u32[]{:S(2)}, u32[]{:S(2)}) %collective-permute-start.2) | collective-permute-done | bytes 69664 | tf_op jit(solution)/shard_map/ppermute | solution.py:400
  13.6 1.6 %collective-permute-start.5 = (s16[1088,128]{1,0:T(8,128)(2,1)S(1)}, s16[1088,128]{1,0:T(8,128)(2,1)S(1)}, u32[]{:S(2)}, u32[]{:S(2)}) collective-permute-start(s16[1088,128]{1,0:T(8,128)(2,1)S(1)} %stack.1.rest_0_), channel_id=1, source_target_pairs={{0,2},{2,0},{4,6},{6,4},{8,10},{10,8},{12,14},{14,12},{1,3},{3,1},... | collective-permute-start | bytes 835592 | tf_op jit(solution)/shard_map/ppermute | solution.py:400
  15.2 3.7 %rows.3.held_in = f32[40968,128]{1,0:T(8,128)S(1)} custom-call(bf16[2,2,30,2,8192]{4,3,2,1,0:T(2,128)(2,1)} %collective-permute-done.volts_ref, s32[1]{0:T(128)} %bitcast.1.rest_0_.chip_ref, s32[1]{0:T(128)} %bitcast.2.rest_1_.core_ref, s32[1]{0:T(128)} %bitcast.3.rest_2_.x_ref, f32[40968,128]{1,0:T(8,128)S(1)} %rows.2.rest_3_.after_ref), custom_call_target="tpu_custom_call", output_to_operand_aliasing={{}: (4, {})} | custom-call | flops 5000000000 | bytes 15000000 | tf_op jit(solution)/shard_map/rows/pallas_call | solution.py:430
  19.0 2.4 %prepare.3 = (f32[40968,128]{1,0:T(8,128)S(1)}, f32[32,128]{1,0:T(8,128)S(1)}, f32[64,128]{1,0:T(8,128)S(1)}, s32[32,128]{1,0:T(8,128)}) custom-call(s32[1]{0:T(128)} %bitcast.1.rest_0_.chip_ref, s32[1]{0:T(128)} %bitcast.2.rest_1_.core_ref, s32[1]{0:T(128)} %bitcast.3.rest_2_.x_ref, s32[1,2,30]{2,1,0:T(2,128)S(1)} %copy-done.1, ...), custom_call_target="tpu_custom_call", output_to_operand_aliasing={{0}: (5, {})} | custom-call | flops 2000000000 | bytes 6000000 | tf_op jit(solution)/shard_map/prepare/pallas_call | solution.py:473
  21.4 0.6 %collective-permute-done.5.rest_0_ = s16[1088,128]{1,0:T(8,128)(2,1)S(1)} collective-permute-done((s16[1088,128]{1,0:T(8,128)(2,1)S(1)}, s16[1088,128]{1,0:T(8,128)(2,1)S(1)}, u32[]{:S(2)}, u32[]{:S(2)}) %collective-permute-start.5) | collective-permute-done | bytes 278560 | tf_op jit(solution)/shard_map/ppermute | solution.py:400
  22.0 1.3 %prepare.4 = (f32[40968,128]{1,0:T(8,128)S(1)}, f32[32,128]{1,0:T(8,128)S(1)}, f32[64,128]{1,0:T(8,128)S(1)}, s32[32,128]{1,0:T(8,128)}) custom-call(s32[1]{0:T(128)} %bitcast.1.rest_0_.chip_ref, s32[1]{0:T(128)} %bitcast.2.rest_1_.core_ref, s32[1]{0:T(128)} %bitcast.3.rest_2_.x_ref, s32[1,2,30]{2,1,0:T(2,128)S(1)} %copy-done.1, ...), custom_call_target="tpu_custom_call", output_to_operand_aliasing={{0}: (5, {})} | custom-call | flops 2000000000 | bytes 6000000 | tf_op jit(solution)/shard_map/prepare/pallas_call | solution.py:473
  23.3 0.2 collective-permute-done.6.rest_0_
  23.6 1.3 %prepare.5 = (f32[40968,128]{1,0:T(8,128)S(1)}, f32[32,128]{1,0:T(8,128)}, f32[64,128]{1,0:T(8,128)}, s32[32,128]{1,0:T(8,128)S(1)}) custom-call(s32[1]{0:T(128)} %bitcast.1.rest_0_.chip_ref, s32[1]{0:T(128)} %bitcast.2.rest_1_.core_ref, s32[1]{0:T(128)} %bitcast.3.rest_2_.x_ref, s32[1,2,30]{2,1,0:T(2,128)S(1)} %copy-done.1, ...), custom_call_target="tpu_custom_call", output_to_operand_aliasing={{0}: (5, {})} | custom-call | flops 2000000000 | bytes 6000000 | tf_op jit(solution)/shard_map/prepare/pallas_call | solution.py:473
  24.9 7.8 %correlate.3 = s16[2,512,128]{2,1,0:T(8,128)(2,1)S(1)} custom-call(s32[32,128]{1,0:T(8,128)S(1)} %get-tuple-element.33.source_ref, f32[40968,128]{1,0:T(8,128)S(1)} %get-tuple-element.34.held), custom_call_target="tpu_custom_call" | custom-call | flops 8999999488 | bytes 27000000 | tf_op jit(solution)/shard_map/correlate/pallas_call | solution.py:499
  32.8 1.6 %collective-permute-start.7 = (s16[2,512,128]{2,1,0:T(8,128)(2,1)S(1)}, s16[2,512,128]{2,1,0:T(8,128)(2,1)S(1)}, u32[]{:S(2)}, u32[]{:S(2)}) collective-permute-start(s16[2,512,128]{2,1,0:T(8,128)(2,1)S(1)} %correlate.3), channel_id=1, source_target_pairs={{0,2},{2,0},{4,6},{6,4},{8,10},{10,8},{12,14},{14,12},{1,3},{3,1},... | collective-permute-start | bytes 786440 | tf_op jit(solution)/shard_map/ppermute | solution.py:400
  34.3 7.7 %correlate.2 = (f32[512,128]{1,0:T(8,128)S(1)}, f32[512,128]{1,0:T(8,128)S(1)}) custom-call(s32[32,128]{1,0:T(8,128)S(1)} %get-tuple-element.33.source_ref, f32[40968,128]{1,0:T(8,128)S(1)} %get-tuple-element.34.held), custom_call_target="tpu_custom_call" | custom-call | flops 8999999488 | bytes 27000000 | tf_op jit(solution)/shard_map/correlate/pallas_call | solution.py:499
  42.0 0.2 join.1
  42.3 1.6 %collective-permute-start.8 = (s16[512,128]{1,0:T(8,128)(2,1)S(1)}, s16[512,128]{1,0:T(8,128)(2,1)S(1)}, u32[]{:S(2)}, u32[]{:S(2)}) collective-permute-start(s16[512,128]{1,0:T(8,128)(2,1)S(1)} %get-tuple-element.38), channel_id=1, source_target_pairs={{0,16},{16,0},{1,17},{17,1},{2,18},{18,2},{3,19},{19,3},{4,20},{20... | collective-permute-start | bytes 393224 | tf_op jit(solution)/shard_map/ppermute | solution.py:548
  43.8 3.9 %collective-permute-done.8.refs_0_ = s16[512,128]{1,0:T(8,128)(2,1)S(1)} collective-permute-done((s16[512,128]{1,0:T(8,128)(2,1)S(1)}, s16[512,128]{1,0:T(8,128)(2,1)S(1)}, u32[]{:S(2)}, u32[]{:S(2)}) %collective-permute-start.8) | collective-permute-done | bytes 131104 | tf_op jit(solution)/shard_map/ppermute | solution.py:548
  47.9 2.5 %collective-permute-start.9 = (s16[128,128]{1,0:T(8,128)(2,1)S(1)}, s16[128,128]{1,0:T(8,128)(2,1)S(1)}, u32[]{:S(2)}, u32[]{:S(2)}) collective-permute-start(s16[128,128]{1,0:T(8,128)(2,1)S(1)} %get-tuple-element.40), channel_id=1, source_target_pairs={{0,12},{2,14},{4,8},{6,10},{8,4},{10,6},{12,0},{14,2},{1,13},{3,15... | collective-permute-start | bytes 98312 | tf_op jit(solution)/shard_map/ppermute | solution.py:400
  50.6 1.8 %collective-permute-start.11 = (s16[128,128]{1,0:T(8,128)(2,1)S(1)}, s16[128,128]{1,0:T(8,128)(2,1)S(1)}, u32[]{:S(2)}, u32[]{:S(2)}) collective-permute-start(s16[128,128]{1,0:T(8,128)(2,1)S(1)} %get-tuple-element.42), channel_id=1, source_target_pairs={{0,4},{2,6},{4,0},{6,2},{8,12},{10,14},{12,8},{14,10},{1,5},{3,7},... | collective-permute-start | bytes 98312 | tf_op jit(solution)/shard_map/ppermute | solution.py:400
  52.4 1.3 %collective-permute-done.9.refs_0_ = s16[128,128]{1,0:T(8,128)(2,1)S(1)} collective-permute-done((s16[128,128]{1,0:T(8,128)(2,1)S(1)}, s16[128,128]{1,0:T(8,128)(2,1)S(1)}, u32[]{:S(2)}, u32[]{:S(2)}) %collective-permute-start.9) | collective-permute-done | bytes 32800 | tf_op jit(solution)/shard_map/ppermute | solution.py:400
  53.7 1.6 %collective-permute-done.10.refs_1_ = s16[128,128]{1,0:T(8,128)(2,1)S(1)} collective-permute-done((s16[128,128]{1,0:T(8,128)(2,1)S(1)}, s16[128,128]{1,0:T(8,128)(2,1)S(1)}, u32[]{:S(2)}, u32[]{:S(2)}) %collective-permute-start.10) | collective-permute-done | bytes 32800 | tf_op jit(solution)/shard_map/ppermute | solution.py:400
  55.3 1.6 %finish.1 = f32[4,2,4,435]{3,2,1,0:T(4,128)} custom-call(s32[2,435]{1,0:T(2,128)S(1)} %bitcast.5, f32[128,128]{1,0:T(8,128)S(1)} %get-tuple-element.39.own_ref, s16[128,128]{1,0:T(8,128)(2,1)S(1)} %collective-permute-done.9.refs_0_, s16[128,128]{1,0:T(8,128)(2,1)S(1)} %collective-permute-done.10.refs_1_, s16[128,128]{1,0:T(8,128)(2,1)S(1)} %collective-permute-done.11.refs_2_), custom_call_target="tpu_custom_call" | custom-call | flops 2000000000 | bytes 6000000 | tf_op jit(solution)/shard_map/finish/pallas_call | solution.py:564
  (18 shorter events, 0.4 us)
Async XLA Ops:
  0.0 15.2 %collective-permute-start = (bf16[2,2,30,2,8192]{4,3,2,1,0:T(2,128)(2,1)}, bf16[2,2,30,2,8192]{4,3,2,1,0:T(2,128)(2,1)}, u32[]{:S(2)}, u32[]{:S(2)}) collective-permute-start(bf16[2,2,30,2,8192]{4,3,2,1,0:T(2,128)(2,1)} %volts_ref.1), channel_id=1, source_target_pairs={{0,1},{1,0},{2,3},{3,2},{4,5},{5,4},{6,7},{7,6},{8,9},{9,8},{10,11... | collective-permute-start | bytes 11796488 | tf_op jit(solution)/shard_map/ppermute | solution.py:403
  2.2 11.4 %copy-start = (s16[272,128]{1,0:T(8,128)(2,1)S(1)}, s16[272,128]{1,0:T(8,128)(2,1)}, u32[]{:S(2)}) copy-start(s16[272,128]{1,0:T(8,128)(2,1)} %pack.1.refs_0_) | copy-start | bytes 208900
  2.2 9.1 %collective-permute-start.3 = (s16[272,128]{1,0:T(8,128)(2,1)}, s16[272,128]{1,0:T(8,128)(2,1)S(1)}, u32[]{:S(2)}, u32[]{:S(2)}) collective-permute-start(s16[272,128]{1,0:T(8,128)(2,1)} %pack.1.refs_0_), channel_id=1, source_target_pairs={{0,12},{2,14},{4,8},{6,10},{8,4},{10,6},{12,0},{14,2},{1,13},{3,15... | collective-permute-start | bytes 208904 | tf_op jit(solution)/shard_map/ppermute | solution.py:400
  6.9 6.7 %collective-permute-start.2 = (s16[272,128]{1,0:T(8,128)(2,1)}, s16[272,128]{1,0:T(8,128)(2,1)S(1)}, u32[]{:S(2)}, u32[]{:S(2)}) collective-permute-start(s16[272,128]{1,0:T(8,128)(2,1)} %pack.1.refs_0_), channel_id=1, source_target_pairs={{0,8},{2,10},{4,12},{6,14},{8,0},{10,2},{12,4},{14,6},{1,9},{3,11}... | collective-permute-start | bytes 208904 | tf_op jit(solution)/shard_map/ppermute | solution.py:400
  6.9 6.7 %collective-permute-start.1 = (s16[272,128]{1,0:T(8,128)(2,1)}, s16[272,128]{1,0:T(8,128)(2,1)S(1)}, u32[]{:S(2)}, u32[]{:S(2)}) collective-permute-start(s16[272,128]{1,0:T(8,128)(2,1)} %pack.1.refs_0_), channel_id=1, source_target_pairs={{0,4},{2,6},{4,0},{6,2},{8,12},{10,14},{12,8},{14,10},{1,5},{3,7},... | collective-permute-start | bytes 208904 | tf_op jit(solution)/shard_map/ppermute | solution.py:400
  13.6 5.4 %copy-start.1 = (s32[1,2,30]{2,1,0:T(2,128)S(1)}, s32[1,2,30]{2,1,0:T(2,128)}, u32[]{:S(2)}) copy-start(s32[1,2,30]{2,1,0:T(2,128)} %after_ref.5) | copy-start | bytes 724
  13.6 8.4 %collective-permute-start.5 = (s16[1088,128]{1,0:T(8,128)(2,1)S(1)}, s16[1088,128]{1,0:T(8,128)(2,1)S(1)}, u32[]{:S(2)}, u32[]{:S(2)}) collective-permute-start(s16[1088,128]{1,0:T(8,128)(2,1)S(1)} %stack.1.rest_0_), channel_id=1, source_target_pairs={{0,2},{2,0},{4,6},{6,4},{8,10},{10,8},{12,14},{14,12},{1,3},{3,1},... | collective-permute-start | bytes 835592 | tf_op jit(solution)/shard_map/ppermute | solution.py:400
  15.2 3.8 %collective-permute-start.4 = (s16[1088,128]{1,0:T(8,128)(2,1)S(1)}, s16[1088,128]{1,0:T(8,128)(2,1)S(1)}, u32[]{:S(2)}, u32[]{:S(2)}) collective-permute-start(s16[1088,128]{1,0:T(8,128)(2,1)S(1)} %stack.1.rest_0_), channel_id=1, source_target_pairs={{0,1},{1,0},{2,3},{3,2},{4,5},{5,4},{6,7},{7,6},{8,9},{9,8},{10,11... | collective-permute-start | bytes 835592 | tf_op jit(solution)/shard_map/ppermute | solution.py:403
  22.0 1.6 %collective-permute-start.6 = (s16[1088,128]{1,0:T(8,128)(2,1)S(1)}, s16[1088,128]{1,0:T(8,128)(2,1)S(1)}, u32[]{:S(2)}, u32[]{:S(2)}) collective-permute-start(s16[1088,128]{1,0:T(8,128)(2,1)S(1)} %collective-permute-done.5.rest_0_), channel_id=1, source_target_pairs={{0,1},{1,0},{2,3},{3,2},{4,5},{5,4},{6,7},{7,6},{8,9},{9,8},{10,11... | collective-permute-start | bytes 835592 | tf_op jit(solution)/shard_map/ppermute | solution.py:403
  32.7 22.6 %copy-start.2 = (s32[435,2]{0,1:T(2,128)S(1)}, s32[435,2]{0,1:T(2,128)}, u32[]{:S(2)}) copy-start(s32[435,2]{0,1:T(2,128)} %param.8) | copy-start | bytes 10444
  32.8 9.3 %collective-permute-start.7 = (s16[2,512,128]{2,1,0:T(8,128)(2,1)S(1)}, s16[2,512,128]{2,1,0:T(8,128)(2,1)S(1)}, u32[]{:S(2)}, u32[]{:S(2)}) collective-permute-start(s16[2,512,128]{2,1,0:T(8,128)(2,1)S(1)} %correlate.3), channel_id=1, source_target_pairs={{0,2},{2,0},{4,6},{6,4},{8,10},{10,8},{12,14},{14,12},{1,3},{3,1},... | collective-permute-start | bytes 786440 | tf_op jit(solution)/shard_map/ppermute | solution.py:400
  42.3 5.5 %collective-permute-start.8 = (s16[512,128]{1,0:T(8,128)(2,1)S(1)}, s16[512,128]{1,0:T(8,128)(2,1)S(1)}, u32[]{:S(2)}, u32[]{:S(2)}) collective-permute-start(s16[512,128]{1,0:T(8,128)(2,1)S(1)} %get-tuple-element.38), channel_id=1, source_target_pairs={{0,16},{16,0},{1,17},{17,1},{2,18},{18,2},{3,19},{19,3},{4,20},{20... | collective-permute-start | bytes 393224 | tf_op jit(solution)/shard_map/ppermute | solution.py:548
  47.9 5.8 %collective-permute-start.9 = (s16[128,128]{1,0:T(8,128)(2,1)S(1)}, s16[128,128]{1,0:T(8,128)(2,1)S(1)}, u32[]{:S(2)}, u32[]{:S(2)}) collective-permute-start(s16[128,128]{1,0:T(8,128)(2,1)S(1)} %get-tuple-element.40), channel_id=1, source_target_pairs={{0,12},{2,14},{4,8},{6,10},{8,4},{10,6},{12,0},{14,2},{1,13},{3,15... | collective-permute-start | bytes 98312 | tf_op jit(solution)/shard_map/ppermute | solution.py:400
  50.5 4.8 %collective-permute-start.10 = (s16[128,128]{1,0:T(8,128)(2,1)S(1)}, s16[128,128]{1,0:T(8,128)(2,1)S(1)}, u32[]{:S(2)}, u32[]{:S(2)}) collective-permute-start(s16[128,128]{1,0:T(8,128)(2,1)S(1)} %get-tuple-element.41), channel_id=1, source_target_pairs={{0,8},{2,10},{4,12},{6,14},{8,0},{10,2},{12,4},{14,6},{1,9},{3,11}... | collective-permute-start | bytes 98312 | tf_op jit(solution)/shard_map/ppermute | solution.py:400
  50.6 4.7 %collective-permute-start.11 = (s16[128,128]{1,0:T(8,128)(2,1)S(1)}, s16[128,128]{1,0:T(8,128)(2,1)S(1)}, u32[]{:S(2)}, u32[]{:S(2)}) collective-permute-start(s16[128,128]{1,0:T(8,128)(2,1)S(1)} %get-tuple-element.42), channel_id=1, source_target_pairs={{0,4},{2,6},{4,0},{6,2},{8,12},{10,14},{12,8},{14,10},{1,5},{3,7},... | collective-permute-start | bytes 98312 | tf_op jit(solution)/shard_map/ppermute | solution.py:400

commit v7 on v6

--- a/solution.py
+++ b/solution.py
@@ -349,6 +349,7 @@
     second = members_ref[1:2, :]
     rising = first < second
     station = iota((HALF, baselines), 0)
+    stacks = []
     for pair in range(pairs):
         at = pl.ds(pair * HALF, HALF)
         total = own_ref[at, :]
@@ -359,27 +360,31 @@
         flipped = total.T
         coarse = flipped.astype(jnp.bfloat16)
         medium = (flipped - coarse.astype(jnp.float32)).astype(jnp.bfloat16)
-        stack = jnp.concatenate([coarse, medium], axis=0)
-        picked = {}
-        for side, members in enumerate((first, second)):
-            for p in range(2):
-                choose = (station == 2 * members + p).astype(jnp.bfloat16)
-                rows = jnp.dot(stack, choose, preferred_element_type=jnp.float32)
-                rows = rows[:LANES] + rows[LANES:]
-                partner = second if side == 0 else first
+        stacks += [coarse, medium]
+    stack = jnp.concatenate(stacks, axis=0)
+    picked = {}
+    for side, members in enumerate((first, second)):
+        partner = second if side == 0 else first
+        for p in range(2):
+            choose = (station == 2 * members + p).astype(jnp.bfloat16)
+            rows = jnp.dot(stack, choose, preferred_element_type=jnp.float32)
+            for pair in range(pairs):
+                base = pair * 2 * LANES
+                both = rows[base : base + LANES] + rows[base + LANES : base + 2 * LANES]
                 for half in range(2):
                     for p2 in range(2):
                         match = station == 2 * partner + p2
-                        part = rows[half * HALF : (half + 1) * HALF]
-                        picked[side, half, p, p2] = jnp.sum(
+                        part = both[half * HALF : (half + 1) * HALF]
+                        picked[pair, side, half, p, p2] = jnp.sum(
                             jnp.where(match, part, 0.0), axis=0, keepdims=True
                         )
+    for pair in range(pairs):
         for half in range(2):
             real, imaginary = [], []
             for p in range(2):
                 for p2 in range(2):
-                    a = picked[0, half, p, p2]
-                    b = picked[1, half, p2, p]
+                    a = picked[pair, 0, half, p, p2]
+                    b = picked[pair, 1, half, p2, p]
                     real.append(jnp.where(rising, a, b))
                     imaginary.append(jnp.where(rising, b, -a))
             out_ref[2 * pair + half, 0] = jnp.concatenate(real, axis=0)

time: 57.1 us -> 57.1 us (level)
  no operation moved by 1% of the time
where the time goes in v7:
time: 57.1 us; the launch traced here: 56.9 us
  Pallas kernels  31.9 us (56%)
  starting transfers between devices  14.9 us (26%)
  waiting for transfers between devices  9.95 us (17%)
    pallas_call x2, Pallas kernels, correlate(): pl.pallas_call(functools.partial(correlate_kernel, first_pair=first_pair,...  15.5 us
    ppermute x8, starting transfers between devices, across_chips(): return lax.ppermute(x, 'chip', [(i, i ^ step) for i in range(chips)])  12.9 us
    pallas_call x2, Pallas kernels, rows(): pl.pallas_call(functools.partial(rows_kernel, first=side * spectra, pitch...  7.47 us
    ppermute x8, waiting for transfers between devices, across_chips(): return lax.ppermute(x, 'chip', [(i, i ^ step) for i in range(chips)])  5.81 us
    pallas_call x3, Pallas kernels, on_device(): pl.pallas_call(functools.partial(prepare_kernel, columns=columns, started...  5.08 us
    ppermute x1, waiting for transfers between devices, on_device(): lax.ppermute(own[c], 'tm', [(i, i ^ centre) for i in range(tm)])  3.92 us
    pallas_call x1, Pallas kernels, on_device(): pl.pallas_call(pack_kernel, in_specs=[HBM, HBM], out_specs=VMEM, out_shap...  1.77 us
    pallas_call x1, Pallas kernels, on_device(): pl.pallas_call(functools.partial(finish_kernel, arrivals=len(final), pair...  1.61 us
  transfers between devices with their start and end apart: 12, of which 6 were waited for; matrix products, arithmetic and copies ran while one was open for 0% of the time, Pallas kernels for 36%

profile of v7, /device:TPU:0, one launch (start us, length us, event | category | flops | bytes accessed | tf_op | source)
XLA Modules:
  0.0 56.9 jit_solution(4228085835395459793)
XLA Ops:
  0.0 0.5 collective-permute-start
  0.5 1.8 %pack.1.refs_0_ = s16[272,128]{1,0:T(8,128)(2,1)} custom-call(f32[64,512]{1,0:T(8,128)} %turning_hbm.1, s32[4,128]{1,0:T(4,128)} %bitcast.6), custom_call_target="tpu_custom_call" | custom-call | flops 1000000000 | bytes 3000000 | tf_op jit(solution)/shard_map/pack/pallas_call | solution.py:415
  2.2 4.7 %collective-permute-start.3 = (s16[272,128]{1,0:T(8,128)(2,1)}, s16[272,128]{1,0:T(8,128)(2,1)S(1)}, u32[]{:S(2)}, u32[]{:S(2)}) collective-permute-start(s16[272,128]{1,0:T(8,128)(2,1)} %pack.1.refs_0_), channel_id=1, source_target_pairs={{0,12},{2,14},{4,8},{6,10},{8,4},{10,6},{12,0},{14,2},{1,13},{3,15... | collective-permute-start | bytes 208904 | tf_op jit(solution)/shard_map/ppermute | solution.py:405
  6.9 0.6 %collective-permute-start.1 = (s16[272,128]{1,0:T(8,128)(2,1)}, s16[272,128]{1,0:T(8,128)(2,1)S(1)}, u32[]{:S(2)}, u32[]{:S(2)}) collective-permute-start(s16[272,128]{1,0:T(8,128)(2,1)} %pack.1.refs_0_), channel_id=1, source_target_pairs={{0,4},{2,6},{4,0},{6,2},{8,12},{10,14},{12,8},{14,10},{1,5},{3,7},... | collective-permute-start | bytes 208904 | tf_op jit(solution)/shard_map/ppermute | solution.py:405
  7.6 3.7 %rows.2.rest_3_.after_ref = f32[40968,128]{1,0:T(8,128)S(1)} custom-call(bf16[2,2,30,2,8192]{4,3,2,1,0:T(2,128)(2,1)} %volts_ref.1, s32[1]{0:T(128)} %bitcast.1.rest_0_.chip_ref, s32[1]{0:T(128)} %bitcast.2.rest_1_.core_ref, s32[1]{0:T(128)} %bitcast.3.rest_2_.x_ref), custom_call_target="tpu_custom_call" | custom-call | flops 5000000000 | bytes 15000000 | tf_op jit(solution)/shard_map/rows/pallas_call | solution.py:435
  11.3 2.3 %collective-permute-done.2.refs_2_ = s16[272,128]{1,0:T(8,128)(2,1)S(1)} collective-permute-done((s16[272,128]{1,0:T(8,128)(2,1)}, s16[272,128]{1,0:T(8,128)(2,1)S(1)}, u32[]{:S(2)}, u32[]{:S(2)}) %collective-permute-start.2) | collective-permute-done | bytes 69664 | tf_op jit(solution)/shard_map/ppermute | solution.py:405
  13.6 1.6 %collective-permute-start.5 = (s16[1088,128]{1,0:T(8,128)(2,1)S(1)}, s16[1088,128]{1,0:T(8,128)(2,1)S(1)}, u32[]{:S(2)}, u32[]{:S(2)}) collective-permute-start(s16[1088,128]{1,0:T(8,128)(2,1)S(1)} %stack.1.rest_0_), channel_id=1, source_target_pairs={{0,2},{2,0},{4,6},{6,4},{8,10},{10,8},{12,14},{14,12},{1,3},{3,1},... | collective-permute-start | bytes 835592 | tf_op jit(solution)/shard_map/ppermute | solution.py:405
  15.2 3.7 %rows.3.held_in = f32[40968,128]{1,0:T(8,128)S(1)} custom-call(bf16[2,2,30,2,8192]{4,3,2,1,0:T(2,128)(2,1)} %collective-permute-done.volts_ref, s32[1]{0:T(128)} %bitcast.1.rest_0_.chip_ref, s32[1]{0:T(128)} %bitcast.2.rest_1_.core_ref, s32[1]{0:T(128)} %bitcast.3.rest_2_.x_ref, f32[40968,128]{1,0:T(8,128)S(1)} %rows.2.rest_3_.after_ref), custom_call_target="tpu_custom_call", output_to_operand_aliasing={{}: (4, {})} | custom-call | flops 5000000000 | bytes 15000000 | tf_op jit(solution)/shard_map/rows/pallas_call | solution.py:435
  19.0 2.4 %prepare.3 = (f32[40968,128]{1,0:T(8,128)S(1)}, f32[32,128]{1,0:T(8,128)S(1)}, f32[64,128]{1,0:T(8,128)S(1)}, s32[32,128]{1,0:T(8,128)}) custom-call(s32[1]{0:T(128)} %bitcast.1.rest_0_.chip_ref, s32[1]{0:T(128)} %bitcast.2.rest_1_.core_ref, s32[1]{0:T(128)} %bitcast.3.rest_2_.x_ref, s32[1,2,30]{2,1,0:T(2,128)S(1)} %copy-done.1, ...), custom_call_target="tpu_custom_call", output_to_operand_aliasing={{0}: (5, {})} | custom-call | flops 2000000000 | bytes 6000000 | tf_op jit(solution)/shard_map/prepare/pallas_call | solution.py:478
  21.4 0.6 %collective-permute-done.5.rest_0_ = s16[1088,128]{1,0:T(8,128)(2,1)S(1)} collective-permute-done((s16[1088,128]{1,0:T(8,128)(2,1)S(1)}, s16[1088,128]{1,0:T(8,128)(2,1)S(1)}, u32[]{:S(2)}, u32[]{:S(2)}) %collective-permute-start.5) | collective-permute-done | bytes 278560 | tf_op jit(solution)/shard_map/ppermute | solution.py:405
  22.0 1.3 %prepare.4 = (f32[40968,128]{1,0:T(8,128)S(1)}, f32[32,128]{1,0:T(8,128)S(1)}, f32[64,128]{1,0:T(8,128)S(1)}, s32[32,128]{1,0:T(8,128)}) custom-call(s32[1]{0:T(128)} %bitcast.1.rest_0_.chip_ref, s32[1]{0:T(128)} %bitcast.2.rest_1_.core_ref, s32[1]{0:T(128)} %bitcast.3.rest_2_.x_ref, s32[1,2,30]{2,1,0:T(2,128)S(1)} %copy-done.1, ...), custom_call_target="tpu_custom_call", output_to_operand_aliasing={{0}: (5, {})} | custom-call | flops 2000000000 | bytes 6000000 | tf_op jit(solution)/shard_map/prepare/pallas_call | solution.py:478
  23.3 0.2 collective-permute-done.6.rest_0_
  23.6 1.3 %prepare.5 = (f32[40968,128]{1,0:T(8,128)S(1)}, f32[32,128]{1,0:T(8,128)}, f32[64,128]{1,0:T(8,128)}, s32[32,128]{1,0:T(8,128)S(1)}) custom-call(s32[1]{0:T(128)} %bitcast.1.rest_0_.chip_ref, s32[1]{0:T(128)} %bitcast.2.rest_1_.core_ref, s32[1]{0:T(128)} %bitcast.3.rest_2_.x_ref, s32[1,2,30]{2,1,0:T(2,128)S(1)} %copy-done.1, ...), custom_call_target="tpu_custom_call", output_to_operand_aliasing={{0}: (5, {})} | custom-call | flops 2000000000 | bytes 6000000 | tf_op jit(solution)/shard_map/prepare/pallas_call | solution.py:478
  24.9 7.8 %correlate.3 = s16[2,512,128]{2,1,0:T(8,128)(2,1)S(1)} custom-call(s32[32,128]{1,0:T(8,128)S(1)} %get-tuple-element.33.source_ref, f32[40968,128]{1,0:T(8,128)S(1)} %get-tuple-element.34.held), custom_call_target="tpu_custom_call" | custom-call | flops 8999999488 | bytes 27000000 | tf_op jit(solution)/shard_map/correlate/pallas_call | solution.py:504
  32.7 1.6 %collective-permute-start.7 = (s16[2,512,128]{2,1,0:T(8,128)(2,1)S(1)}, s16[2,512,128]{2,1,0:T(8,128)(2,1)S(1)}, u32[]{:S(2)}, u32[]{:S(2)}) collective-permute-start(s16[2,512,128]{2,1,0:T(8,128)(2,1)S(1)} %correlate.3), channel_id=1, source_target_pairs={{0,2},{2,0},{4,6},{6,4},{8,10},{10,8},{12,14},{14,12},{1,3},{3,1},... | collective-permute-start | bytes 786440 | tf_op jit(solution)/shard_map/ppermute | solution.py:405
  34.3 7.7 %correlate.2 = (f32[512,128]{1,0:T(8,128)S(1)}, f32[512,128]{1,0:T(8,128)S(1)}) custom-call(s32[32,128]{1,0:T(8,128)S(1)} %get-tuple-element.33.source_ref, f32[40968,128]{1,0:T(8,128)S(1)} %get-tuple-element.34.held), custom_call_target="tpu_custom_call" | custom-call | flops 8999999488 | bytes 27000000 | tf_op jit(solution)/shard_map/correlate/pallas_call | solution.py:504
  42.0 0.2 join.1
  42.3 1.6 %collective-permute-start.8 = (s16[512,128]{1,0:T(8,128)(2,1)S(1)}, s16[512,128]{1,0:T(8,128)(2,1)S(1)}, u32[]{:S(2)}, u32[]{:S(2)}) collective-permute-start(s16[512,128]{1,0:T(8,128)(2,1)S(1)} %get-tuple-element.38), channel_id=1, source_target_pairs={{0,16},{16,0},{1,17},{17,1},{2,18},{18,2},{3,19},{19,3},{4,20},{20... | collective-permute-start | bytes 393224 | tf_op jit(solution)/shard_map/ppermute | solution.py:553
  43.8 3.9 %collective-permute-done.8.refs_0_ = s16[512,128]{1,0:T(8,128)(2,1)S(1)} collective-permute-done((s16[512,128]{1,0:T(8,128)(2,1)S(1)}, s16[512,128]{1,0:T(8,128)(2,1)S(1)}, u32[]{:S(2)}, u32[]{:S(2)}) %collective-permute-start.8) | collective-permute-done | bytes 131104 | tf_op jit(solution)/shard_map/ppermute | solution.py:553
  47.9 2.5 %collective-permute-start.9 = (s16[128,128]{1,0:T(8,128)(2,1)S(1)}, s16[128,128]{1,0:T(8,128)(2,1)S(1)}, u32[]{:S(2)}, u32[]{:S(2)}) collective-permute-start(s16[128,128]{1,0:T(8,128)(2,1)S(1)} %get-tuple-element.40), channel_id=1, source_target_pairs={{0,12},{2,14},{4,8},{6,10},{8,4},{10,6},{12,0},{14,2},{1,13},{3,15... | collective-permute-start | bytes 98312 | tf_op jit(solution)/shard_map/ppermute | solution.py:405
  50.6 1.8 %collective-permute-start.11 = (s16[128,128]{1,0:T(8,128)(2,1)S(1)}, s16[128,128]{1,0:T(8,128)(2,1)S(1)}, u32[]{:S(2)}, u32[]{:S(2)}) collective-permute-start(s16[128,128]{1,0:T(8,128)(2,1)S(1)} %get-tuple-element.42), channel_id=1, source_target_pairs={{0,4},{2,6},{4,0},{6,2},{8,12},{10,14},{12,8},{14,10},{1,5},{3,7},... | collective-permute-start | bytes 98312 | tf_op jit(solution)/shard_map/ppermute | solution.py:405
  52.4 1.3 %collective-permute-done.9.refs_0_ = s16[128,128]{1,0:T(8,128)(2,1)S(1)} collective-permute-done((s16[128,128]{1,0:T(8,128)(2,1)S(1)}, s16[128,128]{1,0:T(8,128)(2,1)S(1)}, u32[]{:S(2)}, u32[]{:S(2)}) %collective-permute-start.9) | collective-permute-done | bytes 32800 | tf_op jit(solution)/shard_map/ppermute | solution.py:405
  53.7 1.6 %collective-permute-done.10.refs_1_ = s16[128,128]{1,0:T(8,128)(2,1)S(1)} collective-permute-done((s16[128,128]{1,0:T(8,128)(2,1)S(1)}, s16[128,128]{1,0:T(8,128)(2,1)S(1)}, u32[]{:S(2)}, u32[]{:S(2)}) %collective-permute-start.10) | collective-permute-done | bytes 32800 | tf_op jit(solution)/shard_map/ppermute | solution.py:405
  55.3 1.6 %finish.1 = f32[4,2,4,435]{3,2,1,0:T(4,128)} custom-call(s32[2,435]{1,0:T(2,128)S(1)} %bitcast.5, f32[128,128]{1,0:T(8,128)S(1)} %get-tuple-element.39.own_ref, s16[128,128]{1,0:T(8,128)(2,1)S(1)} %collective-permute-done.9.refs_0_, s16[128,128]{1,0:T(8,128)(2,1)S(1)} %collective-permute-done.10.refs_1_, s16[128,128]{1,0:T(8,128)(2,1)S(1)} %collective-permute-done.11.refs_2_), custom_call_target="tpu_custom_call" | custom-call | flops 2000000000 | bytes 6000000 | tf_op jit(solution)/shard_map/finish/pallas_call | solution.py:569
  (18 shorter events, 0.4 us)
Async XLA Ops:
  0.0 15.2 %collective-permute-start = (bf16[2,2,30,2,8192]{4,3,2,1,0:T(2,128)(2,1)}, bf16[2,2,30,2,8192]{4,3,2,1,0:T(2,128)(2,1)}, u32[]{:S(2)}, u32[]{:S(2)}) collective-permute-start(bf16[2,2,30,2,8192]{4,3,2,1,0:T(2,128)(2,1)} %volts_ref.1), channel_id=1, source_target_pairs={{0,1},{1,0},{2,3},{3,2},{4,5},{5,4},{6,7},{7,6},{8,9},{9,8},{10,11... | collective-permute-start | bytes 11796488 | tf_op jit(solution)/shard_map/ppermute | solution.py:408
  2.2 11.4 %copy-start = (s16[272,128]{1,0:T(8,128)(2,1)S(1)}, s16[272,128]{1,0:T(8,128)(2,1)}, u32[]{:S(2)}) copy-start(s16[272,128]{1,0:T(8,128)(2,1)} %pack.1.refs_0_) | copy-start | bytes 208900
  2.2 9.1 %collective-permute-start.3 = (s16[272,128]{1,0:T(8,128)(2,1)}, s16[272,128]{1,0:T(8,128)(2,1)S(1)}, u32[]{:S(2)}, u32[]{:S(2)}) collective-permute-start(s16[272,128]{1,0:T(8,128)(2,1)} %pack.1.refs_0_), channel_id=1, source_target_pairs={{0,12},{2,14},{4,8},{6,10},{8,4},{10,6},{12,0},{14,2},{1,13},{3,15... | collective-permute-start | bytes 208904 | tf_op jit(solution)/shard_map/ppermute | solution.py:405
  6.9 6.7 %collective-permute-start.2 = (s16[272,128]{1,0:T(8,128)(2,1)}, s16[272,128]{1,0:T(8,128)(2,1)S(1)}, u32[]{:S(2)}, u32[]{:S(2)}) collective-permute-start(s16[272,128]{1,0:T(8,128)(2,1)} %pack.1.refs_0_), channel_id=1, source_target_pairs={{0,8},{2,10},{4,12},{6,14},{8,0},{10,2},{12,4},{14,6},{1,9},{3,11}... | collective-permute-start | bytes 208904 | tf_op jit(solution)/shard_map/ppermute | solution.py:405
  6.9 6.7 %collective-permute-start.1 = (s16[272,128]{1,0:T(8,128)(2,1)}, s16[272,128]{1,0:T(8,128)(2,1)S(1)}, u32[]{:S(2)}, u32[]{:S(2)}) collective-permute-start(s16[272,128]{1,0:T(8,128)(2,1)} %pack.1.refs_0_), channel_id=1, source_target_pairs={{0,4},{2,6},{4,0},{6,2},{8,12},{10,14},{12,8},{14,10},{1,5},{3,7},... | collective-permute-start | bytes 208904 | tf_op jit(solution)/shard_map/ppermute | solution.py:405
  13.6 5.4 %copy-start.1 = (s32[1,2,30]{2,1,0:T(2,128)S(1)}, s32[1,2,30]{2,1,0:T(2,128)}, u32[]{:S(2)}) copy-start(s32[1,2,30]{2,1,0:T(2,128)} %after_ref.5) | copy-start | bytes 724
  13.6 8.4 %collective-permute-start.5 = (s16[1088,128]{1,0:T(8,128)(2,1)S(1)}, s16[1088,128]{1,0:T(8,128)(2,1)S(1)}, u32[]{:S(2)}, u32[]{:S(2)}) collective-permute-start(s16[1088,128]{1,0:T(8,128)(2,1)S(1)} %stack.1.rest_0_), channel_id=1, source_target_pairs={{0,2},{2,0},{4,6},{6,4},{8,10},{10,8},{12,14},{14,12},{1,3},{3,1},... | collective-permute-start | bytes 835592 | tf_op jit(solution)/shard_map/ppermute | solution.py:405
  15.2 3.8 %collective-permute-start.4 = (s16[1088,128]{1,0:T(8,128)(2,1)S(1)}, s16[1088,128]{1,0:T(8,128)(2,1)S(1)}, u32[]{:S(2)}, u32[]{:S(2)}) collective-permute-start(s16[1088,128]{1,0:T(8,128)(2,1)S(1)} %stack.1.rest_0_), channel_id=1, source_target_pairs={{0,1},{1,0},{2,3},{3,2},{4,5},{5,4},{6,7},{7,6},{8,9},{9,8},{10,11... | collective-permute-start | bytes 835592 | tf_op jit(solution)/shard_map/ppermute | solution.py:408
  22.0 1.6 %collective-permute-start.6 = (s16[1088,128]{1,0:T(8,128)(2,1)S(1)}, s16[1088,128]{1,0:T(8,128)(2,1)S(1)}, u32[]{:S(2)}, u32[]{:S(2)}) collective-permute-start(s16[1088,128]{1,0:T(8,128)(2,1)S(1)} %collective-permute-done.5.rest_0_), channel_id=1, source_target_pairs={{0,1},{1,0},{2,3},{3,2},{4,5},{5,4},{6,7},{7,6},{8,9},{9,8},{10,11... | collective-permute-start | bytes 835592 | tf_op jit(solution)/shard_map/ppermute | solution.py:408
  32.7 22.6 %copy-start.2 = (s32[435,2]{0,1:T(2,128)S(1)}, s32[435,2]{0,1:T(2,128)}, u32[]{:S(2)}) copy-start(s32[435,2]{0,1:T(2,128)} %param.8) | copy-start | bytes 10444
  32.7 9.3 %collective-permute-start.7 = (s16[2,512,128]{2,1,0:T(8,128)(2,1)S(1)}, s16[2,512,128]{2,1,0:T(8,128)(2,1)S(1)}, u32[]{:S(2)}, u32[]{:S(2)}) collective-permute-start(s16[2,512,128]{2,1,0:T(8,128)(2,1)S(1)} %correlate.3), channel_id=1, source_target_pairs={{0,2},{2,0},{4,6},{6,4},{8,10},{10,8},{12,14},{14,12},{1,3},{3,1},... | collective-permute-start | bytes 786440 | tf_op jit(solution)/shard_map/ppermute | solution.py:405
  42.3 5.5 %collective-permute-start.8 = (s16[512,128]{1,0:T(8,128)(2,1)S(1)}, s16[512,128]{1,0:T(8,128)(2,1)S(1)}, u32[]{:S(2)}, u32[]{:S(2)}) collective-permute-start(s16[512,128]{1,0:T(8,128)(2,1)S(1)} %get-tuple-element.38), channel_id=1, source_target_pairs={{0,16},{16,0},{1,17},{17,1},{2,18},{18,2},{3,19},{19,3},{4,20},{20... | collective-permute-start | bytes 393224 | tf_op jit(solution)/shard_map/ppermute | solution.py:553
  47.9 5.8 %collective-permute-start.9 = (s16[128,128]{1,0:T(8,128)(2,1)S(1)}, s16[128,128]{1,0:T(8,128)(2,1)S(1)}, u32[]{:S(2)}, u32[]{:S(2)}) collective-permute-start(s16[128,128]{1,0:T(8,128)(2,1)S(1)} %get-tuple-element.40), channel_id=1, source_target_pairs={{0,12},{2,14},{4,8},{6,10},{8,4},{10,6},{12,0},{14,2},{1,13},{3,15... | collective-permute-start | bytes 98312 | tf_op jit(solution)/shard_map/ppermute | solution.py:405
  50.5 4.8 %collective-permute-start.10 = (s16[128,128]{1,0:T(8,128)(2,1)S(1)}, s16[128,128]{1,0:T(8,128)(2,1)S(1)}, u32[]{:S(2)}, u32[]{:S(2)}) collective-permute-start(s16[128,128]{1,0:T(8,128)(2,1)S(1)} %get-tuple-element.41), channel_id=1, source_target_pairs={{0,8},{2,10},{4,12},{6,14},{8,0},{10,2},{12,4},{14,6},{1,9},{3,11}... | collective-permute-start | bytes 98312 | tf_op jit(solution)/shard_map/ppermute | solution.py:405
  50.6 4.7 %collective-permute-start.11 = (s16[128,128]{1,0:T(8,128)(2,1)S(1)}, s16[128,128]{1,0:T(8,128)(2,1)S(1)}, u32[]{:S(2)}, u32[]{:S(2)}) collective-permute-start(s16[128,128]{1,0:T(8,128)(2,1)S(1)} %get-tuple-element.42), channel_id=1, source_target_pairs={{0,4},{2,6},{4,0},{6,2},{8,12},{10,14},{12,8},{14,10},{1,5},{3,7},... | collective-permute-start | bytes 98312 | tf_op jit(solution)/shard_map/ppermute | solution.py:405
